TPU v7x, 32 devices: a whole 2x2x4 slice. The times are simulated.
32 devices in a mesh: groups: 2 (over y), neg: 4 (over z), rep: 2 (over x), sub: 2 (over core).
Axes of the slice: x: 2, y: 2, z: 4, core: 2. Of those that a mesh axis runs over, the one named last changes fastest.
Arguments:
- query_feats: bfloat16 [16384, 512], P(('groups', 'neg', 'rep', 'sub')), parts along dimension 0, may hold values from -6 to 6
- item_feats: bfloat16 [8192, 512], P(('groups', 'neg', 'rep', 'sub')), parts along dimension 0, may hold values from -6 to 6
- query_proj: bfloat16 [512, 128], replicated, may hold values from -0.25 to 0.25
- item_proj: bfloat16 [512, 128], replicated, may hold values from -0.25 to 0.25
- item_ids: int32 [8192], P(('groups', 'neg', 'rep', 'sub')), parts along dimension 0, may hold values from 0 to 999999
- item_counts: int32 [8192], P(('groups', 'neg', 'rep', 'sub')), parts along dimension 0, may hold values from 1 to 999
- positives: int32 [16384], P(('groups', 'neg', 'rep', 'sub')), parts along dimension 0, may hold values from 0 to 255
Outputs:
- grad_query_proj: float32 [1024, 128], P('groups'), parts along dimension 0
- grad_item_proj: float32 [1024, 128], P('groups'), parts along dimension 0
- losses: float32 [16384], P(('groups', 'neg', 'rep', 'sub')), parts along dimension 0
There are 2 independent parts, one for each index of `groups`. A program takes and returns all parts, laid end to end along the dimension named above; an argument that names none is the same for every part. Nothing has to cross between parts.
Inputs may be any that keep to these rules, and one draw needn't show every extreme that they name: `positives`: each value indexes one of the 256 item rows held by the query's own device.
All inputs are finite; a program needn't handle non-finite values.
Results may differ from a plain program's by a relative error of at most 0.0049.
Values may be sent and summed in bfloat16 or wider, within the bound.
No kernel may reach another device: no remote copies, remote signals or barrier semaphores. Data moves between devices by JAX's collectives and lax.ppermute only.
A program may use at most 64 MiB of HBM per device.

v0:
```python
import math

import jax
import jax.numpy as jnp
from jax import lax
from jax.sharding import PartitionSpec as P

inverse_softness = 20.0


def normalize(values):
    return values / jnp.sqrt(jnp.sum(values * values, axis=-1, keepdims=True) + 1e-06)


def block_rows(total_rows, unit_rows):
    return unit_rows * math.gcd(total_rows // unit_rows, max(1, 1024 // unit_rows))


def on_device(query_feats, item_feats, query_proj, item_proj, item_ids, item_counts, positives):
    request_number = query_feats.shape[0]
    i_rows = item_feats.shape[0]
    adjusted_derivative = inverse_softness / request_number
    query_z = jnp.dot(query_feats, query_proj, preferred_element_type=jnp.float32)
    item_z = jnp.dot(item_feats, item_proj, preferred_element_type=jnp.float32)
    query_batch = normalize(query_z).astype(jnp.bfloat16)
    items = normalize(item_z).astype(jnp.bfloat16)
    width = query_batch.shape[1]
    own_index = lax.axis_index("neg")
    local_logq = jnp.log(item_counts.astype(jnp.float32))
    pos_ids = jnp.take(item_ids, positives)
    pos_global = own_index * i_rows + positives
    stacked = jnp.stack([item_ids, item_counts], axis=1)
    all_items, all_ints = (
        lax.all_gather(items, "neg", axis=0, tiled=True),
        lax.all_gather(stacked, "neg", axis=0, tiled=True),
    )
    all_logq = jnp.log(all_ints[:, 1].astype(jnp.float32))
    all_ids = all_ints[:, 0]
    n_all = all_items.shape[0]
    step_rows = block_rows(n_all, i_rows)
    starts = jnp.arange(n_all // step_rows, dtype=jnp.int32) * step_rows

    def exp_block(start, count):
        block_slice = lax.dynamic_slice_in_dim(all_items, start, count, 0)
        logq_block = lax.dynamic_slice_in_dim(all_logq, start, count, 0)
        ids_block = lax.dynamic_slice_in_dim(all_ids, start, count, 0)
        similarity_table = inverse_softness * jnp.dot(
            query_batch, block_slice.T, preferred_element_type=jnp.float32
        )
        similarity_table = similarity_table - logq_block[None, :]
        cand_index = start + jnp.arange(count, dtype=jnp.int32)
        onehot = cand_index[None, :] == pos_global[:, None]
        collide = (ids_block[None, :] == pos_ids[:, None]) & jnp.logical_not(onehot)
        return (jnp.where(collide, 0.0, jnp.exp(similarity_table)), onehot, block_slice)

    def add_total(running, start):
        total_run, weighted_run = running
        weights, onehot, block_slice = exp_block(start, step_rows)
        weighted_run = weighted_run + jnp.dot(
            weights.astype(jnp.bfloat16), block_slice, preferred_element_type=jnp.float32
        )
        return ((total_run + jnp.sum(weights, axis=1), weighted_run), None)

    (totals, weighted), _ = lax.scan(
        add_total,
        (
            jnp.zeros((request_number,), jnp.float32),
            jnp.zeros((request_number, width), jnp.float32),
        ),
        starts,
    )
    pos_vectors = jnp.take(items, positives, axis=0).astype(jnp.float32)
    target_similarity = inverse_softness * jnp.sum(
        query_batch.astype(jnp.float32) * pos_vectors, axis=1
    ) - jnp.take(local_logq, positives)
    losses = jnp.log(totals) - target_similarity

    def grad_block(start, count):
        weights, onehot, block_slice = exp_block(start, count)
        grads = (weights / totals[:, None] - onehot.astype(jnp.float32)).astype(jnp.bfloat16)
        return (grads, block_slice)

    query_sum = weighted / totals[:, None] - pos_vectors
    query_dz = jax.vjp(normalize, query_z)[1](query_sum * adjusted_derivative)[0].astype(
        jnp.bfloat16
    )
    grad_query = jnp.einsum("qd,qe->de", query_feats, query_dz, preferred_element_type=jnp.float32)
    piece_rows = math.gcd(lax.axis_size("neg") * i_rows, step_rows)

    def one_piece(begin):
        grads, block_slice = grad_block(begin, piece_rows)
        return jnp.einsum("qi,qe->ie", grads, query_batch, preferred_element_type=jnp.float32)

    pieces = lax.map(
        one_piece,
        jnp.arange(lax.axis_size("neg") * i_rows // piece_rows, dtype=jnp.int32) * piece_rows,
    )
    item_sum = lax.psum_scatter(
        pieces.reshape(lax.axis_size("neg") * i_rows, width), "neg", scatter_dimension=0, tiled=True
    )
    item_dz = jax.vjp(normalize, item_z)[1](item_sum * adjusted_derivative)[0].astype(jnp.bfloat16)
    grad_item = jnp.einsum("qd,qe->de", item_feats, item_dz, preferred_element_type=jnp.float32)
    grad_query_total, grad_item_total = lax.psum((grad_query, grad_item), ("neg", "rep", "sub"))
    return (grad_query_total, grad_item_total, losses)


def solution(mesh):
    return jax.shard_map(
        on_device,
        mesh=mesh,
        in_specs=(
            P(("groups", "neg", "rep", "sub"), None),
            P(("groups", "neg", "rep", "sub"), None),
            P(),
            P(),
            P(("groups", "neg", "rep", "sub")),
            P(("groups", "neg", "rep", "sub")),
            P(("groups", "neg", "rep", "sub")),
        ),
        out_specs=(P("groups", None), P("groups", None), P(("groups", "neg", "rep", "sub"))),
        check_vma=False,
    )
```

profile of v0, /device:TPU:0, one launch (start us, length us, event | category | flops | bytes accessed | tf_op | source)
XLA Modules:
  0.0 170.9 jit_solution(10531279684485107960)
XLA Ops:
  7.2 0.0 copy-start
  7.2 0.0 copy-start.1
  7.2 0.0 copy-start.2
  7.2 0.0 reduce-scatter.2.cloned.1.call-start
  7.3 1.3 multiply_reduce_fusion.3
  8.6 0.1 copy.15
  8.7 15.6 %all_gather.7 = bf16[1024,128]{0,1:T(8,128)(2,1)S(1)} all-gather(bf16[256,128]{0,1:T(8,128)(2,1)S(1)} %divide_convert_fusion.1), channel_id=1, replica_groups=mesh['groups'=2,'neg'=4,'rep'=2,'sub'=2] {'neg'}, dimensions={0}, use_global_device_ids=true | all-gather | bytes 327680 | tf_op jit(solution)/shard_map/all_gather | solution.py:34
  24.3 0.7 pad_add_fusion
  25.0 11.9 %all_gather.6 = s32[1024,2]{0,1:T(2,128)S(1)} all-gather(s32[256,2]{0,1:T(2,128)S(1)} %pad_add_fusion), channel_id=1, replica_groups=mesh['groups'=2,'neg'=4,'rep'=2,'sub'=2] {'neg'}, dimensions={0}, use_global_device_ids=true | all-gather | bytes 10240 | tf_op jit(solution)/shard_map/all_gather | solution.py:35
  37.0 0.0 copy-done
  37.0 1.2 multiply_reduce_fusion.1
  38.3 0.0 copy-done.2
  38.3 0.0 copy-done.1
  38.3 3.5 %gather_fusion = s32[512]{0:T(512)S(1)} fusion(s32[256]{0:T(256)S(1)} %copy-done.1, s32[1024]{0:T(1024)S(1)} %pad_clamp_fusion), kind=kCustom, calls=%fused_computation | custom fusion | bytes 6144 | tf_op jit(solution)/shard_map/jit(_take)/gather | solution.py:30
  41.8 1.3 gather_fusion.1
  43.2 0.1 copy.16
  43.3 0.1 fusion.5
  43.4 1.2 fusion.19
  44.6 1.4 fusion.4
  46.0 0.0 reduce-scatter.2.cloned.1.call-update
  46.1 0.0 all-reduce.3.cloned.1.call-start
  46.1 0.5 multiply_reduce_fusion
  46.6 0.0 copy-start.3
  46.7 0.9 convolution_bitcast_fusion
  47.6 20.5 %reduce-scatter.2.cloned.1.call-done = f32[256,128]{0,1:T(8,128)} async-done(((f32[1024,128]{0,1:T(8,128)}), f32[256,128]{0,1:T(8,128)}) %reduce-scatter.2.cloned.1.call-update) | async-done | bytes 131088 | tf_op jit(solution)/shard_map/reduce_scatter | solution.py:98
  68.1 0.9 multiply_reduce_fusion.2
  69.1 1.9 %convolution_bitcast_fusion.1 = f32[512,128]{0,1:T(8,128)} fusion(bf16[256,512]{1,0:T(8,128)(2,1)} %param.8, f32[256,128]{0,1:T(8,128)S(1)} %get-tuple-element.75, f32[256,128]{0,1:T(8,128)} %reduce-scatter.2.cloned.1.call-done, f32[256]{0:T(256)S(1)} %multiply_multiply_fusion.1, f32[256]{0:T(256)S(1)} %get-tuple-element.73), kind=kOutput, calls=%fused_computation.9 | convolution fusion | flops 33751040 | bytes 788480 | tf_op jit(solution)/shard_map/qd,qe->de/dot_general | solution.py:102
  71.0 0.0 all-reduce.3.cloned.1.call-update
  71.0 0.0 copy-done.3
  71.0 3.5 %gather_fusion.2 = f32[512]{0:T(512)S(1)} fusion(f32[256]{0:T(256)S(1)} %convert_log_fusion, s32[1024]{0:T(1024)S(1)} %pad_clamp_fusion), kind=kCustom, calls=%fused_computation.2 | custom fusion | bytes 6144 | tf_op jit(solution)/shard_map/jit(_take)/gather | solution.py:75
  74.5 0.6 subtract_subtract_fusion
  75.1 85.4 %all-reduce.3.cloned.1.call-done = (f32[512,128]{0,1:T(8,128)}, f32[512,128]{0,1:T(8,128)}) async-done(((f32[512,128]{0,1:T(8,128)}, f32[512,128]{0,1:T(8,128)}), (f32[512,128]{0,1:T(8,128)}, f32[512,128]{0,1:T(8,128)})) %all-reduce.3.cloned.1.call-update) | async-done | bytes 524304 | tf_op jit(solution)/shard_map/psum | solution.py:103
  160.5 1.8 %copy.18 = f32[512,128]{1,0:T(8,128)} copy(f32[512,128]{0,1:T(8,128)} %get-tuple-element.54) | data formatting | bytes 524288
  162.3 1.8 %copy.19 = f32[512,128]{1,0:T(8,128)} copy(f32[512,128]{0,1:T(8,128)} %get-tuple-element.55) | data formatting | bytes 524288
  (11 shorter events, 0.1 us)
Async XLA Ops:
  7.2 29.8 %copy-start = (bf16[512,512]{1,0:T(8,128)(2,1)S(1)}, bf16[512,512]{1,0:T(8,128)(2,1)}, u32[]{:S(2)}) copy-start(bf16[512,512]{1,0:T(8,128)(2,1)} %param.7) | copy-start | bytes 1572868
  7.2 31.1 %copy-start.1 = (s32[256]{0:T(256)S(1)}, s32[256]{0:T(256)}, u32[]{:S(2)}) copy-start(s32[256]{0:T(256)} %param.11) | copy-start | bytes 3076
  7.2 31.1 %copy-start.2 = (s32[512]{0:T(512)S(1)}, s32[512]{0:T(512)}, u32[]{:S(2)}) copy-start(s32[512]{0:T(512)} %param.13) | copy-start | bytes 6148
  7.2 60.9 %reduce-scatter.2.cloned.1.call-start = ((), (), s32[]{:S(2)}) async-start(), calls=%async_computation.1 | async-start | bytes 655360 | tf_op jit(solution)/shard_map/reduce_scatter | solution.py:98
  46.1 114.5 %all-reduce.3.cloned.1.call-start = ((), (), s32[]{:S(2)}) async-start(), calls=%async_computation.2 | async-start | bytes 1048576 | tf_op jit(solution)/shard_map/psum | solution.py:103
  46.6 24.4 %copy-start.3 = (s32[256]{0:T(256)S(1)}, s32[256]{0:T(256)}, u32[]{:S(2)}) copy-start(s32[256]{0:T(256)} %param.12) | copy-start | bytes 3076
Sparse Core Ops, SparseCore 0:
  46.2 21.8 reduce-scatter.1
  72.1 88.3 all-reduce.2
where the time goes:
time: 171 us
  waiting for transfers between devices  106 us (62%)
  blocking collectives  27.6 us (16%)
  between operations  14.2 us (8%)
  local copies, waits for them, and re-layouts  12.2 us (7%)
  matrix products  8.54 us (5%)
  other arithmetic  2.41 us (1%)
    psum x1, waiting for transfers between devices, on_device(): lax.psum((grad_query, grad_item), ('neg', 'rep', 'sub'))  85.4 us
    reduce_scatter x1, waiting for transfers between devices, on_device(): lax.psum_scatter(pieces.reshape(lax.axis_size('neg') * i_rows, width), 'n...  20.5 us
    all_gather x1, blocking collectives, on_device(): lax.all_gather(items, 'neg', axis=0, tiled=True)  15.6 us
    all_gather x1, blocking collectives, on_device(): lax.all_gather(stacked, 'neg', axis=0, tiled=True)  11.9 us
    unnamed x10, local copies, waits for them, and re-layouts  3.6 us
    gather x1, local copies, waits for them, and re-layouts, on_device(): pos_ids = jnp.take(item_ids, positives)  3.51 us
    gather x1, local copies, waits for them, and re-layouts, on_device(): jnp.take(local_logq, positives)  3.51 us
  transfers between devices with their start and end apart: 2, of which 2 were waited for; matrix products, arithmetic and copies ran while one was open for 3% of the time, Pallas kernels for 0%

commit v1 on v0

v1 whole, which is shorter than its diff:
```python
import functools
import math

import jax
import jax.numpy as jnp
from jax import lax
from jax.experimental import pallas as pl
from jax.experimental.pallas import tpu as pltpu
from jax.sharding import PartitionSpec as P

inverse_softness = 20.0
epsilon = 1e-06
log2e = math.log2(math.e)
ln2 = math.log(2.0)
tail_rows = 16
f32 = jnp.float32
bf16 = jnp.bfloat16


def contract(lhs, rhs, over):
    return lax.dot_general(lhs, rhs, (((over[0],), (over[1],)), ((), ())), preferred_element_type=f32)


def split_terms(values):
    terms = []
    for _ in range(3):
        term = values.astype(bf16).astype(f32)
        terms.append(term)
        values = values - term
    return terms


def item_tower(feats_ref, proj_ref, ids_ref, counts_ref, message_ref, z_ref):
    rows = feats_ref.shape[0]
    z = jnp.dot(feats_ref[...], proj_ref[...], preferred_element_type=f32)
    z_ref[...] = z
    inverse = 1.0 / jnp.sqrt(jnp.sum(z * z, axis=1, keepdims=True) + epsilon)
    message_ref[0:rows, :] = (z * inverse).astype(bf16)
    ids = ids_ref[...]
    digits = [ids >> 16, (ids >> 8) & 255, ids & 255]
    log_counts = jnp.log(counts_ref[...].astype(f32)) * log2e
    lines = [digit.astype(f32) for digit in digits] + split_terms(log_counts)
    halves = ids.shape[0]
    lines.append(jnp.zeros((tail_rows - 6 * halves, ids.shape[1]), f32))
    message_ref[rows : rows + tail_rows, :] = jnp.concatenate(lines, axis=0).astype(bf16)


def item_columns(message_ref, half, halves):
    rows = message_ref.shape[0] - tail_rows
    tail = message_ref[rows : rows + tail_rows, :]
    line = lax.broadcasted_iota(jnp.int32, (tail_rows, 128), 0)

    def weights(scales, first):
        table = jnp.zeros((tail_rows, 128), f32)
        for step, scale in enumerate(scales):
            table = jnp.where(line == (first + step) * halves + half, scale, table)
        return table.astype(bf16)

    ids = contract(tail, weights((65536.0, 256.0, 1.0), 0), (0, 0))
    logs = contract(tail, weights((1.0, 1.0, 1.0), 3), (0, 0))
    return ids, logs


def wide(column, width):
    return jnp.concatenate([column] * (width // column.shape[1]), axis=1)


def query_tower(
    feats_ref, proj_ref, message_ref, positives_ref, z_ref, query_ref, weights_ref, weighted_ref, pos_ref, lines_ref
):
    rows = message_ref.shape[0] - tail_rows
    halves = rows // 128
    z = contract(proj_ref[...], feats_ref[...], (0, 1))
    z_ref[...] = z
    inverse = 1.0 / jnp.sqrt(jnp.sum(z * z, axis=0, keepdims=True) + epsilon)
    queries = (z * inverse).astype(bf16)
    query_ref[...] = queries
    count = queries.shape[1]
    positives = positives_ref[...]
    tail = message_ref[rows : rows + tail_rows, :]
    own = []
    pos_id = jnp.zeros((1, count), f32)
    for half in range(halves):
        spot = lax.broadcasted_iota(jnp.int32, (128, count), 0) + half * 128
        own.append(spot == positives)
        found = jnp.dot(tail, own[half].astype(f32).astype(bf16), preferred_element_type=f32)
        for step, scale in enumerate((65536.0, 256.0, 1.0)):
            line = step * halves + half
            pos_id = pos_id + scale * found[line : line + 1, :]
    totals = jnp.zeros((1, count), f32)
    target = jnp.zeros((1, count), f32)
    weighted = jnp.zeros((queries.shape[0], count), f32)
    pos_items = jnp.zeros((queries.shape[0], count), f32)
    for half in range(halves):
        items = message_ref[half * 128 : half * 128 + 128, :]
        ids, logs = item_columns(message_ref, half, halves)
        scores = jnp.dot(items, queries, preferred_element_type=f32)
        scores = scores * (inverse_softness * log2e) - wide(logs, count)
        collide = (wide(ids, count) == pos_id) & jnp.logical_not(own[half])
        weights = jnp.where(collide, 0.0, jnp.exp2(scores))
        weights_ref[half * 128 : half * 128 + 128, :] = weights
        totals = totals + jnp.sum(weights, axis=0, keepdims=True)
        target = target + jnp.sum(jnp.where(own[half], scores, 0.0), axis=0, keepdims=True)
        weighted = weighted + contract(items, weights.astype(bf16), (0, 0))
        pos_items = pos_items + contract(items, own[half].astype(f32).astype(bf16), (0, 0))
    weighted_ref[...] = weighted
    pos_ref[...] = pos_items
    lines_ref[...] = jnp.concatenate([totals, target * ln2, pos_id, jnp.zeros((5, count), f32)], axis=0)


def candidates_kernel(others, query_ref, weights_ref, part_ref, lines_ref, positives_ref, *refs):
    message_refs = refs[:others]
    piece_refs = refs[others : 2 * others]
    own_ref, weighted_ref, sums_ref, losses_ref, scratch_ref = refs[2 * others :]
    rows = weights_ref.shape[0]
    halves = rows // 128
    queries = query_ref[...]
    count = queries.shape[1]
    totals = lines_ref[0:1, :]
    pos_id = lines_ref[2:3, :]
    weighted = part_ref[...]
    for other, message_ref in enumerate(message_refs):
        for half in range(halves):
            items = message_ref[half * 128 : half * 128 + 128, :]
            ids, logs = item_columns(message_ref, half, halves)
            scores = jnp.dot(items, queries, preferred_element_type=f32)
            scores = scores * (inverse_softness * log2e) - wide(logs, count)
            weights = jnp.where(wide(ids, count) == pos_id, 0.0, jnp.exp2(scores))
            scratch_ref[other, half * 128 : half * 128 + 128, :] = weights
            totals = totals + jnp.sum(weights, axis=0, keepdims=True)
            weighted = weighted + contract(items, weights.astype(bf16), (0, 0))
    weighted_ref[...] = weighted
    sums_ref[...] = totals
    losses_ref[...] = jnp.log(totals) - lines_ref[1:2, :]
    share = 1.0 / totals
    for other in range(others):
        grads = (scratch_ref[other] * share).astype(bf16)
        piece_refs[other][...] = contract(grads, queries, (1, 1)).astype(bf16)
    own = lax.broadcasted_iota(jnp.int32, (rows, count), 0) == positives_ref[...]
    grads = (weights_ref[...] * share - own.astype(f32)).astype(bf16)
    own_ref[...] = contract(grads, queries, (1, 1))


def query_gradient(scale, weighted_ref, sums_ref, pos_ref, z_ref, feats_ref, item_feats_ref, grad_ref, turned_ref):
    cot = (weighted_ref[...] / sums_ref[...] - pos_ref[...]) * scale
    z = z_ref[...]
    inverse = 1.0 / jnp.sqrt(jnp.sum(z * z, axis=0, keepdims=True) + epsilon)
    along = jnp.sum(z * cot, axis=0, keepdims=True) * (inverse * inverse * inverse)
    dz = (cot * inverse - z * along).astype(bf16)
    grad_ref[...] = contract(feats_ref[...], dz, (0, 1))
    turned_ref[...] = item_feats_ref[...].T


def item_gradient(scale, others, sub_ref, own_ref, z_ref, turned_ref, query_grad_ref, *refs):
    keep_ref, send_ref = refs[others:]
    cot = own_ref[...]
    for ref in refs[:others]:
        cot = cot + ref[...].astype(f32)
    cot = cot * scale
    z = z_ref[...]
    inverse = 1.0 / jnp.sqrt(jnp.sum(z * z, axis=1, keepdims=True) + epsilon)
    along = jnp.sum(z * cot, axis=1, keepdims=True) * (inverse * inverse * inverse)
    dz = (cot * inverse - z * along).astype(bf16)
    grad = jnp.dot(turned_ref[...], dz, preferred_element_type=f32)
    first = sub_ref[0] == 0
    query_grad = query_grad_ref[...]
    keep_ref[...] = jnp.where(first, query_grad, grad)
    send_ref[...] = jnp.where(first, grad, query_grad)


def call(kernel, outs, args, scratch=(), scalars=0, flops=0):
    vmem = pl.BlockSpec(memory_space=pltpu.VMEM)
    smem = pl.BlockSpec(memory_space=pltpu.SMEM)
    moved = sum(math.prod(s.shape) * s.dtype.itemsize for s in list(outs) + list(args))
    return pl.pallas_call(
        kernel,
        out_shape=tuple(jax.ShapeDtypeStruct(s.shape, s.dtype) for s in outs),
        in_specs=[smem] * scalars + [vmem] * (len(args) - scalars),
        out_specs=tuple([vmem] * len(outs)),
        scratch_shapes=list(scratch),
        compiler_params=pltpu.CompilerParams(vmem_limit_bytes=32 * 1024 * 1024),
        cost_estimate=pl.CostEstimate(flops=flops, bytes_accessed=moved, transcendentals=0),
    )(*args)


def out(shape, dtype=f32):
    return jax.ShapeDtypeStruct(shape, dtype)


def partners(count):
    if count & (count - 1) == 0:
        return [[(j, j ^ step) for j in range(count)] for step in range(1, count)]
    return [[(j, (j + step) % count) for j in range(count)] for step in range(1, count)]


def sent_back(pairs):
    return [(target, source) for source, target in pairs]


def sum_over(values, axis):
    size = lax.axis_size(axis)
    if size == 1:
        return values
    if size not in (2, 4):
        return lax.psum(values, axis)
    values = values.astype(bf16)
    got = [lax.ppermute(values, axis, pairs).astype(f32) for pairs in partners(size)]
    total = values.astype(f32) + got[0]
    return total + (got[1] + got[2]) if size == 4 else total


def scatter_sum(values, axis):
    size = lax.axis_size(axis)
    me = lax.axis_index(axis)
    piece = values.shape[0] // size
    total = lax.dynamic_slice_in_dim(values, me * piece, piece, 0)
    for pairs in partners(size):
        target = jnp.asarray([t for _, t in pairs], jnp.int32)[me] if size > 2 else 1 - me
        sent = lax.dynamic_slice_in_dim(values, target * piece, piece, 0)
        total = total + lax.ppermute(sent.astype(bf16), axis, pairs).astype(f32)
    return total


def gather_pieces(values, axis):
    size = lax.axis_size(axis)
    me = lax.axis_index(axis)
    piece = values.shape[0]
    whole = jnp.zeros((size * piece,) + values.shape[1:], values.dtype)
    whole = lax.dynamic_update_slice_in_dim(whole, values, me * piece, 0)
    for pairs in partners(size):
        source = jnp.asarray([s for s, _ in sorted(pairs, key=lambda p: p[1])], jnp.int32)[me] if size > 2 else 1 - me
        whole = lax.dynamic_update_slice_in_dim(whole, lax.ppermute(values, axis, pairs), source * piece, 0)
    return whole


def on_device(query_feats, item_feats, query_proj, item_proj, item_ids, item_counts, positives):
    count, hidden = query_feats.shape
    rows = item_feats.shape[0]
    width = query_proj.shape[1]
    scale = inverse_softness / count
    halves = rows // 128
    exchange = partners(lax.axis_size("neg"))
    others = len(exchange)
    message, item_z = call(
        item_tower,
        [out((rows + tail_rows, width), bf16), out((rows, width))],
        [item_feats, item_proj, item_ids.reshape(halves, 128), item_counts.reshape(halves, 128)],
        flops=2 * rows * hidden * width,
    )
    received = [lax.ppermute(message, "neg", pairs) for pairs in exchange]
    spots = positives.reshape(1, count)
    query_z, queries, own_weights, part, pos_items, lines = call(
        query_tower,
        [
            out((width, count)),
            out((width, count), bf16),
            out((rows, count)),
            out((width, count)),
            out((width, count)),
            out((8, count)),
        ],
        [query_feats, query_proj, message, spots],
        flops=2 * count * width * (hidden + 3 * rows),
    )
    results = call(
        functools.partial(candidates_kernel, others),
        [out((rows, width), bf16)] * others + [out((rows, width)), out((width, count)), out((1, count)), out((1, count))],
        [queries, own_weights, part, lines, spots] + received,
        scratch=[pltpu.VMEM((others, rows, count), f32)],
        flops=6 * count * width * rows * (others + 1),
    )
    pieces = results[:others]
    own_piece, weighted, sums, losses = results[others:]
    back = [lax.ppermute(piece, "neg", sent_back(pairs)) for piece, pairs in zip(pieces, exchange)]
    query_grad, turned = call(
        functools.partial(query_gradient, scale),
        [out((hidden, width)), out((hidden, rows), bf16)],
        [weighted, sums, pos_items, query_z, query_feats, item_feats],
        flops=2 * count * width * hidden,
    )
    sub = lax.axis_index("sub")
    keep, send = call(
        functools.partial(item_gradient, scale, others),
        [out((hidden, width)), out((hidden, width))],
        [sub.reshape(1).astype(jnp.int32), own_piece, item_z, turned, query_grad] + back,
        scalars=1,
        flops=2 * rows * width * hidden,
    )
    swap = [(0, 1), (1, 0)]
    half = keep + lax.ppermute(send, "sub", swap)
    half = sum_over(scatter_sum(half, "rep"), "neg").astype(bf16)
    mine = gather_pieces(half, "rep")
    other = lax.ppermute(mine, "sub", swap)
    first = sub == 0
    grad_query = jnp.where(first, mine, other).astype(f32)
    grad_item = jnp.where(first, other, mine).astype(f32)
    return (grad_query, grad_item, losses.reshape(count))


def solution(mesh):
    split = ("groups", "neg", "rep", "sub")
    return jax.shard_map(
        on_device,
        mesh=mesh,
        in_specs=(P(split, None), P(split, None), P(), P(), P(split), P(split), P(split)),
        out_specs=(P("groups", None), P("groups", None), P(split)),
        check_vma=False,
    )
```

time: 171 us -> 47.3 us (0.28)
  waiting for transfers between devices: 106 us -> 19.5 us
  blocking collectives: 27.6 us -> 0 us
  starting transfers between devices: 0.08 us -> 17.8 us
  between operations: 14.2 us -> 0.77 us
  local copies, waits for them, and re-layouts: 12.2 us -> 3.64 us
  matrix products: 8.54 us -> 0 us
  Pallas kernels: 0 us -> 4.48 us
    psum x1 -> x0, waiting for transfers between devices: 85.4 us -> none  [on_device(): lax.psum((grad_query, grad_item), ('neg', 'rep', 'sub'))]
    all_gather x2 -> x0, blocking collectives: 27.6 us -> none  [the longest x1 15.6 us: on_device(): lax.all_gather(items, 'neg', axis=0, tiled=True)]
    reduce_scatter x1 -> x0, waiting for transfers between devices: 20.5 us -> none  [on_device(): lax.psum_scatter(pieces.reshape(lax.axis_size('neg') * i_rows, width), 'n...]
    ppermute x0 -> x13, waiting for transfers between devices: none -> 19.5 us  [the longest x3 4.22 us: on_device(): received = [lax.ppermute(message, 'neg', pairs) for pairs in exchange]]
    ppermute x0 -> x13, starting transfers between devices: none -> 17.8 us  [the longest x3 5.68 us: on_device(): received = [lax.ppermute(message, 'neg', pairs) for pairs in exchange]]
    dot_general x7 -> x0, matrix products: 8.54 us -> none  [the longest x1 1.92 us: on_device(): jnp.einsum('qd,qe->de', item_feats, item_dz, preferred_element_type=jnp.f...]
    gather x4 -> x0, local copies, waits for them, and re-layouts: 8.47 us -> none  [the longest x1 3.51 us: on_device(): pos_ids = jnp.take(item_ids, positives)]
    pallas_call x0 -> x5, Pallas kernels: none -> 4.48 us  [call(): pl.pallas_call(kernel, out_shape=tuple((jax.ShapeDtypeStruct(s.shape, s.d...]
  transfers between devices with their start and end apart: 2 -> 13, of which waited for: 2 -> 10; matrix products, arithmetic and copies ran while one was open for 3% -> 0% of each run, Pallas kernels for 0% -> 3%
where the time goes in v1:
time: 47.3 us; the launch traced here: 47.1 us
  waiting for transfers between devices  19.5 us (41%)
  starting transfers between devices  17.8 us (38%)
  Pallas kernels  4.48 us (9%)
  local copies, waits for them, and re-layouts  3.64 us (8%)
  other arithmetic  0.94 us (2%)
  between operations  0.77 us (2%)
    ppermute x3, starting transfers between devices, on_device(): received = [lax.ppermute(message, 'neg', pairs) for pairs in exchange]  5.68 us
    pallas_call x5, Pallas kernels, call(): pl.pallas_call(kernel, out_shape=tuple((jax.ShapeDtypeStruct(s.shape, s.d...  4.48 us
    ppermute x3, starting transfers between devices, sum_over(): lax.ppermute(values, axis, pairs).astype(f32)  4.45 us
    ppermute x3, starting transfers between devices, on_device(): lax.ppermute(piece, 'neg', sent_back(pairs))  4.39 us
    ppermute x3, waiting for transfers between devices, on_device(): received = [lax.ppermute(message, 'neg', pairs) for pairs in exchange]  4.22 us
    ppermute x3, waiting for transfers between devices, on_device(): lax.ppermute(piece, 'neg', sent_back(pairs))  3.73 us
    unnamed x18, local copies, waits for them, and re-layouts  3.59 us
    ppermute x3, waiting for transfers between devices, sum_over(): lax.ppermute(values, axis, pairs).astype(f32)  3.15 us
  transfers between devices with their start and end apart: 13, of which 10 were waited for; matrix products, arithmetic and copies ran while one was open for 0% of the time, Pallas kernels for 3%

profile of v1, /device:TPU:0, one launch (start us, length us, event | category | flops | bytes accessed | tf_op | source)
XLA Modules:
  0.0 47.1 jit_solution(5739405511895700094)
XLA Ops:
  0.6 0.0 copy-start.8
  0.6 0.0 copy-start.7
  0.7 0.7 %copy-done.8 = s32[256]{0:T(256)S(1)} copy-done((s32[256]{0:T(256)S(1)}, s32[256]{0:T(256)}, u32[]{:S(2)}) %copy-start.8) | copy-done | bytes 1048
  1.3 0.0 copy-done.7
  1.3 0.0 copy-start.2
  1.3 0.9 %copy-done.2 = bf16[256,512]{1,0:T(8,128)(2,1)S(1)} copy-done((bf16[256,512]{1,0:T(8,128)(2,1)S(1)}, bf16[256,512]{1,0:T(8,128)(2,1)}, u32[]{:S(2)}) %copy-start.2) | copy-done | bytes 262168
  2.3 0.0 copy-start.4
  2.3 0.9 %copy-done.4 = bf16[512,128]{1,0:T(8,128)(2,1)S(1)} copy-done((bf16[512,128]{1,0:T(8,128)(2,1)S(1)}, bf16[512,128]{1,0:T(8,128)(2,1)}, u32[]{:S(2)}) %copy-start.4) | copy-done | bytes 131096
  3.2 0.0 copy-start.5
  3.2 0.3 shard_map.94
  3.5 0.0 copy-start.6
  3.5 3.1 %collective-permute-start = (bf16[272,128]{1,0:T(8,128)(2,1)S(1)}, bf16[272,128]{1,0:T(8,128)(2,1)S(1)}, u32[]{:S(2)}, u32[]{:S(2)}) collective-permute-start(bf16[272,128]{1,0:T(8,128)(2,1)S(1)} %get-tuple-element.22.message_ref), channel_id=1, source_target_pairs={{0,4},{4,0},{8,12},{12,8},{1,5},{5,1},{9,13},{13,9},{2,6},{6,2},{1... | collective-permute-start | bytes 208904 | tf_op jit(solution)/shard_map/ppermute | solution.py:250
  6.6 2.6 %collective-permute-start.1 = (bf16[272,128]{1,0:T(8,128)(2,1)S(1)}, bf16[272,128]{1,0:T(8,128)(2,1)S(1)}, u32[]{:S(2)}, u32[]{:S(2)}) collective-permute-start(bf16[272,128]{1,0:T(8,128)(2,1)S(1)} %get-tuple-element.22.message_ref), channel_id=1, source_target_pairs={{0,8},{4,12},{8,0},{12,4},{1,9},{5,13},{9,1},{13,5},{2,10},{6,14},... | collective-permute-start | bytes 208904 | tf_op jit(solution)/shard_map/ppermute | solution.py:250
  9.2 0.0 collective-permute-start.2
  9.2 0.0 copy-done.5
  9.2 0.0 copy-done.6
  9.2 0.0 copy-start
  9.2 1.0 %copy-done = bf16[512,512]{1,0:T(8,128)(2,1)S(1)} copy-done((bf16[512,512]{1,0:T(8,128)(2,1)S(1)}, bf16[512,512]{1,0:T(8,128)(2,1)}, u32[]{:S(2)}) %copy-start) | copy-done | bytes 524312
  10.2 0.9 %shard_map.95 = (f32[128,512]{1,0:T(8,128)S(1)}, bf16[128,512]{1,0:T(8,128)(2,1)S(1)}, f32[256,512]{1,0:T(8,128)S(1)}, f32[128,512]{1,0:T(8,128)S(1)}, f32[128,512]{1,0:T(8,128)S(1)}, /*index=5*/f32[8,512]{1,0:T(8,128)S(1)}) custom-call(bf16[512,512]{1,0:T(8,128)(2,1)S(1)} %copy-done, bf16[512,128]{1,0:T(8,128)(2,1)S(1)} %copy-done.5, ...), custom_call_target="tpu_custom_call" | custom-call | flops 167772160 | bytes 2185216 | tf_op jit(solution)/shard_map/pallas_call | solution.py:175
  11.2 0.0 collective-permute-done.refs_0_
  11.2 2.9 %collective-permute-done.1.refs_1_ = bf16[272,128]{1,0:T(8,128)(2,1)S(1)} collective-permute-done((bf16[272,128]{1,0:T(8,128)(2,1)S(1)}, bf16[272,128]{1,0:T(8,128)(2,1)S(1)}, u32[]{:S(2)}, u32[]{:S(2)}) %collective-permute-start.1) | collective-permute-done | bytes 69664 | tf_op jit(solution)/shard_map/ppermute | solution.py:250
  14.1 1.3 %collective-permute-done.2.refs_2_ = bf16[272,128]{1,0:T(8,128)(2,1)S(1)} collective-permute-done((bf16[272,128]{1,0:T(8,128)(2,1)S(1)}, bf16[272,128]{1,0:T(8,128)(2,1)S(1)}, u32[]{:S(2)}, u32[]{:S(2)}) %collective-permute-start.2) | collective-permute-done | bytes 69664 | tf_op jit(solution)/shard_map/ppermute | solution.py:250
  15.4 0.0 copy-start.1
  15.4 0.0 copy-start.3
  15.4 2.5 %shard_map.96 = (bf16[256,128]{1,0:T(8,128)(2,1)S(1)}, bf16[256,128]{1,0:T(8,128)(2,1)S(1)}, bf16[256,128]{1,0:T(8,128)(2,1)S(1)}, f32[256,128]{1,0:T(8,128)S(1)...) custom-call(bf16[128,512]{1,0:T(8,128)(2,1)S(1)} %get-tuple-element.23.query_ref, ...), custom_call_target="tpu_custom_call" | custom-call | flops 402653184 | bytes 1738752 | tf_op jit(solution)/shard_map/pallas_call | solution.py:175
  17.9 0.8 %collective-permute-start.3 = (bf16[256,128]{1,0:T(8,128)(2,1)S(1)}, bf16[256,128]{1,0:T(8,128)(2,1)S(1)}, u32[]{:S(2)}, u32[]{:S(2)}) collective-permute-start(bf16[256,128]{1,0:T(8,128)(2,1)S(1)} %get-tuple-element.35), channel_id=1, source_target_pairs={{4,0},{0,4},{12,8},{8,12},{5,1},{1,5},{13,9},{9,13},{6,2},{2,6},{1... | collective-permute-start | bytes 196616 | tf_op jit(solution)/shard_map/ppermute | solution.py:274
  18.7 1.7 %collective-permute-start.4 = (bf16[256,128]{1,0:T(8,128)(2,1)S(1)}, bf16[256,128]{1,0:T(8,128)(2,1)S(1)}, u32[]{:S(2)}, u32[]{:S(2)}) collective-permute-start(bf16[256,128]{1,0:T(8,128)(2,1)S(1)} %get-tuple-element.36), channel_id=1, source_target_pairs={{8,0},{12,4},{0,8},{4,12},{9,1},{13,5},{1,9},{5,13},{10,2},{14,6},... | collective-permute-start | bytes 196616 | tf_op jit(solution)/shard_map/ppermute | solution.py:274
  20.4 1.9 %collective-permute-start.5 = (bf16[256,128]{1,0:T(8,128)(2,1)S(1)}, bf16[256,128]{1,0:T(8,128)(2,1)S(1)}, u32[]{:S(2)}, u32[]{:S(2)}) collective-permute-start(bf16[256,128]{1,0:T(8,128)(2,1)S(1)} %get-tuple-element.37), channel_id=1, source_target_pairs={{12,0},{8,4},{4,8},{0,12},{13,1},{9,5},{5,9},{1,13},{14,2},{10,6},... | collective-permute-start | bytes 196616 | tf_op jit(solution)/shard_map/ppermute | solution.py:274
  22.3 0.0 copy-done.1
  22.3 0.0 copy-done.3
  22.3 0.4 shard_map.97
  22.7 0.0 collective-permute-done.3.refs_0_
  22.7 2.0 %collective-permute-done.4.refs_1_ = bf16[256,128]{1,0:T(8,128)(2,1)S(1)} collective-permute-done((bf16[256,128]{1,0:T(8,128)(2,1)S(1)}, bf16[256,128]{1,0:T(8,128)(2,1)S(1)}, u32[]{:S(2)}, u32[]{:S(2)}) %collective-permute-start.4) | collective-permute-done | bytes 65568 | tf_op jit(solution)/shard_map/ppermute | solution.py:274
  24.8 1.7 %collective-permute-done.5.refs_2_ = bf16[256,128]{1,0:T(8,128)(2,1)S(1)} collective-permute-done((bf16[256,128]{1,0:T(8,128)(2,1)S(1)}, bf16[256,128]{1,0:T(8,128)(2,1)S(1)}, u32[]{:S(2)}, u32[]{:S(2)}) %collective-permute-start.5) | collective-permute-done | bytes 65568 | tf_op jit(solution)/shard_map/ppermute | solution.py:274
  26.5 0.3 shard_map.98
  26.8 0.1 collective-permute-start.6
  26.9 1.5 %collective-permute-done.6 = f32[512,128]{1,0:T(8,128)S(1)} collective-permute-done((f32[512,128]{1,0:T(8,128)S(1)}, f32[512,128]{1,0:T(8,128)S(1)}, u32[]{:S(2)}, u32[]{:S(2)}) %collective-permute-start.6) | collective-permute-done | bytes 262176 | tf_op jit(solution)/shard_map/ppermute | solution.py:290
  28.5 1.6 %collective-permute-start.7 = (bf16[256,128]{1,0:T(8,128)(2,1)S(1)}, bf16[256,128]{1,0:T(8,128)(2,1)S(1)}, u32[]{:S(2)}, u32[]{:S(2)}) collective-permute-start(bf16[256,128]{1,0:T(8,128)(2,1)S(1)} %dynamic-slice_convert_fusion), channel_id=1, source_target_pairs={{0,2},{2,0},{1,3},{3,1},{4,6},{6,4},{5,7},{7,5},{8,10},{10,8},{9,1... | collective-permute-start | bytes 196616 | tf_op jit(solution)/shard_map/ppermute | solution.py:220
  30.0 2.8 %collective-permute-done.7 = bf16[256,128]{1,0:T(8,128)(2,1)S(1)} collective-permute-done((bf16[256,128]{1,0:T(8,128)(2,1)S(1)}, bf16[256,128]{1,0:T(8,128)(2,1)S(1)}, u32[]{:S(2)}, u32[]{:S(2)}) %collective-permute-start.7) | collective-permute-done | bytes 65568 | tf_op jit(solution)/shard_map/ppermute | solution.py:220
  32.8 2.0 %collective-permute-start.10 = (bf16[256,128]{1,0:T(8,128)(2,1)S(1)}, bf16[256,128]{1,0:T(8,128)(2,1)S(1)}, u32[]{:S(2)}, u32[]{:S(2)}) collective-permute-start(bf16[256,128]{1,0:T(8,128)(2,1)S(1)} %add_convert_fusion.1), channel_id=1, source_target_pairs={{0,12},{4,8},{8,4},{12,0},{1,13},{5,9},{9,5},{13,1},{2,14},{6,10},... | collective-permute-start | bytes 196616 | tf_op jit(solution)/shard_map/ppermute | solution.py:207
  34.8 0.0 collective-permute-start.8
  34.8 2.4 %collective-permute-start.9 = (bf16[256,128]{1,0:T(8,128)(2,1)S(1)}, bf16[256,128]{1,0:T(8,128)(2,1)S(1)}, u32[]{:S(2)}, u32[]{:S(2)}) collective-permute-start(bf16[256,128]{1,0:T(8,128)(2,1)S(1)} %add_convert_fusion.1), channel_id=1, source_target_pairs={{0,8},{4,12},{8,0},{12,4},{1,9},{5,13},{9,1},{13,5},{2,10},{6,14},... | collective-permute-start | bytes 196616 | tf_op jit(solution)/shard_map/ppermute | solution.py:207
  37.3 2.4 %collective-permute-done.10 = bf16[256,128]{1,0:T(8,128)(2,1)S(1)} collective-permute-done((bf16[256,128]{1,0:T(8,128)(2,1)S(1)}, bf16[256,128]{1,0:T(8,128)(2,1)S(1)}, u32[]{:S(2)}, u32[]{:S(2)}) %collective-permute-start.10) | collective-permute-done | bytes 65568 | tf_op jit(solution)/shard_map/ppermute | solution.py:207
  39.7 0.8 %collective-permute-done.8 = bf16[256,128]{1,0:T(8,128)(2,1)S(1)} collective-permute-done((bf16[256,128]{1,0:T(8,128)(2,1)S(1)}, bf16[256,128]{1,0:T(8,128)(2,1)S(1)}, u32[]{:S(2)}, u32[]{:S(2)}) %collective-permute-start.8) | collective-permute-done | bytes 65568 | tf_op jit(solution)/shard_map/ppermute | solution.py:207
  40.4 0.0 collective-permute-done.9
  40.5 0.1 constant_dynamic-update-slice_fusion.1
  40.5 1.6 %collective-permute-start.11 = (bf16[256,128]{1,0:T(8,128)(2,1)S(1)}, bf16[256,128]{1,0:T(8,128)(2,1)S(1)}, u32[]{:S(2)}, u32[]{:S(2)}) collective-permute-start(bf16[256,128]{1,0:T(8,128)(2,1)S(1)} %get-tuple-element.42), channel_id=1, source_target_pairs={{0,2},{2,0},{1,3},{3,1},{4,6},{6,4},{5,7},{7,5},{8,10},{10,8},{9,1... | collective-permute-start | bytes 196616 | tf_op jit(solution)/shard_map/ppermute | solution.py:232
  42.1 2.8 %collective-permute-done.11 = bf16[256,128]{1,0:T(8,128)(2,1)S(1)} collective-permute-done((bf16[256,128]{1,0:T(8,128)(2,1)S(1)}, bf16[256,128]{1,0:T(8,128)(2,1)S(1)}, u32[]{:S(2)}, u32[]{:S(2)}) %collective-permute-start.11) | collective-permute-done | bytes 65568 | tf_op jit(solution)/shard_map/ppermute | solution.py:232
  44.9 0.1 collective-permute-start.12
  44.9 1.3 %collective-permute-done.12 = bf16[512,128]{1,0:T(8,128)(2,1)S(1)} collective-permute-done((bf16[512,128]{1,0:T(8,128)(2,1)S(1)}, bf16[512,128]{1,0:T(8,128)(2,1)S(1)}, u32[]{:S(2)}, u32[]{:S(2)}) %collective-permute-start.12) | collective-permute-done | bytes 131104 | tf_op jit(solution)/shard_map/ppermute | solution.py:293
  46.3 0.8 %select_convert_fusion = (f32[512,128]{1,0:T(8,128)}, f32[512,128]{1,0:T(8,128)}) fusion(bf16[512,128]{1,0:T(8,128)(2,1)S(1)} %collective-permute-done.12, bf16[512,128]{1,0:T(8,128)(2,1)S(1)} %constant_dynamic-update-slice_fusion, pred[]{:T(512)S(6)} %eq.3), kind=kLoop, calls=%fused_computation | loop fusion | flops 262144 | bytes 786433 | tf_op jit(solution)/shard_map/convert_element_type | solution.py:296
  (5 shorter events, 0.1 us)
Async XLA Ops:
  0.6 0.7 %copy-start.8 = (s32[256]{0:T(256)S(1)}, s32[256]{0:T(256)}, u32[]{:S(2)}) copy-start(s32[256]{0:T(256)} %param.12) | copy-start | bytes 3076
  0.6 0.7 %copy-start.7 = (s32[256]{0:T(256)S(1)}, s32[256]{0:T(256)}, u32[]{:S(2)}) copy-start(s32[256]{0:T(256)} %param.11) | copy-start | bytes 3076
  1.3 0.9 %copy-start.2 = (bf16[256,512]{1,0:T(8,128)(2,1)S(1)}, bf16[256,512]{1,0:T(8,128)(2,1)}, u32[]{:S(2)}) copy-start(bf16[256,512]{1,0:T(8,128)(2,1)} %item_feats_ref.1) | copy-start | bytes 786436
  2.3 0.9 %copy-start.4 = (bf16[512,128]{1,0:T(8,128)(2,1)S(1)}, bf16[512,128]{1,0:T(8,128)(2,1)}, u32[]{:S(2)}) copy-start(bf16[512,128]{1,0:T(8,128)(2,1)} %proj_ref.2) | copy-start | bytes 393220
  3.2 6.0 %copy-start.5 = (bf16[512,128]{1,0:T(8,128)(2,1)S(1)}, bf16[512,128]{1,0:T(8,128)(2,1)}, u32[]{:S(2)}) copy-start(bf16[512,128]{1,0:T(8,128)(2,1)} %proj_ref.3) | copy-start | bytes 393220
  3.5 5.7 %copy-start.6 = (s32[512]{0:T(512)S(1)}, s32[512]{0:T(512)}, u32[]{:S(2)}) copy-start(s32[512]{0:T(512)} %param.13) | copy-start | bytes 6148
  3.5 7.7 %collective-permute-start = (bf16[272,128]{1,0:T(8,128)(2,1)S(1)}, bf16[272,128]{1,0:T(8,128)(2,1)S(1)}, u32[]{:S(2)}, u32[]{:S(2)}) collective-permute-start(bf16[272,128]{1,0:T(8,128)(2,1)S(1)} %get-tuple-element.22.message_ref), channel_id=1, source_target_pairs={{0,4},{4,0},{8,12},{12,8},{1,5},{5,1},{9,13},{13,9},{2,6},{6,2},{1... | collective-permute-start | bytes 208904 | tf_op jit(solution)/shard_map/ppermute | solution.py:250
  6.6 7.5 %collective-permute-start.1 = (bf16[272,128]{1,0:T(8,128)(2,1)S(1)}, bf16[272,128]{1,0:T(8,128)(2,1)S(1)}, u32[]{:S(2)}, u32[]{:S(2)}) collective-permute-start(bf16[272,128]{1,0:T(8,128)(2,1)S(1)} %get-tuple-element.22.message_ref), channel_id=1, source_target_pairs={{0,8},{4,12},{8,0},{12,4},{1,9},{5,13},{9,1},{13,5},{2,10},{6,14},... | collective-permute-start | bytes 208904 | tf_op jit(solution)/shard_map/ppermute | solution.py:250
  9.2 6.2 %collective-permute-start.2 = (bf16[272,128]{1,0:T(8,128)(2,1)S(1)}, bf16[272,128]{1,0:T(8,128)(2,1)S(1)}, u32[]{:S(2)}, u32[]{:S(2)}) collective-permute-start(bf16[272,128]{1,0:T(8,128)(2,1)S(1)} %get-tuple-element.22.message_ref), channel_id=1, source_target_pairs={{0,12},{4,8},{8,4},{12,0},{1,13},{5,9},{9,5},{13,1},{2,14},{6,10},... | collective-permute-start | bytes 208904 | tf_op jit(solution)/shard_map/ppermute | solution.py:250
  9.2 1.0 %copy-start = (bf16[512,512]{1,0:T(8,128)(2,1)S(1)}, bf16[512,512]{1,0:T(8,128)(2,1)}, u32[]{:S(2)}) copy-start(bf16[512,512]{1,0:T(8,128)(2,1)} %feats_ref.5) | copy-start | bytes 1572868
  15.4 6.9 %copy-start.1 = (bf16[512,512]{1,0:T(8,128)(2,1)S(1)}, bf16[512,512]{1,0:T(8,128)(2,1)}, u32[]{:S(2)}) copy-start(bf16[512,512]{1,0:T(8,128)(2,1)} %feats_ref.5) | copy-start | bytes 1572868
  15.4 6.9 %copy-start.3 = (bf16[256,512]{1,0:T(8,128)(2,1)S(1)}, bf16[256,512]{1,0:T(8,128)(2,1)}, u32[]{:S(2)}) copy-start(bf16[256,512]{1,0:T(8,128)(2,1)} %item_feats_ref.1) | copy-start | bytes 786436
  17.9 4.8 %collective-permute-start.3 = (bf16[256,128]{1,0:T(8,128)(2,1)S(1)}, bf16[256,128]{1,0:T(8,128)(2,1)S(1)}, u32[]{:S(2)}, u32[]{:S(2)}) collective-permute-start(bf16[256,128]{1,0:T(8,128)(2,1)S(1)} %get-tuple-element.35), channel_id=1, source_target_pairs={{4,0},{0,4},{12,8},{8,12},{5,1},{1,5},{13,9},{9,13},{6,2},{2,6},{1... | collective-permute-start | bytes 196616 | tf_op jit(solution)/shard_map/ppermute | solution.py:274
  18.7 6.1 %collective-permute-start.4 = (bf16[256,128]{1,0:T(8,128)(2,1)S(1)}, bf16[256,128]{1,0:T(8,128)(2,1)S(1)}, u32[]{:S(2)}, u32[]{:S(2)}) collective-permute-start(bf16[256,128]{1,0:T(8,128)(2,1)S(1)} %get-tuple-element.36), channel_id=1, source_target_pairs={{8,0},{12,4},{0,8},{4,12},{9,1},{13,5},{1,9},{5,13},{10,2},{14,6},... | collective-permute-start | bytes 196616 | tf_op jit(solution)/shard_map/ppermute | solution.py:274
  20.4 6.1 %collective-permute-start.5 = (bf16[256,128]{1,0:T(8,128)(2,1)S(1)}, bf16[256,128]{1,0:T(8,128)(2,1)S(1)}, u32[]{:S(2)}, u32[]{:S(2)}) collective-permute-start(bf16[256,128]{1,0:T(8,128)(2,1)S(1)} %get-tuple-element.37), channel_id=1, source_target_pairs={{12,0},{8,4},{4,8},{0,12},{13,1},{9,5},{5,9},{1,13},{14,2},{10,6},... | collective-permute-start | bytes 196616 | tf_op jit(solution)/shard_map/ppermute | solution.py:274
  26.8 1.6 %collective-permute-start.6 = (f32[512,128]{1,0:T(8,128)S(1)}, f32[512,128]{1,0:T(8,128)S(1)}, u32[]{:S(2)}, u32[]{:S(2)}) collective-permute-start(f32[512,128]{1,0:T(8,128)S(1)} %get-tuple-element.39), channel_id=1, source_target_pairs={{0,1},{1,0},{2,3},{3,2},{4,5},{5,4},{6,7},{7,6},{8,9},{9,8},{10,11... | collective-permute-start | bytes 786440 | tf_op jit(solution)/shard_map/ppermute | solution.py:290
  28.5 4.3 %collective-permute-start.7 = (bf16[256,128]{1,0:T(8,128)(2,1)S(1)}, bf16[256,128]{1,0:T(8,128)(2,1)S(1)}, u32[]{:S(2)}, u32[]{:S(2)}) collective-permute-start(bf16[256,128]{1,0:T(8,128)(2,1)S(1)} %dynamic-slice_convert_fusion), channel_id=1, source_target_pairs={{0,2},{2,0},{1,3},{3,1},{4,6},{6,4},{5,7},{7,5},{8,10},{10,8},{9,1... | collective-permute-start | bytes 196616 | tf_op jit(solution)/shard_map/ppermute | solution.py:220
  32.8 6.8 %collective-permute-start.10 = (bf16[256,128]{1,0:T(8,128)(2,1)S(1)}, bf16[256,128]{1,0:T(8,128)(2,1)S(1)}, u32[]{:S(2)}, u32[]{:S(2)}) collective-permute-start(bf16[256,128]{1,0:T(8,128)(2,1)S(1)} %add_convert_fusion.1), channel_id=1, source_target_pairs={{0,12},{4,8},{8,4},{12,0},{1,13},{5,9},{9,5},{13,1},{2,14},{6,10},... | collective-permute-start | bytes 196616 | tf_op jit(solution)/shard_map/ppermute | solution.py:207
  34.8 5.6 %collective-permute-start.8 = (bf16[256,128]{1,0:T(8,128)(2,1)S(1)}, bf16[256,128]{1,0:T(8,128)(2,1)S(1)}, u32[]{:S(2)}, u32[]{:S(2)}) collective-permute-start(bf16[256,128]{1,0:T(8,128)(2,1)S(1)} %add_convert_fusion.1), channel_id=1, source_target_pairs={{0,4},{4,0},{8,12},{12,8},{1,5},{5,1},{9,13},{13,9},{2,6},{6,2},{1... | collective-permute-start | bytes 196616 | tf_op jit(solution)/shard_map/ppermute | solution.py:207
  34.8 5.6 %collective-permute-start.9 = (bf16[256,128]{1,0:T(8,128)(2,1)S(1)}, bf16[256,128]{1,0:T(8,128)(2,1)S(1)}, u32[]{:S(2)}, u32[]{:S(2)}) collective-permute-start(bf16[256,128]{1,0:T(8,128)(2,1)S(1)} %add_convert_fusion.1), channel_id=1, source_target_pairs={{0,8},{4,12},{8,0},{12,4},{1,9},{5,13},{9,1},{13,5},{2,10},{6,14},... | collective-permute-start | bytes 196616 | tf_op jit(solution)/shard_map/ppermute | solution.py:207
  40.5 4.3 %collective-permute-start.11 = (bf16[256,128]{1,0:T(8,128)(2,1)S(1)}, bf16[256,128]{1,0:T(8,128)(2,1)S(1)}, u32[]{:S(2)}, u32[]{:S(2)}) collective-permute-start(bf16[256,128]{1,0:T(8,128)(2,1)S(1)} %get-tuple-element.42), channel_id=1, source_target_pairs={{0,2},{2,0},{1,3},{3,1},{4,6},{6,4},{5,7},{7,5},{8,10},{10,8},{9,1... | collective-permute-start | bytes 196616 | tf_op jit(solution)/shard_map/ppermute | solution.py:232
  44.9 1.4 %collective-permute-start.12 = (bf16[512,128]{1,0:T(8,128)(2,1)S(1)}, bf16[512,128]{1,0:T(8,128)(2,1)S(1)}, u32[]{:S(2)}, u32[]{:S(2)}) collective-permute-start(bf16[512,128]{1,0:T(8,128)(2,1)S(1)} %constant_dynamic-update-slice_fusion), channel_id=1, source_target_pairs={{0,1},{1,0},{2,3},{3,2},{4,5},{5,4},{6,7},{7,6},{8,9},{9,8},{10,11... | collective-permute-start | bytes 393224 | tf_op jit(solution)/shard_map/ppermute | solution.py:293

commit v2 on v1

v2 whole, which is shorter than its diff:
```python
import functools
import math

import jax
import jax.numpy as jnp
from jax import lax
from jax.experimental import pallas as pl
from jax.experimental.pallas import tpu as pltpu
from jax.sharding import PartitionSpec as P

inverse_softness = 20.0
epsilon = 1e-06
log2e = math.log2(math.e)
ln2 = math.log(2.0)
tail_rows = 16
f32 = jnp.float32
bf16 = jnp.bfloat16


def contract(lhs, rhs, over):
    return lax.dot_general(lhs, rhs, (((over[0],), (over[1],)), ((), ())), preferred_element_type=f32)


def split_terms(values):
    terms = []
    for _ in range(3):
        term = values.astype(bf16).astype(f32)
        terms.append(term)
        values = values - term
    return terms


def item_tower(feats_hbm, proj_hbm, ids_hbm, counts_hbm, message_ref, z_ref, feats_ref, proj_ref, ids_ref, counts_ref, sems):
    pairs = ((ids_hbm, ids_ref), (counts_hbm, counts_ref), (proj_hbm, proj_ref), (feats_hbm, feats_ref))
    copies = [pltpu.make_async_copy(source, target, sems.at[k]) for k, (source, target) in enumerate(pairs)]
    for copy in copies:
        copy.start()
    rows = feats_ref.shape[0]
    copies[0].wait()
    copies[1].wait()
    ids = ids_ref[...]
    digits = [ids >> 16, (ids >> 8) & 255, ids & 255]
    log_counts = jnp.log(counts_ref[...].astype(f32)) * log2e
    lines = [digit.astype(f32) for digit in digits] + split_terms(log_counts)
    halves = ids.shape[0]
    lines.append(jnp.zeros((tail_rows - 6 * halves, ids.shape[1]), f32))
    message_ref[rows : rows + tail_rows, :] = jnp.concatenate(lines, axis=0).astype(bf16)
    copies[2].wait()
    copies[3].wait()
    z = jnp.dot(feats_ref[...], proj_ref[...], preferred_element_type=f32)
    z_ref[...] = z
    inverse = 1.0 / jnp.sqrt(jnp.sum(z * z, axis=1, keepdims=True) + epsilon)
    message_ref[0:rows, :] = (z * inverse).astype(bf16)


def item_columns(message_ref, half, halves):
    rows = message_ref.shape[0] - tail_rows
    tail = message_ref[rows : rows + tail_rows, :]
    line = lax.broadcasted_iota(jnp.int32, (tail_rows, 128), 0)

    def weights(scales, first):
        table = jnp.zeros((tail_rows, 128), f32)
        for step, scale in enumerate(scales):
            table = jnp.where(line == (first + step) * halves + half, scale, table)
        return table.astype(bf16)

    ids = contract(tail, weights((65536.0, 256.0, 1.0), 0), (0, 0))
    logs = contract(tail, weights((1.0, 1.0, 1.0), 3), (0, 0))
    return ids, logs


def wide(column, width):
    return jnp.concatenate([column] * (width // column.shape[1]), axis=1)


def block_scores(message_ref, queries, half):
    items = message_ref[half * 128 : half * 128 + 128, :]
    ids, logs = item_columns(message_ref, half, (message_ref.shape[0] - tail_rows) // 128)
    return items, ids, logs, jnp.dot(items, queries, preferred_element_type=f32)


def query_tower(
    feats_ref,
    proj_ref,
    message_ref,
    positives_ref,
    item_feats_ref,
    z_ref,
    query_ref,
    plain_ref,
    weights_ref,
    weighted_ref,
    pos_ref,
    lines_ref,
    turned_ref,
    item_turned_ref,
):
    rows = message_ref.shape[0] - tail_rows
    halves = rows // 128
    z = contract(proj_ref[...], feats_ref[...], (0, 1))
    z_ref[...] = z
    inverse = 1.0 / jnp.sqrt(jnp.sum(z * z, axis=0, keepdims=True) + epsilon)
    scaled = z * inverse
    queries = scaled.astype(bf16)
    query_ref[...] = queries
    plain_ref[...] = queries.T
    count = queries.shape[1]
    positives = positives_ref[...]
    tail = message_ref[rows : rows + tail_rows, :]
    own = []
    pos_id = jnp.zeros((1, count), f32)
    for half in range(halves):
        spot = lax.broadcasted_iota(jnp.int32, (128, count), 0) + half * 128
        own.append(spot == positives)
        found = jnp.dot(tail, own[half].astype(f32).astype(bf16), preferred_element_type=f32)
        for step, scale in enumerate((65536.0, 256.0, 1.0)):
            line = step * halves + half
            pos_id = pos_id + scale * found[line : line + 1, :]
    totals = jnp.zeros((1, count), f32)
    target = jnp.zeros((1, count), f32)
    weighted = jnp.zeros((queries.shape[0], count), f32)
    pos_items = jnp.zeros((queries.shape[0], count), f32)
    for half in range(halves):
        items, ids, logs, scores = block_scores(message_ref, queries, half)
        scores = scores * (inverse_softness * log2e) - wide(logs, count)
        collide = (wide(ids, count) == pos_id) & jnp.logical_not(own[half])
        weights = jnp.where(collide, 0.0, jnp.exp2(scores))
        weights_ref[half * 128 : half * 128 + 128, :] = weights
        totals = totals + jnp.sum(weights, axis=0, keepdims=True)
        target = target + jnp.sum(jnp.where(own[half], scores, 0.0), axis=0, keepdims=True)
        weighted = weighted + contract(items, weights.astype(bf16), (0, 0))
        pos_items = pos_items + contract(items, own[half].astype(f32).astype(bf16), (0, 0))
    weighted_ref[...] = weighted
    pos_ref[...] = pos_items
    lines_ref[...] = jnp.concatenate([totals, target * ln2, pos_id, jnp.zeros((5, count), f32)], axis=0)
    turned_ref[...] = feats_ref[...].T
    item_turned_ref[...] = item_feats_ref[...].T


def add_block(message_ref, query_ref, lines_ref, before_ref, totals, weights_ref, chunk=32):
    queries = query_ref[...]
    count = queries.shape[1]
    pos_id = lines_ref[2:3, :]
    weighted = before_ref[...]
    partial = jnp.zeros((8, count), f32)
    for half in range(weights_ref.shape[0] // 128):
        items, ids, logs, scores = block_scores(message_ref, queries, half)
        rounded = []
        for first in range(0, 128, chunk):
            part = slice(first, first + chunk)
            exponent = scores[part] * (inverse_softness * log2e) - wide(logs[part], count)
            weights = jnp.where(wide(ids[part], count) == pos_id, 0.0, jnp.exp2(exponent))
            weights_ref[half * 128 + first : half * 128 + first + chunk, :] = weights
            for line in range(0, chunk, 8):
                partial = partial + weights[line : line + 8]
            rounded.append(weights.astype(bf16))
        weighted = weighted + contract(items, jnp.concatenate(rounded, axis=0), (0, 0))
    return totals + jnp.sum(partial, axis=0, keepdims=True), weighted


def middle_block(message_ref, query_ref, lines_ref, before_ref, totals_ref, weights_ref, after_ref, sums_ref):
    totals, weighted = add_block(message_ref, query_ref, lines_ref, before_ref, totals_ref[0:1, :], weights_ref)
    after_ref[...] = weighted
    sums_ref[...] = jnp.broadcast_to(totals, sums_ref.shape)


def last_block(scale, others, ring, *refs):
    (
        message_ref,
        query_ref,
        plain_ref,
        lines_ref,
        before_ref,
        totals_ref,
        positives_ref,
        own_weights_ref,
        pos_ref,
        z_ref,
        turned_ref,
    ) = refs[:11]
    weights_refs = refs[11 : 10 + others]
    piece_refs = refs[10 + others : 10 + 2 * others]
    own_ref, own_grad_ref, losses_ref, last_ref, grad_ref = refs[10 + 2 * others :]
    rows, count = own_weights_ref.shape
    totals, weighted = add_block(message_ref, query_ref, lines_ref, before_ref, totals_ref[0:1, :], last_ref)
    losses_ref[...] = jnp.log(totals) - lines_ref[1:2, :]
    share = 1.0 / totals
    queries = plain_ref[...]
    for piece_ref, weights_ref in zip(piece_refs, list(weights_refs) + [last_ref]):
        grads = (weights_ref[...] * share).astype(bf16)
        piece_ref[0:rows, :] = jnp.dot(grads, queries, preferred_element_type=f32).astype(bf16)
    own = lax.broadcasted_iota(jnp.int32, (rows, count), 0) == positives_ref[...]
    grads = (own_weights_ref[...] * share - own.astype(f32)).astype(bf16)
    own_ref[...] = jnp.dot(grads, queries, preferred_element_type=f32)
    cot = (weighted * share - pos_ref[...]) * scale
    z = z_ref[...]
    inverse = 1.0 / jnp.sqrt(jnp.sum(z * z, axis=0, keepdims=True) + epsilon)
    along = jnp.sum(z * cot, axis=0, keepdims=True) * (inverse * inverse * inverse)
    dz = (cot * inverse - z * along).astype(bf16)
    grad_ref[...] = contract(turned_ref[...], dz, (1, 1))
    me = lax.axis_index("neg")
    part = grad_ref.shape[0] // ring
    own_grad_ref[...] = grad_ref[pl.ds(pl.multiple_of(me * part, part), part), :]
    for step, piece_ref in enumerate(piece_refs):
        target = source_of(me, step + 1, ring)
        piece_ref[rows : rows + part, :] = grad_ref[pl.ds(pl.multiple_of(target * part, part), part), :].astype(bf16)


def item_gradient(scale, others, own_ref, own_grad_ref, z_ref, turned_ref, *refs):
    keep_ref, send_ref = refs[others:]
    rows = own_ref.shape[0]
    cot = own_ref[...]
    query_grad = own_grad_ref[...]
    for ref in refs[:others]:
        cot = cot + ref[0:rows, :].astype(f32)
        query_grad = query_grad + ref[rows:, :].astype(f32)
    cot = cot * scale
    z = z_ref[...]
    inverse = 1.0 / jnp.sqrt(jnp.sum(z * z, axis=1, keepdims=True) + epsilon)
    along = jnp.sum(z * cot, axis=1, keepdims=True) * (inverse * inverse * inverse)
    dz = (cot * inverse - z * along).astype(bf16)
    grad = jnp.dot(turned_ref[...], dz, preferred_element_type=f32)
    first = lax.axis_index("sub") == 0
    for start, whole in ((0, grad), (grad.shape[0] // 2, query_grad)):
        half = whole.shape[0] // 2
        keep_ref[start : start + half, :] = jnp.where(first, whole[:half], whole[half:])
        send_ref[start : start + half, :] = jnp.where(first, whole[half:], whole[:half])


def add_pieces(others, item_rows, own_ref, *refs):
    out_ref = refs[others]
    values = [ref[...].astype(f32) for ref in (own_ref,) + refs[:others]]
    total = values[0] + values[1]
    if others == 3:
        total = total + (values[2] + values[3])
    query_rows = own_ref.shape[0] - item_rows
    out_ref[0:item_rows, :] = total[:item_rows].astype(bf16)
    for step, value in enumerate(values):
        start = item_rows + step * query_rows
        out_ref[start : start + query_rows, :] = value[item_rows:].astype(bf16)


def final_kernel(ring, direct, mine_ref, other_ref, query_ref, item_ref):
    sub = lax.axis_index("sub")
    base = lax.axis_index("neg") if direct else 0
    half = item_ref.shape[0] // 2
    part = half // ring
    for side, ref in ((sub, mine_ref), (1 - sub, other_ref)):
        values = ref[...].astype(f32)
        item_ref[pl.ds(pl.multiple_of(side * half, half), half), :] = values[:half]
        for step in range(ring):
            source = partner_of(base, step, ring)
            start = pl.multiple_of(source * (2 * part) + side * part, part)
            query_ref[pl.ds(start, part), :] = values[half + step * part : half + (step + 1) * part]


def call(kernel, outs, args, scratch=(), flops=0, fetch=False):
    vmem = pl.BlockSpec(memory_space=pltpu.VMEM)
    moved = sum(math.prod(s.shape) * s.dtype.itemsize for s in list(outs) + list(args))
    return pl.pallas_call(
        kernel,
        out_shape=tuple(jax.ShapeDtypeStruct(s.shape, s.dtype) for s in outs),
        in_specs=[pl.BlockSpec(memory_space=pltpu.HBM) if fetch else vmem] * len(args),
        out_specs=tuple([vmem] * len(outs)),
        scratch_shapes=list(scratch),
        compiler_params=pltpu.CompilerParams(vmem_limit_bytes=32 * 1024 * 1024),
        cost_estimate=pl.CostEstimate(flops=flops, bytes_accessed=moved, transcendentals=0),
    )(*args)


def out(shape, dtype=f32):
    return jax.ShapeDtypeStruct(shape, dtype)


def partner_of(me, step, count):
    if count & (count - 1) == 0:
        return me ^ step
    return lax.rem(me + step, count)


def source_of(me, step, count):
    return partner_of(me, step if count & (count - 1) == 0 else count - step, count)


def partners(count):
    return [[(j, int(partner_of(j, step, count))) for j in range(count)] for step in range(1, count)]


def sent_back(pairs):
    return [(target, source) for source, target in pairs]


def sum_over(values, axis):
    size = lax.axis_size(axis)
    if size == 1:
        return values
    if size not in (2, 4):
        return lax.psum(values, axis)
    values = values.astype(bf16)
    got = [lax.ppermute(values, axis, pairs).astype(f32) for pairs in partners(size)]
    total = values.astype(f32) + got[0]
    return total + (got[1] + got[2]) if size == 4 else total


def on_device(query_feats, item_feats, query_proj, item_proj, item_ids, item_counts, positives):
    count, hidden = query_feats.shape
    rows = item_feats.shape[0]
    width = query_proj.shape[1]
    scale = inverse_softness / count
    halves = rows // 128
    ring = lax.axis_size("neg")
    exchange = partners(ring)
    others = len(exchange)
    part = hidden // ring
    message, item_z = call(
        item_tower,
        [out((rows + tail_rows, width), bf16), out((rows, width))],
        [item_feats, item_proj, item_ids.reshape(halves, 128), item_counts.reshape(halves, 128)],
        scratch=[
            pltpu.VMEM((rows, hidden), bf16),
            pltpu.VMEM((hidden, width), bf16),
            pltpu.VMEM((halves, 128), jnp.int32),
            pltpu.VMEM((halves, 128), jnp.int32),
            pltpu.SemaphoreType.DMA((4,)),
        ],
        flops=2 * rows * hidden * width,
        fetch=True,
    )
    received = [lax.ppermute(message, "neg", pairs) for pairs in exchange]
    spots = positives.reshape(1, count)
    query_z, queries, plain, own_weights, weighted, pos_items, lines, turned, item_turned = call(
        query_tower,
        [
            out((width, count)),
            out((width, count), bf16),
            out((count, width), bf16),
            out((rows, count)),
            out((width, count)),
            out((width, count)),
            out((8, count)),
            out((hidden, count), bf16),
            out((hidden, rows), bf16),
        ],
        [query_feats, query_proj, message, spots, item_feats],
        flops=2 * count * width * (hidden + 3 * rows),
    )
    totals = lines
    weights = []
    for block in received[:-1]:
        block_weights, weighted, totals = call(
            middle_block,
            [out((rows, count)), out((width, count)), out((8, count))],
            [block, queries, lines, weighted, totals],
            flops=4 * count * width * rows,
        )
        weights.append(block_weights)
    results = call(
        functools.partial(last_block, scale, others, ring),
        [out((rows + part, width), bf16)] * others + [out((rows, width)), out((part, width)), out((1, count))],
        [received[-1], queries, plain, lines, weighted, totals, spots, own_weights, pos_items, query_z, turned] + weights,
        scratch=[pltpu.VMEM((rows, count), f32), pltpu.VMEM((hidden, width), f32)],
        flops=6 * count * width * rows * (others + 1),
    )
    own_piece, own_grad, losses = results[others:]
    back = [lax.ppermute(piece, "neg", sent_back(pairs)) for piece, pairs in zip(results, exchange)]
    kept = (hidden + part) // 2
    keep, send = call(
        functools.partial(item_gradient, scale, others),
        [out((kept, width)), out((kept, width))],
        [own_piece, own_grad, item_z, item_turned] + back,
        flops=2 * rows * width * hidden,
    )
    swap = [(0, 1), (1, 0)]
    half = sum_over(keep + lax.ppermute(send, "sub", swap), "rep")
    direct = ring in (2, 4)
    if direct:
        half = half.astype(bf16)
        mine = call(
            functools.partial(add_pieces, others, hidden // 2),
            [out((hidden, width), bf16)],
            [half] + [lax.ppermute(half, "neg", pairs) for pairs in exchange],
        )[0]
    else:
        item_half = lax.psum(half[: hidden // 2], "neg").astype(bf16)
        query_half = lax.all_gather(half[hidden // 2 :].astype(bf16), "neg", axis=0, tiled=True)
        mine = jnp.concatenate([item_half, query_half], axis=0)
    other = lax.ppermute(mine, "sub", swap)
    grad_query, grad_item = call(
        functools.partial(final_kernel, ring, direct),
        [out((hidden, width)), out((hidden, width))],
        [mine, other],
    )
    return (grad_query, grad_item, losses.reshape(count))


def solution(mesh):
    split = ("groups", "neg", "rep", "sub")
    return jax.shard_map(
        on_device,
        mesh=mesh,
        in_specs=(P(split, None), P(split, None), P(), P(), P(split), P(split), P(split)),
        out_specs=(P("groups", None), P("groups", None), P(split)),
        check_vma=False,
    )
```

time: 47.3 us -> 46.1 us (0.975)
  starting transfers between devices: 17.8 us -> 16.2 us
  Pallas kernels: 4.48 us -> 5.69 us
  other arithmetic: 0.94 us -> 0.04 us
    ppermute x3 -> x1, starting transfers between devices: 4.45 us -> 1.57 us  [sum_over(): lax.ppermute(values, axis, pairs).astype(f32)]
    ppermute x3, waiting for transfers between devices: 3.73 us -> 5.45 us  [on_device(): lax.ppermute(piece, 'neg', sent_back(pairs))]
    ppermute x3, waiting for transfers between devices: 4.22 us -> 2.79 us  [on_device(): received = [lax.ppermute(message, 'neg', pairs) for pairs in exchange]]
    ppermute x3 -> x4, starting transfers between devices: 3.18 us -> 4.52 us  [the longest x3 4.45 us: on_device(): lax.ppermute(half, 'neg', pairs)]
    pallas_call x5 -> x8, Pallas kernels: 4.48 us -> 5.69 us  [call(): pl.pallas_call(kernel, out_shape=tuple((jax.ShapeDtypeStruct(s.shape, s.d...]
    convert_element_type x1, other arithmetic: 0.83 us -> 0.03 us  [on_device(): half = half.astype(bf16)]
    ppermute x3 -> x1, waiting for transfers between devices: 3.15 us -> 2.99 us  [sum_over(): lax.ppermute(values, axis, pairs).astype(f32)]
    ppermute x3 -> x4, waiting for transfers between devices: 7.06 us -> 6.97 us  [the longest x3 5.59 us: on_device(): lax.ppermute(half, 'neg', pairs)]
  transfers between devices with their start and end apart: 13 -> 12, of which waited for: 10 -> 9; matrix products, arithmetic and copies ran while one was open for 0% -> 0% of each run, Pallas kernels for 3% -> 5%
where the time goes in v2:
time: 46.1 us; the launch traced here: 45.8 us
  waiting for transfers between devices  19.5 us (42%)
  starting transfers between devices  16.2 us (35%)
  Pallas kernels  5.69 us (12%)
  local copies, waits for them, and re-layouts  3.58 us (8%)
  between operations  0.75 us (2%)
    pallas_call x8, Pallas kernels, call(): pl.pallas_call(kernel, out_shape=tuple((jax.ShapeDtypeStruct(s.shape, s.d...  5.69 us
    ppermute x3, starting transfers between devices, on_device(): received = [lax.ppermute(message, 'neg', pairs) for pairs in exchange]  5.67 us
    ppermute x3, waiting for transfers between devices, on_device(): lax.ppermute(half, 'neg', pairs)  5.59 us
    ppermute x3, waiting for transfers between devices, on_device(): lax.ppermute(piece, 'neg', sent_back(pairs))  5.45 us
    ppermute x3, starting transfers between devices, on_device(): lax.ppermute(half, 'neg', pairs)  4.45 us
    ppermute x3, starting transfers between devices, on_device(): lax.ppermute(piece, 'neg', sent_back(pairs))  4.39 us
    unnamed x14, local copies, waits for them, and re-layouts  3.58 us
    ppermute x1, waiting for transfers between devices, sum_over(): lax.ppermute(values, axis, pairs).astype(f32)  2.99 us
  transfers between devices with their start and end apart: 12, of which 9 were waited for; matrix products, arithmetic and copies ran while one was open for 0% of the time, Pallas kernels for 5%

profile of v2, /device:TPU:0, one launch (start us, length us, event | category | flops | bytes accessed | tf_op | source)
XLA Modules:
  0.0 45.8 jit_solution(18155286575091667461)
XLA Ops:
  0.6 0.0 copy-start.6
  0.6 0.0 copy-start.5
  0.7 0.7 %copy-done.6 = s32[256]{0:T(256)S(1)} copy-done((s32[256]{0:T(256)S(1)}, s32[256]{0:T(256)}, u32[]{:S(2)}) %copy-start.6) | copy-done | bytes 1048
  1.3 0.0 copy-done.5
  1.3 0.0 copy-start
  1.3 0.9 %copy-done = bf16[256,512]{1,0:T(8,128)(2,1)S(1)} copy-done((bf16[256,512]{1,0:T(8,128)(2,1)S(1)}, bf16[256,512]{1,0:T(8,128)(2,1)}, u32[]{:S(2)}) %copy-start) | copy-done | bytes 262168
  2.3 0.0 copy-start.2
  2.3 0.9 %copy-done.2 = bf16[512,128]{1,0:T(8,128)(2,1)S(1)} copy-done((bf16[512,128]{1,0:T(8,128)(2,1)S(1)}, bf16[512,128]{1,0:T(8,128)(2,1)}, u32[]{:S(2)}) %copy-start.2) | copy-done | bytes 131096
  3.2 0.0 copy-start.3
  3.2 0.5 %shard_map.94 = (bf16[272,128]{1,0:T(8,128)(2,1)S(1)}, f32[256,128]{1,0:T(8,128)S(1)}) custom-call(bf16[256,512]{1,0:T(8,128)(2,1)S(1)} %copy-done, bf16[512,128]{1,0:T(8,128)(2,1)S(1)} %copy-done.2, s32[2,128]{1,0:T(2,128)S(1)} %bitcast.6, s32[2,128]{1,0:T(2,128)S(1)} %bitcast.7), custom_call_target="tpu_custom_call" | custom-call | flops 33554432 | bytes 595968 | tf_op jit(solution)/shard_map/pallas_call | solution.py:260
  3.7 0.0 copy-start.4
  3.8 3.1 %collective-permute-start.2 = (bf16[272,128]{1,0:T(8,128)(2,1)S(1)}, bf16[272,128]{1,0:T(8,128)(2,1)S(1)}, u32[]{:S(2)}, u32[]{:S(2)}) collective-permute-start(bf16[272,128]{1,0:T(8,128)(2,1)S(1)} %get-tuple-element.30.message_ref), channel_id=1, source_target_pairs={{0,4},{4,0},{8,12},{12,8},{1,5},{5,1},{9,13},{13,9},{2,6},{6,2},{1... | collective-permute-start | bytes 208904 | tf_op jit(solution)/shard_map/ppermute | solution.py:329
  6.8 2.6 %collective-permute-start.1 = (bf16[272,128]{1,0:T(8,128)(2,1)S(1)}, bf16[272,128]{1,0:T(8,128)(2,1)S(1)}, u32[]{:S(2)}, u32[]{:S(2)}) collective-permute-start(bf16[272,128]{1,0:T(8,128)(2,1)S(1)} %get-tuple-element.30.message_ref), channel_id=1, source_target_pairs={{0,8},{4,12},{8,0},{12,4},{1,9},{5,13},{9,1},{13,5},{2,10},{6,14},... | collective-permute-start | bytes 208904 | tf_op jit(solution)/shard_map/ppermute | solution.py:329
  9.4 0.0 collective-permute-start
  9.4 0.0 copy-done.3
  9.4 0.0 copy-done.4
  9.4 0.0 copy-start.1
  9.4 1.0 %copy-done.1 = bf16[512,512]{1,0:T(8,128)(2,1)S(1)} copy-done((bf16[512,512]{1,0:T(8,128)(2,1)S(1)}, bf16[512,512]{1,0:T(8,128)(2,1)}, u32[]{:S(2)}) %copy-start.1) | copy-done | bytes 524312
  10.5 1.0 %shard_map.95 = (f32[128,512]{1,0:T(8,128)S(1)}, bf16[128,512]{1,0:T(8,128)(2,1)S(1)}, bf16[512,128]{1,0:T(8,128)(2,1)S(1)}, f32[256,512]{1,0:T(8,128)S(1)}, f32...) custom-call(bf16[512,512]{1,0:T(8,128)(2,1)S(1)} %copy-done.1, ...), custom_call_target="tpu_custom_call" | custom-call | flops 167772160 | bytes 3364864 | tf_op jit(solution)/shard_map/pallas_call | solution.py:260
  11.4 0.0 collective-permute-done.2.message_ref
  11.4 0.7 %shard_map.96 = (f32[256,512]{1,0:T(8,128)S(1)}, f32[128,512]{1,0:T(8,128)S(1)}, f32[8,512]{1,0:T(8,128)S(1)}) custom-call(bf16[272,128]{1,0:T(8,128)(2,1)S(1)} %collective-permute-done.2.message_ref, bf16[128,512]{1,0:T(8,128)(2,1)S(1)} %get-tuple-element.31.query_ref.refs_1_, f32[8,512]{1,0:T(8,128)S(1)} %get-tuple-element.33.lines_ref.totals_ref.refs_3_, ...), custom_call_target="tpu_custom_call" | custom-call | flops 67108864 | bytes 1298432 | tf_op jit(solution)/shard_map/pallas_call | solution.py:260
  12.1 2.2 %collective-permute-done.1.message_ref = bf16[272,128]{1,0:T(8,128)(2,1)S(1)} collective-permute-done((bf16[272,128]{1,0:T(8,128)(2,1)S(1)}, bf16[272,128]{1,0:T(8,128)(2,1)S(1)}, u32[]{:S(2)}, u32[]{:S(2)}) %collective-permute-start.1) | collective-permute-done | bytes 69664 | tf_op jit(solution)/shard_map/ppermute | solution.py:329
  14.4 0.7 %shard_map.97 = (f32[256,512]{1,0:T(8,128)S(1)}, f32[128,512]{1,0:T(8,128)S(1)}, f32[8,512]{1,0:T(8,128)S(1)}) custom-call(bf16[272,128]{1,0:T(8,128)(2,1)S(1)} %collective-permute-done.1.message_ref, bf16[128,512]{1,0:T(8,128)(2,1)S(1)} %get-tuple-element.31.query_ref.refs_1_, f32[8,512]{1,0:T(8,128)S(1)} %get-tuple-element.33.lines_ref.totals_ref.refs_3_, ...), custom_call_target="tpu_custom_call" | custom-call | flops 67108864 | bytes 1298432 | tf_op jit(solution)/shard_map/pallas_call | solution.py:260
  15.1 0.6 %collective-permute-done.refs_0_ = bf16[272,128]{1,0:T(8,128)(2,1)S(1)} collective-permute-done((bf16[272,128]{1,0:T(8,128)(2,1)S(1)}, bf16[272,128]{1,0:T(8,128)(2,1)S(1)}, u32[]{:S(2)}, u32[]{:S(2)}) %collective-permute-start) | collective-permute-done | bytes 69664 | tf_op jit(solution)/shard_map/ppermute | solution.py:329
  15.6 1.6 %shard_map.98 = (bf16[384,128]{1,0:T(8,128)(2,1)S(1)}, bf16[384,128]{1,0:T(8,128)(2,1)S(1)}, bf16[384,128]{1,0:T(8,128)(2,1)S(1)}, f32[256,128]{1,0:T(8,128)S(1)...) custom-call(bf16[272,128]{1,0:T(8,128)(2,1)S(1)} %collective-permute-done.refs_0_, ...), custom_call_target="tpu_custom_call" | custom-call | flops 402653184 | bytes 3743744 | tf_op jit(solution)/shard_map/pallas_call | solution.py:260
  17.2 0.8 %collective-permute-start.3 = (bf16[384,128]{1,0:T(8,128)(2,1)S(1)}, bf16[384,128]{1,0:T(8,128)(2,1)S(1)}, u32[]{:S(2)}, u32[]{:S(2)}) collective-permute-start(bf16[384,128]{1,0:T(8,128)(2,1)S(1)} %get-tuple-element.49), channel_id=1, source_target_pairs={{4,0},{0,4},{12,8},{8,12},{5,1},{1,5},{13,9},{9,13},{6,2},{2,6},{1... | collective-permute-start | bytes 294920 | tf_op jit(solution)/shard_map/ppermute | solution.py:365
  18.0 2.4 %collective-permute-start.4 = (bf16[384,128]{1,0:T(8,128)(2,1)S(1)}, bf16[384,128]{1,0:T(8,128)(2,1)S(1)}, u32[]{:S(2)}, u32[]{:S(2)}) collective-permute-start(bf16[384,128]{1,0:T(8,128)(2,1)S(1)} %get-tuple-element.50), channel_id=1, source_target_pairs={{8,0},{12,4},{0,8},{4,12},{9,1},{13,5},{1,9},{5,13},{10,2},{14,6},... | collective-permute-start | bytes 294920 | tf_op jit(solution)/shard_map/ppermute | solution.py:365
  20.4 1.2 %collective-permute-start.5 = (bf16[384,128]{1,0:T(8,128)(2,1)S(1)}, bf16[384,128]{1,0:T(8,128)(2,1)S(1)}, u32[]{:S(2)}, u32[]{:S(2)}) collective-permute-start(bf16[384,128]{1,0:T(8,128)(2,1)S(1)} %get-tuple-element.51), channel_id=1, source_target_pairs={{12,0},{8,4},{4,8},{0,12},{13,1},{9,5},{5,9},{1,13},{14,2},{10,6},... | collective-permute-start | bytes 294920 | tf_op jit(solution)/shard_map/ppermute | solution.py:365
  21.6 0.2 collective-permute-done.3.refs_0_
  21.8 5.2 %collective-permute-done.4.refs_1_ = bf16[384,128]{1,0:T(8,128)(2,1)S(1)} collective-permute-done((bf16[384,128]{1,0:T(8,128)(2,1)S(1)}, bf16[384,128]{1,0:T(8,128)(2,1)S(1)}, u32[]{:S(2)}, u32[]{:S(2)}) %collective-permute-start.4) | collective-permute-done | bytes 98336 | tf_op jit(solution)/shard_map/ppermute | solution.py:365
  27.1 0.0 collective-permute-done.5.refs_2_
  27.1 0.4 shard_map.99
  27.4 0.1 collective-permute-start.6
  27.5 1.4 %collective-permute-done.6 = f32[320,128]{1,0:T(8,128)S(1)} collective-permute-done((f32[320,128]{1,0:T(8,128)S(1)}, f32[320,128]{1,0:T(8,128)S(1)}, u32[]{:S(2)}, u32[]{:S(2)}) %collective-permute-start.6) | collective-permute-done | bytes 163872 | tf_op jit(solution)/shard_map/ppermute | solution.py:374
  28.9 1.6 %collective-permute-start.7 = (bf16[320,128]{1,0:T(8,128)(2,1)S(1)}, bf16[320,128]{1,0:T(8,128)(2,1)S(1)}, u32[]{:S(2)}, u32[]{:S(2)}) collective-permute-start(bf16[320,128]{1,0:T(8,128)(2,1)S(1)} %add_convert_fusion.1), channel_id=1, source_target_pairs={{0,2},{2,0},{1,3},{3,1},{4,6},{6,4},{5,7},{7,5},{8,10},{10,8},{9,1... | collective-permute-start | bytes 245768 | tf_op jit(solution)/shard_map/ppermute | solution.py:300
  30.5 3.0 %collective-permute-done.7 = bf16[320,128]{1,0:T(8,128)(2,1)S(1)} collective-permute-done((bf16[320,128]{1,0:T(8,128)(2,1)S(1)}, bf16[320,128]{1,0:T(8,128)(2,1)S(1)}, u32[]{:S(2)}, u32[]{:S(2)}) %collective-permute-start.7) | collective-permute-done | bytes 81952 | tf_op jit(solution)/shard_map/ppermute | solution.py:300
  33.5 2.4 %collective-permute-start.10 = (bf16[320,128]{1,0:T(8,128)(2,1)S(1)}, bf16[320,128]{1,0:T(8,128)(2,1)S(1)}, u32[]{:S(2)}, u32[]{:S(2)}) collective-permute-start(bf16[320,128]{1,0:T(8,128)(2,1)S(1)} %add_convert_fusion.own_ref), channel_id=1, source_target_pairs={{0,12},{4,8},{8,4},{12,0},{1,13},{5,9},{9,5},{13,1},{2,14},{6,10},... | collective-permute-start | bytes 245768 | tf_op jit(solution)/shard_map/ppermute | solution.py:381
  35.9 0.7 %collective-permute-start.9 = (bf16[320,128]{1,0:T(8,128)(2,1)S(1)}, bf16[320,128]{1,0:T(8,128)(2,1)S(1)}, u32[]{:S(2)}, u32[]{:S(2)}) collective-permute-start(bf16[320,128]{1,0:T(8,128)(2,1)S(1)} %add_convert_fusion.own_ref), channel_id=1, source_target_pairs={{0,8},{4,12},{8,0},{12,4},{1,9},{5,13},{9,1},{13,5},{2,10},{6,14},... | collective-permute-start | bytes 245768 | tf_op jit(solution)/shard_map/ppermute | solution.py:381
  36.6 1.3 %collective-permute-start.8 = (bf16[320,128]{1,0:T(8,128)(2,1)S(1)}, bf16[320,128]{1,0:T(8,128)(2,1)S(1)}, u32[]{:S(2)}, u32[]{:S(2)}) collective-permute-start(bf16[320,128]{1,0:T(8,128)(2,1)S(1)} %add_convert_fusion.own_ref), channel_id=1, source_target_pairs={{0,4},{4,0},{8,12},{12,8},{1,5},{5,1},{9,13},{13,9},{2,6},{6,2},{1... | collective-permute-start | bytes 245768 | tf_op jit(solution)/shard_map/ppermute | solution.py:381
  38.0 2.7 %collective-permute-done.10.refs_2_ = bf16[320,128]{1,0:T(8,128)(2,1)S(1)} collective-permute-done((bf16[320,128]{1,0:T(8,128)(2,1)S(1)}, bf16[320,128]{1,0:T(8,128)(2,1)S(1)}, u32[]{:S(2)}, u32[]{:S(2)}) %collective-permute-start.10) | collective-permute-done | bytes 81952 | tf_op jit(solution)/shard_map/ppermute | solution.py:381
  40.7 2.9 %collective-permute-done.9.refs_1_ = bf16[320,128]{1,0:T(8,128)(2,1)S(1)} collective-permute-done((bf16[320,128]{1,0:T(8,128)(2,1)S(1)}, bf16[320,128]{1,0:T(8,128)(2,1)S(1)}, u32[]{:S(2)}, u32[]{:S(2)}) %collective-permute-start.9) | collective-permute-done | bytes 81952 | tf_op jit(solution)/shard_map/ppermute | solution.py:381
  43.5 0.0 collective-permute-done.8.refs_0_
  43.6 0.1 collective-permute-start.11
  43.7 1.3 %collective-permute-done.11.other_ref = bf16[512,128]{1,0:T(8,128)(2,1)S(1)} collective-permute-done((bf16[512,128]{1,0:T(8,128)(2,1)S(1)}, bf16[512,128]{1,0:T(8,128)(2,1)S(1)}, u32[]{:S(2)}, u32[]{:S(2)}) %collective-permute-start.11) | collective-permute-done | bytes 131104 | tf_op jit(solution)/shard_map/ppermute | solution.py:387
  45.0 0.8 %shard_map.101 = (f32[512,128]{1,0:T(8,128)}, f32[512,128]{1,0:T(8,128)}) custom-call(bf16[512,128]{1,0:T(8,128)(2,1)S(1)} %shard_map.100.mine_ref, bf16[512,128]{1,0:T(8,128)(2,1)S(1)} %collective-permute-done.11.other_ref), custom_call_target="tpu_custom_call" | custom-call | bytes 786432 | tf_op jit(solution)/shard_map/pallas_call | solution.py:260
  (3 shorter events, 0.1 us)
Async XLA Ops:
  0.6 0.7 %copy-start.6 = (s32[256]{0:T(256)S(1)}, s32[256]{0:T(256)}, u32[]{:S(2)}) copy-start(s32[256]{0:T(256)} %param.12) | copy-start | bytes 3076
  0.6 0.7 %copy-start.5 = (s32[256]{0:T(256)S(1)}, s32[256]{0:T(256)}, u32[]{:S(2)}) copy-start(s32[256]{0:T(256)} %param.11) | copy-start | bytes 3076
  1.3 0.9 %copy-start = (bf16[256,512]{1,0:T(8,128)(2,1)S(1)}, bf16[256,512]{1,0:T(8,128)(2,1)}, u32[]{:S(2)}) copy-start(bf16[256,512]{1,0:T(8,128)(2,1)} %item_feats_ref.1) | copy-start | bytes 786436
  2.3 0.9 %copy-start.2 = (bf16[512,128]{1,0:T(8,128)(2,1)S(1)}, bf16[512,128]{1,0:T(8,128)(2,1)}, u32[]{:S(2)}) copy-start(bf16[512,128]{1,0:T(8,128)(2,1)} %proj_hbm.1) | copy-start | bytes 393220
  3.2 6.2 %copy-start.3 = (bf16[512,128]{1,0:T(8,128)(2,1)S(1)}, bf16[512,128]{1,0:T(8,128)(2,1)}, u32[]{:S(2)}) copy-start(bf16[512,128]{1,0:T(8,128)(2,1)} %proj_ref.1) | copy-start | bytes 393220
  3.7 5.7 %copy-start.4 = (s32[512]{0:T(512)S(1)}, s32[512]{0:T(512)}, u32[]{:S(2)}) copy-start(s32[512]{0:T(512)} %param.13) | copy-start | bytes 6148
  3.8 7.7 %collective-permute-start.2 = (bf16[272,128]{1,0:T(8,128)(2,1)S(1)}, bf16[272,128]{1,0:T(8,128)(2,1)S(1)}, u32[]{:S(2)}, u32[]{:S(2)}) collective-permute-start(bf16[272,128]{1,0:T(8,128)(2,1)S(1)} %get-tuple-element.30.message_ref), channel_id=1, source_target_pairs={{0,4},{4,0},{8,12},{12,8},{1,5},{5,1},{9,13},{13,9},{2,6},{6,2},{1... | collective-permute-start | bytes 208904 | tf_op jit(solution)/shard_map/ppermute | solution.py:329
  6.8 7.5 %collective-permute-start.1 = (bf16[272,128]{1,0:T(8,128)(2,1)S(1)}, bf16[272,128]{1,0:T(8,128)(2,1)S(1)}, u32[]{:S(2)}, u32[]{:S(2)}) collective-permute-start(bf16[272,128]{1,0:T(8,128)(2,1)S(1)} %get-tuple-element.30.message_ref), channel_id=1, source_target_pairs={{0,8},{4,12},{8,0},{12,4},{1,9},{5,13},{9,1},{13,5},{2,10},{6,14},... | collective-permute-start | bytes 208904 | tf_op jit(solution)/shard_map/ppermute | solution.py:329
  9.4 6.2 %collective-permute-start = (bf16[272,128]{1,0:T(8,128)(2,1)S(1)}, bf16[272,128]{1,0:T(8,128)(2,1)S(1)}, u32[]{:S(2)}, u32[]{:S(2)}) collective-permute-start(bf16[272,128]{1,0:T(8,128)(2,1)S(1)} %get-tuple-element.30.message_ref), channel_id=1, source_target_pairs={{0,12},{4,8},{8,4},{12,0},{1,13},{5,9},{9,5},{13,1},{2,14},{6,10},... | collective-permute-start | bytes 208904 | tf_op jit(solution)/shard_map/ppermute | solution.py:329
  9.4 1.0 %copy-start.1 = (bf16[512,512]{1,0:T(8,128)(2,1)S(1)}, bf16[512,512]{1,0:T(8,128)(2,1)}, u32[]{:S(2)}) copy-start(bf16[512,512]{1,0:T(8,128)(2,1)} %feats_ref.1) | copy-start | bytes 1572868
  17.2 4.6 %collective-permute-start.3 = (bf16[384,128]{1,0:T(8,128)(2,1)S(1)}, bf16[384,128]{1,0:T(8,128)(2,1)S(1)}, u32[]{:S(2)}, u32[]{:S(2)}) collective-permute-start(bf16[384,128]{1,0:T(8,128)(2,1)S(1)} %get-tuple-element.49), channel_id=1, source_target_pairs={{4,0},{0,4},{12,8},{8,12},{5,1},{1,5},{13,9},{9,13},{6,2},{2,6},{1... | collective-permute-start | bytes 294920 | tf_op jit(solution)/shard_map/ppermute | solution.py:365
  18.0 9.1 %collective-permute-start.4 = (bf16[384,128]{1,0:T(8,128)(2,1)S(1)}, bf16[384,128]{1,0:T(8,128)(2,1)S(1)}, u32[]{:S(2)}, u32[]{:S(2)}) collective-permute-start(bf16[384,128]{1,0:T(8,128)(2,1)S(1)} %get-tuple-element.50), channel_id=1, source_target_pairs={{8,0},{12,4},{0,8},{4,12},{9,1},{13,5},{1,9},{5,13},{10,2},{14,6},... | collective-permute-start | bytes 294920 | tf_op jit(solution)/shard_map/ppermute | solution.py:365
  20.4 6.6 %collective-permute-start.5 = (bf16[384,128]{1,0:T(8,128)(2,1)S(1)}, bf16[384,128]{1,0:T(8,128)(2,1)S(1)}, u32[]{:S(2)}, u32[]{:S(2)}) collective-permute-start(bf16[384,128]{1,0:T(8,128)(2,1)S(1)} %get-tuple-element.51), channel_id=1, source_target_pairs={{12,0},{8,4},{4,8},{0,12},{13,1},{9,5},{5,9},{1,13},{14,2},{10,6},... | collective-permute-start | bytes 294920 | tf_op jit(solution)/shard_map/ppermute | solution.py:365
  27.4 1.5 %collective-permute-start.6 = (f32[320,128]{1,0:T(8,128)S(1)}, f32[320,128]{1,0:T(8,128)S(1)}, u32[]{:S(2)}, u32[]{:S(2)}) collective-permute-start(f32[320,128]{1,0:T(8,128)S(1)} %get-tuple-element.53), channel_id=1, source_target_pairs={{0,1},{1,0},{2,3},{3,2},{4,5},{5,4},{6,7},{7,6},{8,9},{9,8},{10,11... | collective-permute-start | bytes 491528 | tf_op jit(solution)/shard_map/ppermute | solution.py:374
  28.9 4.6 %collective-permute-start.7 = (bf16[320,128]{1,0:T(8,128)(2,1)S(1)}, bf16[320,128]{1,0:T(8,128)(2,1)S(1)}, u32[]{:S(2)}, u32[]{:S(2)}) collective-permute-start(bf16[320,128]{1,0:T(8,128)(2,1)S(1)} %add_convert_fusion.1), channel_id=1, source_target_pairs={{0,2},{2,0},{1,3},{3,1},{4,6},{6,4},{5,7},{7,5},{8,10},{10,8},{9,1... | collective-permute-start | bytes 245768 | tf_op jit(solution)/shard_map/ppermute | solution.py:300
  33.5 7.2 %collective-permute-start.10 = (bf16[320,128]{1,0:T(8,128)(2,1)S(1)}, bf16[320,128]{1,0:T(8,128)(2,1)S(1)}, u32[]{:S(2)}, u32[]{:S(2)}) collective-permute-start(bf16[320,128]{1,0:T(8,128)(2,1)S(1)} %add_convert_fusion.own_ref), channel_id=1, source_target_pairs={{0,12},{4,8},{8,4},{12,0},{1,13},{5,9},{9,5},{13,1},{2,14},{6,10},... | collective-permute-start | bytes 245768 | tf_op jit(solution)/shard_map/ppermute | solution.py:381
  35.9 7.6 %collective-permute-start.9 = (bf16[320,128]{1,0:T(8,128)(2,1)S(1)}, bf16[320,128]{1,0:T(8,128)(2,1)S(1)}, u32[]{:S(2)}, u32[]{:S(2)}) collective-permute-start(bf16[320,128]{1,0:T(8,128)(2,1)S(1)} %add_convert_fusion.own_ref), channel_id=1, source_target_pairs={{0,8},{4,12},{8,0},{12,4},{1,9},{5,13},{9,1},{13,5},{2,10},{6,14},... | collective-permute-start | bytes 245768 | tf_op jit(solution)/shard_map/ppermute | solution.py:381
  36.6 6.9 %collective-permute-start.8 = (bf16[320,128]{1,0:T(8,128)(2,1)S(1)}, bf16[320,128]{1,0:T(8,128)(2,1)S(1)}, u32[]{:S(2)}, u32[]{:S(2)}) collective-permute-start(bf16[320,128]{1,0:T(8,128)(2,1)S(1)} %add_convert_fusion.own_ref), channel_id=1, source_target_pairs={{0,4},{4,0},{8,12},{12,8},{1,5},{5,1},{9,13},{13,9},{2,6},{6,2},{1... | collective-permute-start | bytes 245768 | tf_op jit(solution)/shard_map/ppermute | solution.py:381
  43.6 1.4 %collective-permute-start.11 = (bf16[512,128]{1,0:T(8,128)(2,1)S(1)}, bf16[512,128]{1,0:T(8,128)(2,1)S(1)}, u32[]{:S(2)}, u32[]{:S(2)}) collective-permute-start(bf16[512,128]{1,0:T(8,128)(2,1)S(1)} %shard_map.100.mine_ref), channel_id=1, source_target_pairs={{0,1},{1,0},{2,3},{3,2},{4,5},{5,4},{6,7},{7,6},{8,9},{9,8},{10,11... | collective-permute-start | bytes 393224 | tf_op jit(solution)/shard_map/ppermute | solution.py:387

commit v3 on v2

--- a/solution.py
+++ b/solution.py
@@ -30,14 +30,19 @@
     return terms
 
 
-def item_tower(feats_hbm, proj_hbm, ids_hbm, counts_hbm, message_ref, z_ref, feats_ref, proj_ref, ids_ref, counts_ref, sems):
-    pairs = ((ids_hbm, ids_ref), (counts_hbm, counts_ref), (proj_hbm, proj_ref), (feats_hbm, feats_ref))
-    copies = [pltpu.make_async_copy(source, target, sems.at[k]) for k, (source, target) in enumerate(pairs)]
-    for copy in copies:
-        copy.start()
+def item_tower(*refs):
+    hbm, rest = refs[:7], refs[7:]
+    message_ref, z_ref = rest[:2]
+    targets = rest[2:5] + rest[6:8] + rest[5:6] + rest[8:9]
+    sems = rest[9]
+    copies = [pltpu.make_async_copy(source, target, sems.at[k]) for k, (source, target) in enumerate(zip(hbm, targets))]
+    order = (5, 6, 3, 4, 0, 1, 2)
+    for k in order:
+        copies[k].start()
+    feats_ref, proj_ref, ids_ref, counts_ref = targets[5], targets[6], targets[3], targets[4]
     rows = feats_ref.shape[0]
-    copies[0].wait()
-    copies[1].wait()
+    copies[3].wait()
+    copies[4].wait()
     ids = ids_ref[...]
     digits = [ids >> 16, (ids >> 8) & 255, ids & 255]
     log_counts = jnp.log(counts_ref[...].astype(f32)) * log2e
@@ -45,12 +50,14 @@
     halves = ids.shape[0]
     lines.append(jnp.zeros((tail_rows - 6 * halves, ids.shape[1]), f32))
     message_ref[rows : rows + tail_rows, :] = jnp.concatenate(lines, axis=0).astype(bf16)
-    copies[2].wait()
-    copies[3].wait()
+    copies[6].wait()
+    copies[5].wait()
     z = jnp.dot(feats_ref[...], proj_ref[...], preferred_element_type=f32)
     z_ref[...] = z
     inverse = 1.0 / jnp.sqrt(jnp.sum(z * z, axis=1, keepdims=True) + epsilon)
     message_ref[0:rows, :] = (z * inverse).astype(bf16)
+    for k in (0, 1, 2):
+        copies[k].wait()
 
 
 def item_columns(message_ref, half, halves):
@@ -164,7 +171,7 @@
     sums_ref[...] = jnp.broadcast_to(totals, sums_ref.shape)
 
 
-def last_block(scale, others, ring, *refs):
+def last_block(scale, others, ring, chain, *refs):
     (
         message_ref,
         query_ref,
@@ -186,7 +193,8 @@
     losses_ref[...] = jnp.log(totals) - lines_ref[1:2, :]
     share = 1.0 / totals
     queries = plain_ref[...]
-    for piece_ref, weights_ref in zip(piece_refs, list(weights_refs) + [last_ref]):
+    for step, weights_ref in zip(chain, list(weights_refs) + [last_ref]):
+        piece_ref = piece_refs[step - 1]
         grads = (weights_ref[...] * share).astype(bf16)
         piece_ref[0:rows, :] = jnp.dot(grads, queries, preferred_element_type=f32).astype(bf16)
     own = lax.broadcasted_iota(jnp.int32, (rows, count), 0) == positives_ref[...]
@@ -227,11 +235,13 @@
         send_ref[start : start + half, :] = jnp.where(first, whole[half:], whole[:half])
 
 
-def add_pieces(others, item_rows, own_ref, *refs):
-    out_ref = refs[others]
-    values = [ref[...].astype(f32) for ref in (own_ref,) + refs[:others]]
+def add_pieces(turns, item_rows, own_ref, *refs):
+    out_ref = refs[-1]
+    values = [own_ref[...].astype(f32)]
+    for step in range(1, len(turns) + 1):
+        values.append(refs[turns.index(step)][...].astype(f32))
     total = values[0] + values[1]
-    if others == 3:
+    if len(values) == 4:
         total = total + (values[2] + values[3])
     query_rows = own_ref.shape[0] - item_rows
     out_ref[0:item_rows, :] = total[:item_rows].astype(bf16)
@@ -254,7 +264,7 @@
             query_ref[pl.ds(start, part), :] = values[half + step * part : half + (step + 1) * part]
 
 
-def call(kernel, outs, args, scratch=(), flops=0, fetch=False):
+def call(kernel, outs, args, scratch=(), flops=0, fetch=False, room=32):
     vmem = pl.BlockSpec(memory_space=pltpu.VMEM)
     moved = sum(math.prod(s.shape) * s.dtype.itemsize for s in list(outs) + list(args))
     return pl.pallas_call(
@@ -263,9 +273,13 @@
         in_specs=[pl.BlockSpec(memory_space=pltpu.HBM) if fetch else vmem] * len(args),
         out_specs=tuple([vmem] * len(outs)),
         scratch_shapes=list(scratch),
-        compiler_params=pltpu.CompilerParams(vmem_limit_bytes=32 * 1024 * 1024),
+        compiler_params=pltpu.CompilerParams(vmem_limit_bytes=room * 1024 * 1024),
         cost_estimate=pl.CostEstimate(flops=flops, bytes_accessed=moved, transcendentals=0),
     )(*args)
+
+
+def pin(values):
+    return pltpu.with_memory_space_constraint(values, pltpu.HBM)
 
 
 def out(shape, dtype=f32):
@@ -284,6 +298,10 @@
 
 def partners(count):
     return [[(j, int(partner_of(j, step, count))) for j in range(count)] for step in range(1, count)]
+
+
+def ordered(others, order):
+    return list(order) if len(order) == others else list(range(1, others + 1))
 
 
 def sent_back(pairs):
@@ -312,22 +330,36 @@
     exchange = partners(ring)
     others = len(exchange)
     part = hidden // ring
-    message, item_z = call(
+    message, item_z, query_feats, query_proj, spots, item_feats = call(
         item_tower,
-        [out((rows + tail_rows, width), bf16), out((rows, width))],
-        [item_feats, item_proj, item_ids.reshape(halves, 128), item_counts.reshape(halves, 128)],
+        [
+            out((rows + tail_rows, width), bf16),
+            out((rows, width)),
+            out((count, hidden), bf16),
+            out((hidden, width), bf16),
+            out((1, count), jnp.int32),
+            out((rows, hidden), bf16),
+        ],
+        [
+            pin(query_feats),
+            pin(query_proj),
+            pin(positives.reshape(1, count)),
+            pin(item_ids.reshape(halves, 128)),
+            pin(item_counts.reshape(halves, 128)),
+            pin(item_feats),
+            pin(item_proj),
+        ],
         scratch=[
-            pltpu.VMEM((rows, hidden), bf16),
-            pltpu.VMEM((hidden, width), bf16),
             pltpu.VMEM((halves, 128), jnp.int32),
             pltpu.VMEM((halves, 128), jnp.int32),
-            pltpu.SemaphoreType.DMA((4,)),
+            pltpu.VMEM((hidden, width), bf16),
+            pltpu.SemaphoreType.DMA((7,)),
         ],
         flops=2 * rows * hidden * width,
         fetch=True,
+        room=32,
     )
     received = [lax.ppermute(message, "neg", pairs) for pairs in exchange]
-    spots = positives.reshape(1, count)
     query_z, queries, plain, own_weights, weighted, pos_items, lines, turned, item_turned = call(
         query_tower,
         [
@@ -346,7 +378,9 @@
     )
     totals = lines
     weights = []
-    for block in received[:-1]:
+    chain = ordered(others, (1, 2, 3))
+    for step in chain[:-1]:
+        block = received[step - 1]
         block_weights, weighted, totals = call(
             middle_block,
             [out((rows, count)), out((width, count)), out((8, count))],
@@ -355,9 +389,9 @@
         )
         weights.append(block_weights)
     results = call(
-        functools.partial(last_block, scale, others, ring),
+        functools.partial(last_block, scale, others, ring, chain),
         [out((rows + part, width), bf16)] * others + [out((rows, width)), out((part, width)), out((1, count))],
-        [received[-1], queries, plain, lines, weighted, totals, spots, own_weights, pos_items, query_z, turned] + weights,
+        [received[chain[-1] - 1], queries, plain, lines, weighted, totals, spots, own_weights, pos_items, query_z, turned] + weights,
         scratch=[pltpu.VMEM((rows, count), f32), pltpu.VMEM((hidden, width), f32)],
         flops=6 * count * width * rows * (others + 1),
     )
@@ -367,7 +401,7 @@
     keep, send = call(
         functools.partial(item_gradient, scale, others),
         [out((kept, width)), out((kept, width))],
-        [own_piece, own_grad, item_z, item_turned] + back,
+        [own_piece, own_grad, item_z, item_turned] + [back[step - 1] for step in ordered(others, (3, 2, 1))],
         flops=2 * rows * width * hidden,
     )
     swap = [(0, 1), (1, 0)]
@@ -375,10 +409,12 @@
     direct = ring in (2, 4)
     if direct:
         half = half.astype(bf16)
+        got = [lax.ppermute(half, "neg", pairs) for pairs in exchange]
+        turns = ordered(others, (1, 3, 2))
         mine = call(
-            functools.partial(add_pieces, others, hidden // 2),
+            functools.partial(add_pieces, turns, hidden // 2),
             [out((hidden, width), bf16)],
-            [half] + [lax.ppermute(half, "neg", pairs) for pairs in exchange],
+            [half] + [got[step - 1] for step in turns],
         )[0]
     else:
         item_half = lax.psum(half[: hidden // 2], "neg").astype(bf16)

time: 46.1 us -> 42.8 us (0.928)
  local copies, waits for them, and re-layouts: 3.58 us -> 0 us
  starting transfers between devices: 16.2 us -> 15.3 us
  Pallas kernels: 5.69 us -> 6.51 us
  waiting for transfers between devices: 19.5 us -> 20.1 us
    unnamed x14 -> x0, local copies, waits for them, and re-layouts: 3.58 us -> none
    ppermute x3, waiting for transfers between devices: 2.79 us -> 3.84 us  [on_device(): received = [lax.ppermute(message, 'neg', pairs) for pairs in exchange]]
    ppermute x3, starting transfers between devices: 4.45 us -> 3.55 us  [on_device(): got = [lax.ppermute(half, 'neg', pairs) for pairs in exchange]]
    pallas_call x8, Pallas kernels: 5.69 us -> 6.51 us  [call(): pl.pallas_call(kernel, out_shape=tuple((jax.ShapeDtypeStruct(s.shape, s.d...]
    ppermute x3, waiting for transfers between devices: 5.59 us -> 5.12 us  [on_device(): got = [lax.ppermute(half, 'neg', pairs) for pairs in exchange]]
where the time goes in v3:
time: 42.8 us; the launch traced here: 42.7 us
  waiting for transfers between devices  20.1 us (47%)
  starting transfers between devices  15.3 us (36%)
  Pallas kernels  6.51 us (15%)
  between operations  0.71 us (2%)
    pallas_call x8, Pallas kernels, call(): pl.pallas_call(kernel, out_shape=tuple((jax.ShapeDtypeStruct(s.shape, s.d...  6.51 us
    ppermute x3, starting transfers between devices, on_device(): received = [lax.ppermute(message, 'neg', pairs) for pairs in exchange]  5.67 us
    ppermute x3, waiting for transfers between devices, on_device(): lax.ppermute(piece, 'neg', sent_back(pairs))  5.4 us
    ppermute x3, waiting for transfers between devices, on_device(): got = [lax.ppermute(half, 'neg', pairs) for pairs in exchange]  5.12 us
    ppermute x3, starting transfers between devices, on_device(): lax.ppermute(piece, 'neg', sent_back(pairs))  4.39 us
    ppermute x3, waiting for transfers between devices, on_device(): received = [lax.ppermute(message, 'neg', pairs) for pairs in exchange]  3.84 us
    ppermute x3, starting transfers between devices, on_device(): got = [lax.ppermute(half, 'neg', pairs) for pairs in exchange]  3.55 us
    ppermute x1, waiting for transfers between devices, sum_over(): lax.ppermute(values, axis, pairs).astype(f32)  3 us
  transfers between devices with their start and end apart: 12, of which 9 were waited for; matrix products, arithmetic and copies ran while one was open for 0% of the time, Pallas kernels for 5%

profile of v3, /device:TPU:0, one launch (start us, length us, event | category | flops | bytes accessed | tf_op | source)
XLA Modules:
  0.0 42.7 jit_solution(9303155584350500087)
XLA Ops:
  0.6 1.4 %shard_map.94 = (bf16[272,128]{1,0:T(8,128)(2,1)S(1)}, f32[256,128]{1,0:T(8,128)S(1)}, bf16[512,512]{1,0:T(8,128)(2,1)S(1)}, bf16[512,128]{1,0:T(8,128)(2,1)S(1)...) custom-call(bf16[512,512]{1,0:T(8,128)(2,1)} %refs_0_.1, bf16[512,128]{1,0:T(8,128)(2,1)} %refs_1_.1, ...), custom_call_target="tpu_custom_call" | custom-call | flops 33554432 | bytes 2172928 | tf_op jit(solution)/shard_map/pallas_call | solution.py:270
  2.0 3.1 %collective-permute-start.2 = (bf16[272,128]{1,0:T(8,128)(2,1)S(1)}, bf16[272,128]{1,0:T(8,128)(2,1)S(1)}, u32[]{:S(2)}, u32[]{:S(2)}) collective-permute-start(bf16[272,128]{1,0:T(8,128)(2,1)S(1)} %get-tuple-element.34.message_ref), channel_id=1, source_target_pairs={{0,4},{4,0},{8,12},{12,8},{1,5},{5,1},{9,13},{13,9},{2,6},{6,2},{1... | collective-permute-start | bytes 208904 | tf_op jit(solution)/shard_map/ppermute | solution.py:362
  5.1 2.6 %collective-permute-start.1 = (bf16[272,128]{1,0:T(8,128)(2,1)S(1)}, bf16[272,128]{1,0:T(8,128)(2,1)S(1)}, u32[]{:S(2)}, u32[]{:S(2)}) collective-permute-start(bf16[272,128]{1,0:T(8,128)(2,1)S(1)} %get-tuple-element.34.message_ref), channel_id=1, source_target_pairs={{0,8},{4,12},{8,0},{12,4},{1,9},{5,13},{9,1},{13,5},{2,10},{6,14},... | collective-permute-start | bytes 208904 | tf_op jit(solution)/shard_map/ppermute | solution.py:362
  7.7 0.0 collective-permute-start
  7.7 1.0 %shard_map.95 = (f32[128,512]{1,0:T(8,128)S(1)}, bf16[128,512]{1,0:T(8,128)(2,1)S(1)}, bf16[512,128]{1,0:T(8,128)(2,1)S(1)}, f32[256,512]{1,0:T(8,128)S(1)}, f32...) custom-call(bf16[512,512]{1,0:T(8,128)(2,1)S(1)} %get-tuple-element., ...), custom_call_target="tpu_custom_call" | custom-call | flops 167772160 | bytes 3364864 | tf_op jit(solution)/shard_map/pallas_call | solution.py:270
  8.6 0.0 collective-permute-done.2.message_ref
  8.7 0.7 %shard_map.96 = (f32[256,512]{1,0:T(8,128)S(1)}, f32[128,512]{1,0:T(8,128)S(1)}, f32[8,512]{1,0:T(8,128)S(1)}) custom-call(bf16[272,128]{1,0:T(8,128)(2,1)S(1)} %collective-permute-done.2.message_ref, bf16[128,512]{1,0:T(8,128)(2,1)S(1)} %get-tuple-element.39.query_ref.refs_1_, f32[8,512]{1,0:T(8,128)S(1)} %get-tuple-element.41.lines_ref.totals_ref.refs_3_, ...), custom_call_target="tpu_custom_call" | custom-call | flops 67108864 | bytes 1298432 | tf_op jit(solution)/shard_map/pallas_call | solution.py:270
  9.3 3.3 %collective-permute-done.1.message_ref = bf16[272,128]{1,0:T(8,128)(2,1)S(1)} collective-permute-done((bf16[272,128]{1,0:T(8,128)(2,1)S(1)}, bf16[272,128]{1,0:T(8,128)(2,1)S(1)}, u32[]{:S(2)}, u32[]{:S(2)}) %collective-permute-start.1) | collective-permute-done | bytes 69664 | tf_op jit(solution)/shard_map/ppermute | solution.py:362
  12.6 0.7 %shard_map.97 = (f32[256,512]{1,0:T(8,128)S(1)}, f32[128,512]{1,0:T(8,128)S(1)}, f32[8,512]{1,0:T(8,128)S(1)}) custom-call(bf16[272,128]{1,0:T(8,128)(2,1)S(1)} %collective-permute-done.1.message_ref, bf16[128,512]{1,0:T(8,128)(2,1)S(1)} %get-tuple-element.39.query_ref.refs_1_, f32[8,512]{1,0:T(8,128)S(1)} %get-tuple-element.41.lines_ref.totals_ref.refs_3_, ...), custom_call_target="tpu_custom_call" | custom-call | flops 67108864 | bytes 1298432 | tf_op jit(solution)/shard_map/pallas_call | solution.py:270
  13.3 0.6 %collective-permute-done.refs_0_ = bf16[272,128]{1,0:T(8,128)(2,1)S(1)} collective-permute-done((bf16[272,128]{1,0:T(8,128)(2,1)S(1)}, bf16[272,128]{1,0:T(8,128)(2,1)S(1)}, u32[]{:S(2)}, u32[]{:S(2)}) %collective-permute-start) | collective-permute-done | bytes 69664 | tf_op jit(solution)/shard_map/ppermute | solution.py:362
  13.9 1.6 %shard_map.98 = (bf16[384,128]{1,0:T(8,128)(2,1)S(1)}, bf16[384,128]{1,0:T(8,128)(2,1)S(1)}, bf16[384,128]{1,0:T(8,128)(2,1)S(1)}, f32[256,128]{1,0:T(8,128)S(1)...) custom-call(bf16[272,128]{1,0:T(8,128)(2,1)S(1)} %collective-permute-done.refs_0_, ...), custom_call_target="tpu_custom_call" | custom-call | flops 402653184 | bytes 3743744 | tf_op jit(solution)/shard_map/pallas_call | solution.py:270
  15.5 2.7 %collective-permute-start.3 = (bf16[384,128]{1,0:T(8,128)(2,1)S(1)}, bf16[384,128]{1,0:T(8,128)(2,1)S(1)}, u32[]{:S(2)}, u32[]{:S(2)}) collective-permute-start(bf16[384,128]{1,0:T(8,128)(2,1)S(1)} %get-tuple-element.57), channel_id=1, source_target_pairs={{12,0},{8,4},{4,8},{0,12},{13,1},{9,5},{5,9},{1,13},{14,2},{10,6},... | collective-permute-start | bytes 294920 | tf_op jit(solution)/shard_map/ppermute | solution.py:399
  18.1 0.0 collective-permute-start.4
  18.1 1.7 %collective-permute-start.5 = (bf16[384,128]{1,0:T(8,128)(2,1)S(1)}, bf16[384,128]{1,0:T(8,128)(2,1)S(1)}, u32[]{:S(2)}, u32[]{:S(2)}) collective-permute-start(bf16[384,128]{1,0:T(8,128)(2,1)S(1)} %get-tuple-element.59), channel_id=1, source_target_pairs={{4,0},{0,4},{12,8},{8,12},{5,1},{1,5},{13,9},{9,13},{6,2},{2,6},{1... | collective-permute-start | bytes 294920 | tf_op jit(solution)/shard_map/ppermute | solution.py:399
  19.9 2.6 %collective-permute-done.3.refs_0_ = bf16[384,128]{1,0:T(8,128)(2,1)S(1)} collective-permute-done((bf16[384,128]{1,0:T(8,128)(2,1)S(1)}, bf16[384,128]{1,0:T(8,128)(2,1)S(1)}, u32[]{:S(2)}, u32[]{:S(2)}) %collective-permute-start.3) | collective-permute-done | bytes 98336 | tf_op jit(solution)/shard_map/ppermute | solution.py:399
  22.5 2.8 %collective-permute-done.4.refs_1_ = bf16[384,128]{1,0:T(8,128)(2,1)S(1)} collective-permute-done((bf16[384,128]{1,0:T(8,128)(2,1)S(1)}, bf16[384,128]{1,0:T(8,128)(2,1)S(1)}, u32[]{:S(2)}, u32[]{:S(2)}) %collective-permute-start.4) | collective-permute-done | bytes 98336 | tf_op jit(solution)/shard_map/ppermute | solution.py:399
  25.3 0.0 collective-permute-done.5.refs_2_
  25.3 0.3 shard_map.99
  25.6 0.1 collective-permute-start.6
  25.7 1.4 %collective-permute-done.6 = f32[320,128]{1,0:T(8,128)S(1)} collective-permute-done((f32[320,128]{1,0:T(8,128)S(1)}, f32[320,128]{1,0:T(8,128)S(1)}, u32[]{:S(2)}, u32[]{:S(2)}) %collective-permute-start.6) | collective-permute-done | bytes 163872 | tf_op jit(solution)/shard_map/ppermute | solution.py:408
  27.1 1.6 %collective-permute-start.7 = (bf16[320,128]{1,0:T(8,128)(2,1)S(1)}, bf16[320,128]{1,0:T(8,128)(2,1)S(1)}, u32[]{:S(2)}, u32[]{:S(2)}) collective-permute-start(bf16[320,128]{1,0:T(8,128)(2,1)S(1)} %add_convert_fusion.1), channel_id=1, source_target_pairs={{0,2},{2,0},{1,3},{3,1},{4,6},{6,4},{5,7},{7,5},{8,10},{10,8},{9,1... | collective-permute-start | bytes 245768 | tf_op jit(solution)/shard_map/ppermute | solution.py:318
  28.7 3.0 %collective-permute-done.7 = bf16[320,128]{1,0:T(8,128)(2,1)S(1)} collective-permute-done((bf16[320,128]{1,0:T(8,128)(2,1)S(1)}, bf16[320,128]{1,0:T(8,128)(2,1)S(1)}, u32[]{:S(2)}, u32[]{:S(2)}) %collective-permute-start.7) | collective-permute-done | bytes 81952 | tf_op jit(solution)/shard_map/ppermute | solution.py:318
  31.7 0.5 %collective-permute-start.10 = (bf16[320,128]{1,0:T(8,128)(2,1)S(1)}, bf16[320,128]{1,0:T(8,128)(2,1)S(1)}, u32[]{:S(2)}, u32[]{:S(2)}) collective-permute-start(bf16[320,128]{1,0:T(8,128)(2,1)S(1)} %add_convert_fusion.own_ref), channel_id=1, source_target_pairs={{0,8},{4,12},{8,0},{12,4},{1,9},{5,13},{9,1},{13,5},{2,10},{6,14},... | collective-permute-start | bytes 245768 | tf_op jit(solution)/shard_map/ppermute | solution.py:412
  32.2 1.9 %collective-permute-start.9 = (bf16[320,128]{1,0:T(8,128)(2,1)S(1)}, bf16[320,128]{1,0:T(8,128)(2,1)S(1)}, u32[]{:S(2)}, u32[]{:S(2)}) collective-permute-start(bf16[320,128]{1,0:T(8,128)(2,1)S(1)} %add_convert_fusion.own_ref), channel_id=1, source_target_pairs={{0,12},{4,8},{8,4},{12,0},{1,13},{5,9},{9,5},{13,1},{2,14},{6,10},... | collective-permute-start | bytes 245768 | tf_op jit(solution)/shard_map/ppermute | solution.py:412
  34.1 1.2 %collective-permute-start.8 = (bf16[320,128]{1,0:T(8,128)(2,1)S(1)}, bf16[320,128]{1,0:T(8,128)(2,1)S(1)}, u32[]{:S(2)}, u32[]{:S(2)}) collective-permute-start(bf16[320,128]{1,0:T(8,128)(2,1)S(1)} %add_convert_fusion.own_ref), channel_id=1, source_target_pairs={{0,4},{4,0},{8,12},{12,8},{1,5},{5,1},{9,13},{13,9},{2,6},{6,2},{1... | collective-permute-start | bytes 245768 | tf_op jit(solution)/shard_map/ppermute | solution.py:412
  35.3 4.9 %collective-permute-done.10.refs_2_ = bf16[320,128]{1,0:T(8,128)(2,1)S(1)} collective-permute-done((bf16[320,128]{1,0:T(8,128)(2,1)S(1)}, bf16[320,128]{1,0:T(8,128)(2,1)S(1)}, u32[]{:S(2)}, u32[]{:S(2)}) %collective-permute-start.10) | collective-permute-done | bytes 81952 | tf_op jit(solution)/shard_map/ppermute | solution.py:412
  40.1 0.0 collective-permute-done.9.refs_1_
  40.1 0.3 collective-permute-done.8.refs_0_
  40.4 0.1 collective-permute-start.11
  40.5 1.3 %collective-permute-done.11.other_ref = bf16[512,128]{1,0:T(8,128)(2,1)S(1)} collective-permute-done((bf16[512,128]{1,0:T(8,128)(2,1)S(1)}, bf16[512,128]{1,0:T(8,128)(2,1)S(1)}, u32[]{:S(2)}, u32[]{:S(2)}) %collective-permute-start.11) | collective-permute-done | bytes 131104 | tf_op jit(solution)/shard_map/ppermute | solution.py:423
  41.8 0.8 %shard_map.101 = (f32[512,128]{1,0:T(8,128)}, f32[512,128]{1,0:T(8,128)}) custom-call(bf16[512,128]{1,0:T(8,128)(2,1)S(1)} %shard_map.100.mine_ref, bf16[512,128]{1,0:T(8,128)(2,1)S(1)} %collective-permute-done.11.other_ref), custom_call_target="tpu_custom_call" | custom-call | bytes 786432 | tf_op jit(solution)/shard_map/pallas_call | solution.py:270
  (3 shorter events, 0.1 us)
Async XLA Ops:
  2.0 6.6 %collective-permute-start.2 = (bf16[272,128]{1,0:T(8,128)(2,1)S(1)}, bf16[272,128]{1,0:T(8,128)(2,1)S(1)}, u32[]{:S(2)}, u32[]{:S(2)}) collective-permute-start(bf16[272,128]{1,0:T(8,128)(2,1)S(1)} %get-tuple-element.34.message_ref), channel_id=1, source_target_pairs={{0,4},{4,0},{8,12},{12,8},{1,5},{5,1},{9,13},{13,9},{2,6},{6,2},{1... | collective-permute-start | bytes 208904 | tf_op jit(solution)/shard_map/ppermute | solution.py:362
  5.1 7.5 %collective-permute-start.1 = (bf16[272,128]{1,0:T(8,128)(2,1)S(1)}, bf16[272,128]{1,0:T(8,128)(2,1)S(1)}, u32[]{:S(2)}, u32[]{:S(2)}) collective-permute-start(bf16[272,128]{1,0:T(8,128)(2,1)S(1)} %get-tuple-element.34.message_ref), channel_id=1, source_target_pairs={{0,8},{4,12},{8,0},{12,4},{1,9},{5,13},{9,1},{13,5},{2,10},{6,14},... | collective-permute-start | bytes 208904 | tf_op jit(solution)/shard_map/ppermute | solution.py:362
  7.7 6.2 %collective-permute-start = (bf16[272,128]{1,0:T(8,128)(2,1)S(1)}, bf16[272,128]{1,0:T(8,128)(2,1)S(1)}, u32[]{:S(2)}, u32[]{:S(2)}) collective-permute-start(bf16[272,128]{1,0:T(8,128)(2,1)S(1)} %get-tuple-element.34.message_ref), channel_id=1, source_target_pairs={{0,12},{4,8},{8,4},{12,0},{1,13},{5,9},{9,5},{13,1},{2,14},{6,10},... | collective-permute-start | bytes 208904 | tf_op jit(solution)/shard_map/ppermute | solution.py:362
  15.5 7.0 %collective-permute-start.3 = (bf16[384,128]{1,0:T(8,128)(2,1)S(1)}, bf16[384,128]{1,0:T(8,128)(2,1)S(1)}, u32[]{:S(2)}, u32[]{:S(2)}) collective-permute-start(bf16[384,128]{1,0:T(8,128)(2,1)S(1)} %get-tuple-element.57), channel_id=1, source_target_pairs={{12,0},{8,4},{4,8},{0,12},{13,1},{9,5},{5,9},{1,13},{14,2},{10,6},... | collective-permute-start | bytes 294920 | tf_op jit(solution)/shard_map/ppermute | solution.py:399
  18.1 7.1 %collective-permute-start.4 = (bf16[384,128]{1,0:T(8,128)(2,1)S(1)}, bf16[384,128]{1,0:T(8,128)(2,1)S(1)}, u32[]{:S(2)}, u32[]{:S(2)}) collective-permute-start(bf16[384,128]{1,0:T(8,128)(2,1)S(1)} %get-tuple-element.58), channel_id=1, source_target_pairs={{8,0},{12,4},{0,8},{4,12},{9,1},{13,5},{1,9},{5,13},{10,2},{14,6},... | collective-permute-start | bytes 294920 | tf_op jit(solution)/shard_map/ppermute | solution.py:399
  18.1 7.1 %collective-permute-start.5 = (bf16[384,128]{1,0:T(8,128)(2,1)S(1)}, bf16[384,128]{1,0:T(8,128)(2,1)S(1)}, u32[]{:S(2)}, u32[]{:S(2)}) collective-permute-start(bf16[384,128]{1,0:T(8,128)(2,1)S(1)} %get-tuple-element.59), channel_id=1, source_target_pairs={{4,0},{0,4},{12,8},{8,12},{5,1},{1,5},{13,9},{9,13},{6,2},{2,6},{1... | collective-permute-start | bytes 294920 | tf_op jit(solution)/shard_map/ppermute | solution.py:399
  25.6 1.5 %collective-permute-start.6 = (f32[320,128]{1,0:T(8,128)S(1)}, f32[320,128]{1,0:T(8,128)S(1)}, u32[]{:S(2)}, u32[]{:S(2)}) collective-permute-start(f32[320,128]{1,0:T(8,128)S(1)} %get-tuple-element.61), channel_id=1, source_target_pairs={{0,1},{1,0},{2,3},{3,2},{4,5},{5,4},{6,7},{7,6},{8,9},{9,8},{10,11... | collective-permute-start | bytes 491528 | tf_op jit(solution)/shard_map/ppermute | solution.py:408
  27.1 4.6 %collective-permute-start.7 = (bf16[320,128]{1,0:T(8,128)(2,1)S(1)}, bf16[320,128]{1,0:T(8,128)(2,1)S(1)}, u32[]{:S(2)}, u32[]{:S(2)}) collective-permute-start(bf16[320,128]{1,0:T(8,128)(2,1)S(1)} %add_convert_fusion.1), channel_id=1, source_target_pairs={{0,2},{2,0},{1,3},{3,1},{4,6},{6,4},{5,7},{7,5},{8,10},{10,8},{9,1... | collective-permute-start | bytes 245768 | tf_op jit(solution)/shard_map/ppermute | solution.py:318
  31.7 8.4 %collective-permute-start.10 = (bf16[320,128]{1,0:T(8,128)(2,1)S(1)}, bf16[320,128]{1,0:T(8,128)(2,1)S(1)}, u32[]{:S(2)}, u32[]{:S(2)}) collective-permute-start(bf16[320,128]{1,0:T(8,128)(2,1)S(1)} %add_convert_fusion.own_ref), channel_id=1, source_target_pairs={{0,8},{4,12},{8,0},{12,4},{1,9},{5,13},{9,1},{13,5},{2,10},{6,14},... | collective-permute-start | bytes 245768 | tf_op jit(solution)/shard_map/ppermute | solution.py:412
  32.2 7.9 %collective-permute-start.9 = (bf16[320,128]{1,0:T(8,128)(2,1)S(1)}, bf16[320,128]{1,0:T(8,128)(2,1)S(1)}, u32[]{:S(2)}, u32[]{:S(2)}) collective-permute-start(bf16[320,128]{1,0:T(8,128)(2,1)S(1)} %add_convert_fusion.own_ref), channel_id=1, source_target_pairs={{0,12},{4,8},{8,4},{12,0},{1,13},{5,9},{9,5},{13,1},{2,14},{6,10},... | collective-permute-start | bytes 245768 | tf_op jit(solution)/shard_map/ppermute | solution.py:412
  34.1 6.3 %collective-permute-start.8 = (bf16[320,128]{1,0:T(8,128)(2,1)S(1)}, bf16[320,128]{1,0:T(8,128)(2,1)S(1)}, u32[]{:S(2)}, u32[]{:S(2)}) collective-permute-start(bf16[320,128]{1,0:T(8,128)(2,1)S(1)} %add_convert_fusion.own_ref), channel_id=1, source_target_pairs={{0,4},{4,0},{8,12},{12,8},{1,5},{5,1},{9,13},{13,9},{2,6},{6,2},{1... | collective-permute-start | bytes 245768 | tf_op jit(solution)/shard_map/ppermute | solution.py:412
  40.4 1.4 %collective-permute-start.11 = (bf16[512,128]{1,0:T(8,128)(2,1)S(1)}, bf16[512,128]{1,0:T(8,128)(2,1)S(1)}, u32[]{:S(2)}, u32[]{:S(2)}) collective-permute-start(bf16[512,128]{1,0:T(8,128)(2,1)S(1)} %shard_map.100.mine_ref), channel_id=1, source_target_pairs={{0,1},{1,0},{2,3},{3,2},{4,5},{5,4},{6,7},{7,6},{8,9},{9,8},{10,11... | collective-permute-start | bytes 393224 | tf_op jit(solution)/shard_map/ppermute | solution.py:423

commit v4 on v3

v4 whole, which is shorter than its diff:
```python
import functools
import math

import jax
import jax.numpy as jnp
from jax import lax
from jax.experimental import pallas as pl
from jax.experimental.pallas import tpu as pltpu
from jax.sharding import PartitionSpec as P

inverse_softness = 20.0
epsilon = 1e-06
log2e = math.log2(math.e)
ln2 = math.log(2.0)
tail_rows = 16
f32 = jnp.float32
bf16 = jnp.bfloat16


def contract(lhs, rhs, over):
    return lax.dot_general(lhs, rhs, (((over[0],), (over[1],)), ((), ())), preferred_element_type=f32)


def split_terms(values):
    terms = []
    for _ in range(3):
        term = values.astype(bf16).astype(f32)
        terms.append(term)
        values = values - term
    return terms


def item_tower(*refs):
    hbm, rest = refs[:7], refs[7:]
    message_ref, unit_ref, inverse_ref = rest[:3]
    targets = rest[3:6] + rest[7:9] + rest[6:7] + rest[9:10]
    sems = rest[10]
    copies = [pltpu.make_async_copy(source, target, sems.at[k]) for k, (source, target) in enumerate(zip(hbm, targets))]
    order = (5, 6, 3, 4, 0, 1, 2)
    for k in order:
        copies[k].start()
    feats_ref, proj_ref, ids_ref, counts_ref = targets[5], targets[6], targets[3], targets[4]
    rows = feats_ref.shape[0]
    copies[3].wait()
    copies[4].wait()
    ids = ids_ref[...]
    digits = [ids >> 16, (ids >> 8) & 255, ids & 255]
    log_counts = jnp.log(counts_ref[...].astype(f32)) * log2e
    lines = [digit.astype(f32) for digit in digits] + split_terms(log_counts)
    halves = ids.shape[0]
    lines.append(jnp.zeros((tail_rows - 6 * halves, ids.shape[1]), f32))
    message_ref[rows : rows + tail_rows, :] = jnp.concatenate(lines, axis=0).astype(bf16)
    copies[6].wait()
    copies[5].wait()
    z = jnp.dot(feats_ref[...], proj_ref[...], preferred_element_type=f32)
    inverse = 1.0 / jnp.sqrt(jnp.sum(z * z, axis=1, keepdims=True) + epsilon)
    unit = z * inverse
    message_ref[0:rows, :] = unit.astype(bf16)
    unit_ref[...] = unit
    inverse_ref[...] = jnp.broadcast_to(inverse, inverse_ref.shape)
    for k in (0, 1, 2):
        copies[k].wait()


def column_table(halves):
    line = lax.broadcasted_iota(jnp.int32, (tail_rows, 128), 0)
    parts = []
    for first, scales in ((0, (65536.0, 256.0, 1.0)), (3, (1.0, 1.0, 1.0))):
        for half in range(halves):
            part = jnp.zeros((tail_rows, 128), f32)
            for step, scale in enumerate(scales):
                part = jnp.where(line == (first + step) * halves + half, scale, part)
            parts.append(part)
    return jnp.concatenate(parts, axis=1).astype(bf16)


def item_columns(message_ref, table):
    rows = message_ref.shape[0] - tail_rows
    halves = rows // 128
    columns = contract(message_ref[rows : rows + tail_rows, :], table, (0, 0))
    ids = [columns[:, half * 128 : half * 128 + 128] for half in range(halves)]
    logs = [columns[:, (halves + half) * 128 : (halves + half) * 128 + 128] for half in range(halves)]
    return jnp.concatenate(ids, axis=0), jnp.concatenate(logs, axis=0)


def wide(column, width):
    return jnp.concatenate([column] * (width // column.shape[1]), axis=1)


def query_tower(
    feats_ref,
    proj_ref,
    message_ref,
    positives_ref,
    item_feats_ref,
    unit_ref,
    query_ref,
    plain_ref,
    weights_ref,
    weighted_ref,
    pos_ref,
    lines_ref,
    turned_ref,
    item_turned_ref,
    table_ref,
):
    rows = message_ref.shape[0] - tail_rows
    halves = rows // 128
    z = contract(proj_ref[...], feats_ref[...], (0, 1))
    inverse = 1.0 / jnp.sqrt(jnp.sum(z * z, axis=0, keepdims=True) + epsilon)
    scaled = z * inverse
    unit_ref[...] = scaled
    queries = scaled.astype(bf16)
    query_ref[...] = queries
    plain_ref[...] = queries.T
    count = queries.shape[1]
    positives = positives_ref[...]
    tail = message_ref[rows : rows + tail_rows, :]
    own = []
    pos_id = jnp.zeros((1, count), f32)
    for half in range(halves):
        spot = lax.broadcasted_iota(jnp.int32, (128, count), 0) + half * 128
        own.append(spot == positives)
        found = jnp.dot(tail, own[half].astype(f32).astype(bf16), preferred_element_type=f32)
        for step, scale in enumerate((65536.0, 256.0, 1.0)):
            line = step * halves + half
            pos_id = pos_id + scale * found[line : line + 1, :]
    table = column_table(halves)
    table_ref[...] = table
    own = jnp.concatenate(own, axis=0)
    items = message_ref[0:rows, :]
    ids, logs = item_columns(message_ref, table)
    scores = jnp.dot(items, queries, preferred_element_type=f32)
    scores = scores * (inverse_softness * log2e) - wide(logs, count)
    collide = (wide(ids, count) == pos_id) & jnp.logical_not(own)
    weights = jnp.where(collide, 0.0, jnp.exp2(scores))
    weights_ref[...] = weights
    totals = jnp.sum(weights, axis=0, keepdims=True)
    target = jnp.sum(jnp.where(own, scores, 0.0), axis=0, keepdims=True)
    weighted = contract(items, weights.astype(bf16), (0, 0))
    pos_items = contract(items, own.astype(f32).astype(bf16), (0, 0))
    weighted_ref[...] = weighted
    pos_ref[...] = pos_items
    lines_ref[...] = jnp.concatenate([totals, target * ln2, pos_id, inverse, jnp.zeros((4, count), f32)], axis=0)
    turned_ref[...] = feats_ref[...].T
    item_turned_ref[...] = item_feats_ref[...].T


def add_block(message_ref, query_ref, lines_ref, table_ref, before_ref, totals, weights_ref, chunk=32):
    rows, count = weights_ref.shape
    pos_id = lines_ref[2:3, :]
    partial = jnp.zeros((8, count), f32)
    items = message_ref[0:rows, :]
    ids, logs = item_columns(message_ref, table_ref[...])
    scores = jnp.dot(items, query_ref[...], preferred_element_type=f32)
    rounded = []
    for first in range(0, rows, chunk):
        part = slice(first, first + chunk)
        exponent = scores[part] * (inverse_softness * log2e) - wide(logs[part], count)
        weights = jnp.where(wide(ids[part], count) == pos_id, 0.0, jnp.exp2(exponent))
        for line in range(0, chunk, 8):
            partial = partial + weights[line : line + 8]
        rounded.append(weights.astype(bf16))
    rounded = jnp.concatenate(rounded, axis=0)
    weights_ref[...] = rounded
    weighted = before_ref[...] + contract(items, rounded, (0, 0))
    return totals + jnp.sum(partial, axis=0, keepdims=True), weighted


def middle_block(message_ref, query_ref, lines_ref, table_ref, before_ref, totals_ref, weights_ref, after_ref, sums_ref):
    totals, weighted = add_block(message_ref, query_ref, lines_ref, table_ref, before_ref, totals_ref[0:1, :], weights_ref)
    after_ref[...] = weighted
    sums_ref[...] = jnp.broadcast_to(totals, sums_ref.shape)


def last_block(scale, others, ring, chain, *refs):
    (
        message_ref,
        query_ref,
        plain_ref,
        lines_ref,
        table_ref,
        before_ref,
        totals_ref,
        positives_ref,
        own_weights_ref,
        pos_ref,
        unit_ref,
        turned_ref,
    ) = refs[:12]
    weights_refs = refs[12 : 11 + others]
    piece_refs = refs[11 + others : 11 + 2 * others]
    own_ref, own_grad_ref, losses_ref, last_ref, grad_ref = refs[11 + 2 * others :]
    rows, count = own_weights_ref.shape
    totals, weighted = add_block(message_ref, query_ref, lines_ref, table_ref, before_ref, totals_ref[0:1, :], last_ref)
    losses_ref[...] = jnp.log(totals) - lines_ref[1:2, :]
    share = 1.0 / totals
    cot = weighted * share - pos_ref[...]
    unit = unit_ref[...]
    along = jnp.sum(unit * cot, axis=0, keepdims=True)
    dz = ((cot - unit * along) * (lines_ref[3:4, :] * scale)).astype(bf16)
    shared = (query_ref[...].astype(f32) * share).astype(bf16)
    for step, weights_ref in zip(chain, list(weights_refs) + [last_ref]):
        piece_refs[step - 1][0:rows, :] = contract(weights_ref[...], shared, (1, 1)).astype(bf16)
    own = lax.broadcasted_iota(jnp.int32, (rows, count), 0) == positives_ref[...]
    grads = (own_weights_ref[...] * share - own.astype(f32)).astype(bf16)
    own_ref[...] = jnp.dot(grads, plain_ref[...], preferred_element_type=f32)
    grad_ref[...] = contract(turned_ref[...], dz, (1, 1))
    me = lax.axis_index("neg")
    part = grad_ref.shape[0] // ring
    own_grad_ref[...] = grad_ref[pl.ds(pl.multiple_of(me * part, part), part), :]
    for step, piece_ref in enumerate(piece_refs):
        target = source_of(me, step + 1, ring)
        piece_ref[rows : rows + part, :] = grad_ref[pl.ds(pl.multiple_of(target * part, part), part), :].astype(bf16)


def item_gradient(scale, others, own_ref, own_grad_ref, unit_ref, inverse_ref, turned_ref, *refs):
    keep_ref, send_ref = refs[others:]
    rows = own_ref.shape[0]
    cot = own_ref[...]
    query_grad = own_grad_ref[...]
    for ref in refs[:others]:
        cot = cot + ref[0:rows, :].astype(f32)
        query_grad = query_grad + ref[rows:, :].astype(f32)
    unit = unit_ref[...]
    along = jnp.sum(unit * cot, axis=1, keepdims=True)
    dz = ((cot - unit * along) * (inverse_ref[...] * scale)).astype(bf16)
    grad = jnp.dot(turned_ref[...], dz, preferred_element_type=f32)
    first = lax.axis_index("sub") == 0
    for start, whole in ((0, grad), (grad.shape[0] // 2, query_grad)):
        half = whole.shape[0] // 2
        keep_ref[start : start + half, :] = jnp.where(first, whole[:half], whole[half:])
        send_ref[start : start + half, :] = jnp.where(first, whole[half:], whole[:half])


def add_pieces(turns, item_rows, own_ref, *refs):
    out_ref = refs[-1]
    values = [own_ref[...].astype(f32)]
    for step in range(1, len(turns) + 1):
        values.append(refs[turns.index(step)][...].astype(f32))
    total = values[0] + values[1]
    if len(values) == 4:
        total = total + (values[2] + values[3])
    query_rows = own_ref.shape[0] - item_rows
    out_ref[0:item_rows, :] = total[:item_rows].astype(bf16)
    for step, value in enumerate(values):
        start = item_rows + step * query_rows
        out_ref[start : start + query_rows, :] = value[item_rows:].astype(bf16)


def place_kernel(ring, direct, other, *refs):
    values_ref = refs[0]
    query_hbm, item_hbm, wide_ref, sems = refs[-4:]
    sub = lax.axis_index("sub")
    side = 1 - sub if other else sub
    base = lax.axis_index("neg") if direct else 0
    half = item_hbm.shape[0] // 2
    part = half // ring
    wide_ref[...] = values_ref[...].astype(f32)
    copies = [
        pltpu.make_async_copy(
            wide_ref.at[pl.ds(0, half)], item_hbm.at[pl.ds(pl.multiple_of(side * half, half), half)], sems.at[ring]
        )
    ]
    for step in range(ring):
        start = pl.multiple_of(partner_of(base, step, ring) * (2 * part) + side * part, part)
        copies.append(
            pltpu.make_async_copy(
                wide_ref.at[pl.ds(half + step * part, part)], query_hbm.at[pl.ds(start, part)], sems.at[step]
            )
        )
    for copy in copies:
        copy.start()
    for copy in copies:
        copy.wait()


def place(ring, direct, other, values, outs):
    hbm = pl.BlockSpec(memory_space=pltpu.HBM)
    shape = jax.ShapeDtypeStruct(values.shape, f32)
    return pl.pallas_call(
        functools.partial(place_kernel, ring, direct, other),
        out_shape=(shape, shape),
        in_specs=[pl.BlockSpec(memory_space=pltpu.VMEM)] + [hbm] * len(outs),
        out_specs=(hbm, hbm),
        input_output_aliases={1: 0, 2: 1} if outs else {},
        scratch_shapes=[pltpu.VMEM(values.shape, f32), pltpu.SemaphoreType.DMA((ring + 1,))],
        compiler_params=pltpu.CompilerParams(vmem_limit_bytes=32 * 1024 * 1024),
        cost_estimate=pl.CostEstimate(flops=0, bytes_accessed=6 * values.size, transcendentals=0),
    )(values, *outs)


def call(kernel, outs, args, scratch=(), flops=0, fetch=False, room=32):
    vmem = pl.BlockSpec(memory_space=pltpu.VMEM)
    moved = sum(math.prod(s.shape) * s.dtype.itemsize for s in list(outs) + list(args))
    return pl.pallas_call(
        kernel,
        out_shape=tuple(jax.ShapeDtypeStruct(s.shape, s.dtype) for s in outs),
        in_specs=[pl.BlockSpec(memory_space=pltpu.HBM) if fetch else vmem] * len(args),
        out_specs=tuple([vmem] * len(outs)),
        scratch_shapes=list(scratch),
        compiler_params=pltpu.CompilerParams(vmem_limit_bytes=room * 1024 * 1024),
        cost_estimate=pl.CostEstimate(flops=flops, bytes_accessed=moved, transcendentals=0),
    )(*args)


def pin(values):
    return pltpu.with_memory_space_constraint(values, pltpu.HBM)


def out(shape, dtype=f32):
    return jax.ShapeDtypeStruct(shape, dtype)


def partner_of(me, step, count):
    if count & (count - 1) == 0:
        return me ^ step
    return lax.rem(me + step, count)


def source_of(me, step, count):
    return partner_of(me, step if count & (count - 1) == 0 else count - step, count)


def partners(count):
    return [[(j, int(partner_of(j, step, count))) for j in range(count)] for step in range(1, count)]


def ordered(others, order):
    return list(order) if len(order) == others else list(range(1, others + 1))


def sent_back(pairs):
    return [(target, source) for source, target in pairs]


def sum_over(values, axis):
    size = lax.axis_size(axis)
    if size == 1:
        return values
    if size not in (2, 4):
        return lax.psum(values, axis)
    values = values.astype(bf16)
    got = [lax.ppermute(values, axis, pairs).astype(f32) for pairs in partners(size)]
    total = values.astype(f32) + got[0]
    return total + (got[1] + got[2]) if size == 4 else total


def on_device(query_feats, item_feats, query_proj, item_proj, item_ids, item_counts, positives):
    count, hidden = query_feats.shape
    rows = item_feats.shape[0]
    width = query_proj.shape[1]
    scale = inverse_softness / count
    halves = rows // 128
    ring = lax.axis_size("neg")
    exchange = partners(ring)
    others = len(exchange)
    part = hidden // ring
    message, item_unit, item_inverse, query_feats, query_proj, spots, item_feats = call(
        item_tower,
        [
            out((rows + tail_rows, width), bf16),
            out((rows, width)),
            out((rows, width)),
            out((count, hidden), bf16),
            out((hidden, width), bf16),
            out((1, count), jnp.int32),
            out((rows, hidden), bf16),
        ],
        [
            pin(query_feats),
            pin(query_proj),
            pin(positives.reshape(1, count)),
            pin(item_ids.reshape(halves, 128)),
            pin(item_counts.reshape(halves, 128)),
            pin(item_feats),
            pin(item_proj),
        ],
        scratch=[
            pltpu.VMEM((halves, 128), jnp.int32),
            pltpu.VMEM((halves, 128), jnp.int32),
            pltpu.VMEM((hidden, width), bf16),
            pltpu.SemaphoreType.DMA((7,)),
        ],
        flops=2 * rows * hidden * width,
        fetch=True,
        room=32,
    )
    received = [lax.ppermute(message, "neg", pairs) for pairs in exchange]
    query_unit, queries, plain, own_weights, weighted, pos_items, lines, turned, item_turned, table = call(
        query_tower,
        [
            out((width, count)),
            out((width, count), bf16),
            out((count, width), bf16),
            out((rows, count)),
            out((width, count)),
            out((width, count)),
            out((8, count)),
            out((hidden, count), bf16),
            out((hidden, rows), bf16),
            out((tail_rows, 2 * rows), bf16),
        ],
        [query_feats, query_proj, message, spots, item_feats],
        flops=2 * count * width * (hidden + 3 * rows),
    )
    totals = lines
    weights = []
    chain = ordered(others, (1, 2, 3))
    for step in chain[:-1]:
        block = received[step - 1]
        block_weights, weighted, totals = call(
            middle_block,
            [out((rows, count), bf16), out((width, count)), out((8, count))],
            [block, queries, lines, table, weighted, totals],
            flops=4 * count * width * rows,
        )
        weights.append(block_weights)
    results = call(
        functools.partial(last_block, scale, others, ring, chain),
        [out((rows + part, width), bf16)] * others + [out((rows, width)), out((part, width)), out((1, count))],
        [received[chain[-1] - 1], queries, plain, lines, table, weighted, totals, spots, own_weights, pos_items, query_unit, turned] + weights,
        scratch=[pltpu.VMEM((rows, count), bf16), pltpu.VMEM((hidden, width), f32)],
        flops=6 * count * width * rows * (others + 1),
    )
    own_piece, own_grad, losses = results[others:]
    back = [lax.ppermute(piece, "neg", sent_back(pairs)) for piece, pairs in zip(results, exchange)]
    kept = (hidden + part) // 2
    keep, send = call(
        functools.partial(item_gradient, scale, others),
        [out((kept, width)), out((kept, width))],
        [own_piece, own_grad, item_unit, item_inverse, item_turned] + [back[step - 1] for step in ordered(others, (3, 2, 1))],
        flops=2 * rows * width * hidden,
    )
    swap = [(0, 1), (1, 0)]
    half = sum_over(keep + lax.ppermute(send, "sub", swap), "rep")
    direct = ring in (2, 4)
    if direct:
        half = half.astype(bf16)
        got = [lax.ppermute(half, "neg", pairs) for pairs in exchange]
        turns = ordered(others, (3, 1, 2))
        mine = call(
            functools.partial(add_pieces, turns, hidden // 2),
            [out((hidden, width), bf16)],
            [half] + [got[step - 1] for step in turns],
        )[0]
    else:
        item_half = lax.psum(half[: hidden // 2], "neg").astype(bf16)
        query_half = lax.all_gather(half[hidden // 2 :].astype(bf16), "neg", axis=0, tiled=True)
        mine = jnp.concatenate([item_half, query_half], axis=0)
    other = lax.ppermute(mine, "sub", swap)
    outs = place(ring, direct, False, mine, ())
    grad_query, grad_item = place(ring, direct, True, other, outs)
    return (grad_query, grad_item, losses.reshape(count))


def solution(mesh):
    split = ("groups", "neg", "rep", "sub")
    return jax.shard_map(
        on_device,
        mesh=mesh,
        in_specs=(P(split, None), P(split, None), P(), P(), P(split), P(split), P(split)),
        out_specs=(P("groups", None), P("groups", None), P(split)),
        check_vma=False,
    )
```

time: 42.8 us -> 42.3 us (0.988)
    pallas_call x8 -> x7, Pallas kernels: 6.51 us -> 4.84 us  [call(): pl.pallas_call(kernel, out_shape=tuple((jax.ShapeDtypeStruct(s.shape, s.d...]
    pallas_call x0 -> x2, Pallas kernels: none -> 1.5 us  [place(): pl.pallas_call(functools.partial(place_kernel, ring, direct, other), out_...]
    ppermute x1, waiting for transfers between devices: 1.33 us -> 0.57 us  [on_device(): other = lax.ppermute(mine, 'sub', swap)]
  transfers between devices with their start and end apart: 12 -> 12, of which waited for: 9 -> 9; matrix products, arithmetic and copies ran while one was open for 0% -> 0% of each run, Pallas kernels for 5% -> 7%
where the time goes in v4:
time: 42.3 us; the launch traced here: 42.1 us
  waiting for transfers between devices  19.7 us (47%)
  starting transfers between devices  15.4 us (36%)
  Pallas kernels  6.34 us (15%)
  between operations  0.72 us (2%)
    ppermute x3, starting transfers between devices, on_device(): received = [lax.ppermute(message, 'neg', pairs) for pairs in exchange]  5.67 us
    ppermute x3, waiting for transfers between devices, on_device(): lax.ppermute(piece, 'neg', sent_back(pairs))  5.42 us
    ppermute x3, waiting for transfers between devices, on_device(): got = [lax.ppermute(half, 'neg', pairs) for pairs in exchange]  5.09 us
    pallas_call x7, Pallas kernels, call(): pl.pallas_call(kernel, out_shape=tuple((jax.ShapeDtypeStruct(s.shape, s.d...  4.84 us
    ppermute x3, starting transfers between devices, on_device(): lax.ppermute(piece, 'neg', sent_back(pairs))  4.44 us
    ppermute x3, waiting for transfers between devices, on_device(): received = [lax.ppermute(message, 'neg', pairs) for pairs in exchange]  4.18 us
    ppermute x3, starting transfers between devices, on_device(): got = [lax.ppermute(half, 'neg', pairs) for pairs in exchange]  3.55 us
    ppermute x1, waiting for transfers between devices, sum_over(): lax.ppermute(values, axis, pairs).astype(f32)  3 us
  transfers between devices with their start and end apart: 12, of which 9 were waited for; matrix products, arithmetic and copies ran while one was open for 0% of the time, Pallas kernels for 7%

profile of v4, /device:TPU:0, one launch (start us, length us, event | category | flops | bytes accessed | tf_op | source)
XLA Modules:
  0.0 42.1 jit_solution(4078838744956480837)
XLA Ops:
  0.6 1.4 %shard_map.94 = (bf16[272,128]{1,0:T(8,128)(2,1)S(1)}, f32[256,128]{1,0:T(8,128)S(1)}, f32[256,128]{1,0:T(8,128)S(1)}, bf16[512,512]{1,0:T(8,128)(2,1)S(1)}, bf1...) custom-call(bf16[512,512]{1,0:T(8,128)(2,1)} %refs_0_.1, bf16[512,128]{1,0:T(8,128)(2,1)} %refs_1_.1, ...), custom_call_target="tpu_custom_call" | custom-call | flops 33554432 | bytes 2304000 | tf_op jit(solution)/shard_map/pallas_call | solution.py:296
  2.0 3.1 %collective-permute-start.2 = (bf16[272,128]{1,0:T(8,128)(2,1)S(1)}, bf16[272,128]{1,0:T(8,128)(2,1)S(1)}, u32[]{:S(2)}, u32[]{:S(2)}) collective-permute-start(bf16[272,128]{1,0:T(8,128)(2,1)S(1)} %get-tuple-element.38.message_ref), channel_id=1, source_target_pairs={{0,4},{4,0},{8,12},{12,8},{1,5},{5,1},{9,13},{13,9},{2,6},{6,2},{1... | collective-permute-start | bytes 208904 | tf_op jit(solution)/shard_map/ppermute | solution.py:389
  5.1 2.6 %collective-permute-start.1 = (bf16[272,128]{1,0:T(8,128)(2,1)S(1)}, bf16[272,128]{1,0:T(8,128)(2,1)S(1)}, u32[]{:S(2)}, u32[]{:S(2)}) collective-permute-start(bf16[272,128]{1,0:T(8,128)(2,1)S(1)} %get-tuple-element.38.message_ref), channel_id=1, source_target_pairs={{0,8},{4,12},{8,0},{12,4},{1,9},{5,13},{9,1},{13,5},{2,10},{6,14},... | collective-permute-start | bytes 208904 | tf_op jit(solution)/shard_map/ppermute | solution.py:389
  7.7 0.0 collective-permute-start
  7.7 0.9 %shard_map.95 = (f32[128,512]{1,0:T(8,128)S(1)}, bf16[128,512]{1,0:T(8,128)(2,1)S(1)}, bf16[512,128]{1,0:T(8,128)(2,1)S(1)}, f32[256,512]{1,0:T(8,128)S(1)}, f32...) custom-call(bf16[512,512]{1,0:T(8,128)(2,1)S(1)} %get-tuple-element., ...), custom_call_target="tpu_custom_call" | custom-call | flops 167772160 | bytes 3381248 | tf_op jit(solution)/shard_map/pallas_call | solution.py:296
  8.6 0.0 collective-permute-done.2.message_ref
  8.6 0.5 %shard_map.96 = (bf16[256,512]{1,0:T(8,128)(2,1)S(1)}, f32[128,512]{1,0:T(8,128)S(1)}, f32[8,512]{1,0:T(8,128)S(1)}) custom-call(bf16[272,128]{1,0:T(8,128)(2,1)S(1)} %collective-permute-done.2.message_ref, bf16[128,512]{1,0:T(8,128)(2,1)S(1)} %get-tuple-element.43.query_ref.refs_1_, f32[8,512]{1,0:T(8,128)S(1)} %get-tuple-element.45.lines_ref.totals_ref.refs_3_, ...), custom_call_target="tpu_custom_call" | custom-call | flops 67108864 | bytes 1052672 | tf_op jit(solution)/shard_map/pallas_call | solution.py:296
  9.2 3.4 %collective-permute-done.1.message_ref = bf16[272,128]{1,0:T(8,128)(2,1)S(1)} collective-permute-done((bf16[272,128]{1,0:T(8,128)(2,1)S(1)}, bf16[272,128]{1,0:T(8,128)(2,1)S(1)}, u32[]{:S(2)}, u32[]{:S(2)}) %collective-permute-start.1) | collective-permute-done | bytes 69664 | tf_op jit(solution)/shard_map/ppermute | solution.py:389
  12.6 0.5 %shard_map.97 = (bf16[256,512]{1,0:T(8,128)(2,1)S(1)}, f32[128,512]{1,0:T(8,128)S(1)}, f32[8,512]{1,0:T(8,128)S(1)}) custom-call(bf16[272,128]{1,0:T(8,128)(2,1)S(1)} %collective-permute-done.1.message_ref, bf16[128,512]{1,0:T(8,128)(2,1)S(1)} %get-tuple-element.43.query_ref.refs_1_, f32[8,512]{1,0:T(8,128)S(1)} %get-tuple-element.45.lines_ref.totals_ref.refs_3_, ...), custom_call_target="tpu_custom_call" | custom-call | flops 67108864 | bytes 1052672 | tf_op jit(solution)/shard_map/pallas_call | solution.py:296
  13.2 0.7 %collective-permute-done.refs_0_ = bf16[272,128]{1,0:T(8,128)(2,1)S(1)} collective-permute-done((bf16[272,128]{1,0:T(8,128)(2,1)S(1)}, bf16[272,128]{1,0:T(8,128)(2,1)S(1)}, u32[]{:S(2)}, u32[]{:S(2)}) %collective-permute-start) | collective-permute-done | bytes 69664 | tf_op jit(solution)/shard_map/ppermute | solution.py:389
  13.9 1.1 %shard_map.98 = (bf16[384,128]{1,0:T(8,128)(2,1)S(1)}, bf16[384,128]{1,0:T(8,128)(2,1)S(1)}, bf16[384,128]{1,0:T(8,128)(2,1)S(1)}, f32[256,128]{1,0:T(8,128)S(1)...) custom-call(bf16[272,128]{1,0:T(8,128)(2,1)S(1)} %collective-permute-done.refs_0_, ...), custom_call_target="tpu_custom_call" | custom-call | flops 402653184 | bytes 3235840 | tf_op jit(solution)/shard_map/pallas_call | solution.py:296
  15.0 2.6 %collective-permute-start.3 = (bf16[384,128]{1,0:T(8,128)(2,1)S(1)}, bf16[384,128]{1,0:T(8,128)(2,1)S(1)}, u32[]{:S(2)}, u32[]{:S(2)}) collective-permute-start(bf16[384,128]{1,0:T(8,128)(2,1)S(1)} %get-tuple-element.63), channel_id=1, source_target_pairs={{12,0},{8,4},{4,8},{0,12},{13,1},{9,5},{5,9},{1,13},{14,2},{10,6},... | collective-permute-start | bytes 294920 | tf_op jit(solution)/shard_map/ppermute | solution.py:427
  17.6 0.0 collective-permute-start.4
  17.6 1.8 %collective-permute-start.5 = (bf16[384,128]{1,0:T(8,128)(2,1)S(1)}, bf16[384,128]{1,0:T(8,128)(2,1)S(1)}, u32[]{:S(2)}, u32[]{:S(2)}) collective-permute-start(bf16[384,128]{1,0:T(8,128)(2,1)S(1)} %get-tuple-element.65), channel_id=1, source_target_pairs={{4,0},{0,4},{12,8},{8,12},{5,1},{1,5},{13,9},{9,13},{6,2},{2,6},{1... | collective-permute-start | bytes 294920 | tf_op jit(solution)/shard_map/ppermute | solution.py:427
  19.4 2.6 %collective-permute-done.3.refs_0_ = bf16[384,128]{1,0:T(8,128)(2,1)S(1)} collective-permute-done((bf16[384,128]{1,0:T(8,128)(2,1)S(1)}, bf16[384,128]{1,0:T(8,128)(2,1)S(1)}, u32[]{:S(2)}, u32[]{:S(2)}) %collective-permute-start.3) | collective-permute-done | bytes 98336 | tf_op jit(solution)/shard_map/ppermute | solution.py:427
  22.0 2.8 %collective-permute-done.4.refs_1_ = bf16[384,128]{1,0:T(8,128)(2,1)S(1)} collective-permute-done((bf16[384,128]{1,0:T(8,128)(2,1)S(1)}, bf16[384,128]{1,0:T(8,128)(2,1)S(1)}, u32[]{:S(2)}, u32[]{:S(2)}) %collective-permute-start.4) | collective-permute-done | bytes 98336 | tf_op jit(solution)/shard_map/ppermute | solution.py:427
  24.9 0.0 collective-permute-done.5.refs_2_
  24.9 0.3 shard_map.99
  25.2 0.1 collective-permute-start.6
  25.3 1.4 %collective-permute-done.6 = f32[320,128]{1,0:T(8,128)S(1)} collective-permute-done((f32[320,128]{1,0:T(8,128)S(1)}, f32[320,128]{1,0:T(8,128)S(1)}, u32[]{:S(2)}, u32[]{:S(2)}) %collective-permute-start.6) | collective-permute-done | bytes 163872 | tf_op jit(solution)/shard_map/ppermute | solution.py:436
  26.7 1.6 %collective-permute-start.7 = (bf16[320,128]{1,0:T(8,128)(2,1)S(1)}, bf16[320,128]{1,0:T(8,128)(2,1)S(1)}, u32[]{:S(2)}, u32[]{:S(2)}) collective-permute-start(bf16[320,128]{1,0:T(8,128)(2,1)S(1)} %add_convert_fusion.1), channel_id=1, source_target_pairs={{0,2},{2,0},{1,3},{3,1},{4,6},{6,4},{5,7},{7,5},{8,10},{10,8},{9,1... | collective-permute-start | bytes 245768 | tf_op jit(solution)/shard_map/ppermute | solution.py:344
  28.2 3.0 %collective-permute-done.7 = bf16[320,128]{1,0:T(8,128)(2,1)S(1)} collective-permute-done((bf16[320,128]{1,0:T(8,128)(2,1)S(1)}, bf16[320,128]{1,0:T(8,128)(2,1)S(1)}, u32[]{:S(2)}, u32[]{:S(2)}) %collective-permute-start.7) | collective-permute-done | bytes 81952 | tf_op jit(solution)/shard_map/ppermute | solution.py:344
  31.3 0.3 collective-permute-start.10
  31.6 2.1 %collective-permute-start.8 = (bf16[320,128]{1,0:T(8,128)(2,1)S(1)}, bf16[320,128]{1,0:T(8,128)(2,1)S(1)}, u32[]{:S(2)}, u32[]{:S(2)}) collective-permute-start(bf16[320,128]{1,0:T(8,128)(2,1)S(1)} %add_convert_fusion.own_ref), channel_id=1, source_target_pairs={{0,12},{4,8},{8,4},{12,0},{1,13},{5,9},{9,5},{13,1},{2,14},{6,10},... | collective-permute-start | bytes 245768 | tf_op jit(solution)/shard_map/ppermute | solution.py:440
  33.7 1.2 %collective-permute-start.9 = (bf16[320,128]{1,0:T(8,128)(2,1)S(1)}, bf16[320,128]{1,0:T(8,128)(2,1)S(1)}, u32[]{:S(2)}, u32[]{:S(2)}) collective-permute-start(bf16[320,128]{1,0:T(8,128)(2,1)S(1)} %add_convert_fusion.own_ref), channel_id=1, source_target_pairs={{0,4},{4,0},{8,12},{12,8},{1,5},{5,1},{9,13},{13,9},{2,6},{6,2},{1... | collective-permute-start | bytes 245768 | tf_op jit(solution)/shard_map/ppermute | solution.py:440
  34.8 4.8 %collective-permute-done.10.refs_2_ = bf16[320,128]{1,0:T(8,128)(2,1)S(1)} collective-permute-done((bf16[320,128]{1,0:T(8,128)(2,1)S(1)}, bf16[320,128]{1,0:T(8,128)(2,1)S(1)}, u32[]{:S(2)}, u32[]{:S(2)}) %collective-permute-start.10) | collective-permute-done | bytes 81952 | tf_op jit(solution)/shard_map/ppermute | solution.py:440
  39.7 0.0 collective-permute-done.8.refs_0_
  39.7 0.2 collective-permute-done.9.refs_1_
  40.0 0.1 collective-permute-start.11
  40.0 0.8 %shard_map.101 = (f32[512,128]{1,0:T(8,128)}, f32[512,128]{1,0:T(8,128)}) custom-call(bf16[512,128]{1,0:T(8,128)(2,1)S(1)} %shard_map.100.refs_0_), custom_call_target="tpu_custom_call" | custom-call | bytes 393216 | tf_op jit(solution)/shard_map/pallas_call | solution.py:281
  40.8 0.6 %collective-permute-done.11.refs_0_ = bf16[512,128]{1,0:T(8,128)(2,1)S(1)} collective-permute-done((bf16[512,128]{1,0:T(8,128)(2,1)S(1)}, bf16[512,128]{1,0:T(8,128)(2,1)S(1)}, u32[]{:S(2)}, u32[]{:S(2)}) %collective-permute-start.11) | collective-permute-done | bytes 131104 | tf_op jit(solution)/shard_map/ppermute | solution.py:451
  41.4 0.8 %shard_map.102 = (f32[512,128]{1,0:T(8,128)}, f32[512,128]{1,0:T(8,128)}) custom-call(bf16[512,128]{1,0:T(8,128)(2,1)S(1)} %collective-permute-done.11.refs_0_, f32[512,128]{1,0:T(8,128)} %get-tuple-element.68.refs_1_, f32[512,128]{1,0:T(8,128)} %get-tuple-element.69.refs_2_), custom_call_target="tpu_custom_call", output_to_operand_aliasing={{0}: (1, {}), {1}: (2, {})} | custom-call | bytes 393216 | tf_op jit(solution)/shard_map/pallas_call | solution.py:281
  (3 shorter events, 0.1 us)
Async XLA Ops:
  2.0 6.6 %collective-permute-start.2 = (bf16[272,128]{1,0:T(8,128)(2,1)S(1)}, bf16[272,128]{1,0:T(8,128)(2,1)S(1)}, u32[]{:S(2)}, u32[]{:S(2)}) collective-permute-start(bf16[272,128]{1,0:T(8,128)(2,1)S(1)} %get-tuple-element.38.message_ref), channel_id=1, source_target_pairs={{0,4},{4,0},{8,12},{12,8},{1,5},{5,1},{9,13},{13,9},{2,6},{6,2},{1... | collective-permute-start | bytes 208904 | tf_op jit(solution)/shard_map/ppermute | solution.py:389
  5.1 7.5 %collective-permute-start.1 = (bf16[272,128]{1,0:T(8,128)(2,1)S(1)}, bf16[272,128]{1,0:T(8,128)(2,1)S(1)}, u32[]{:S(2)}, u32[]{:S(2)}) collective-permute-start(bf16[272,128]{1,0:T(8,128)(2,1)S(1)} %get-tuple-element.38.message_ref), channel_id=1, source_target_pairs={{0,8},{4,12},{8,0},{12,4},{1,9},{5,13},{9,1},{13,5},{2,10},{6,14},... | collective-permute-start | bytes 208904 | tf_op jit(solution)/shard_map/ppermute | solution.py:389
  7.7 6.2 %collective-permute-start = (bf16[272,128]{1,0:T(8,128)(2,1)S(1)}, bf16[272,128]{1,0:T(8,128)(2,1)S(1)}, u32[]{:S(2)}, u32[]{:S(2)}) collective-permute-start(bf16[272,128]{1,0:T(8,128)(2,1)S(1)} %get-tuple-element.38.message_ref), channel_id=1, source_target_pairs={{0,12},{4,8},{8,4},{12,0},{1,13},{5,9},{9,5},{13,1},{2,14},{6,10},... | collective-permute-start | bytes 208904 | tf_op jit(solution)/shard_map/ppermute | solution.py:389
  15.0 7.0 %collective-permute-start.3 = (bf16[384,128]{1,0:T(8,128)(2,1)S(1)}, bf16[384,128]{1,0:T(8,128)(2,1)S(1)}, u32[]{:S(2)}, u32[]{:S(2)}) collective-permute-start(bf16[384,128]{1,0:T(8,128)(2,1)S(1)} %get-tuple-element.63), channel_id=1, source_target_pairs={{12,0},{8,4},{4,8},{0,12},{13,1},{9,5},{5,9},{1,13},{14,2},{10,6},... | collective-permute-start | bytes 294920 | tf_op jit(solution)/shard_map/ppermute | solution.py:427
  17.6 7.3 %collective-permute-start.4 = (bf16[384,128]{1,0:T(8,128)(2,1)S(1)}, bf16[384,128]{1,0:T(8,128)(2,1)S(1)}, u32[]{:S(2)}, u32[]{:S(2)}) collective-permute-start(bf16[384,128]{1,0:T(8,128)(2,1)S(1)} %get-tuple-element.64), channel_id=1, source_target_pairs={{8,0},{12,4},{0,8},{4,12},{9,1},{13,5},{1,9},{5,13},{10,2},{14,6},... | collective-permute-start | bytes 294920 | tf_op jit(solution)/shard_map/ppermute | solution.py:427
  17.6 7.3 %collective-permute-start.5 = (bf16[384,128]{1,0:T(8,128)(2,1)S(1)}, bf16[384,128]{1,0:T(8,128)(2,1)S(1)}, u32[]{:S(2)}, u32[]{:S(2)}) collective-permute-start(bf16[384,128]{1,0:T(8,128)(2,1)S(1)} %get-tuple-element.65), channel_id=1, source_target_pairs={{4,0},{0,4},{12,8},{8,12},{5,1},{1,5},{13,9},{9,13},{6,2},{2,6},{1... | collective-permute-start | bytes 294920 | tf_op jit(solution)/shard_map/ppermute | solution.py:427
  25.2 1.5 %collective-permute-start.6 = (f32[320,128]{1,0:T(8,128)S(1)}, f32[320,128]{1,0:T(8,128)S(1)}, u32[]{:S(2)}, u32[]{:S(2)}) collective-permute-start(f32[320,128]{1,0:T(8,128)S(1)} %get-tuple-element.67), channel_id=1, source_target_pairs={{0,1},{1,0},{2,3},{3,2},{4,5},{5,4},{6,7},{7,6},{8,9},{9,8},{10,11... | collective-permute-start | bytes 491528 | tf_op jit(solution)/shard_map/ppermute | solution.py:436
  26.7 4.6 %collective-permute-start.7 = (bf16[320,128]{1,0:T(8,128)(2,1)S(1)}, bf16[320,128]{1,0:T(8,128)(2,1)S(1)}, u32[]{:S(2)}, u32[]{:S(2)}) collective-permute-start(bf16[320,128]{1,0:T(8,128)(2,1)S(1)} %add_convert_fusion.1), channel_id=1, source_target_pairs={{0,2},{2,0},{1,3},{3,1},{4,6},{6,4},{5,7},{7,5},{8,10},{10,8},{9,1... | collective-permute-start | bytes 245768 | tf_op jit(solution)/shard_map/ppermute | solution.py:344
  31.3 8.4 %collective-permute-start.10 = (bf16[320,128]{1,0:T(8,128)(2,1)S(1)}, bf16[320,128]{1,0:T(8,128)(2,1)S(1)}, u32[]{:S(2)}, u32[]{:S(2)}) collective-permute-start(bf16[320,128]{1,0:T(8,128)(2,1)S(1)} %add_convert_fusion.own_ref), channel_id=1, source_target_pairs={{0,8},{4,12},{8,0},{12,4},{1,9},{5,13},{9,1},{13,5},{2,10},{6,14},... | collective-permute-start | bytes 245768 | tf_op jit(solution)/shard_map/ppermute | solution.py:440
  31.6 8.1 %collective-permute-start.8 = (bf16[320,128]{1,0:T(8,128)(2,1)S(1)}, bf16[320,128]{1,0:T(8,128)(2,1)S(1)}, u32[]{:S(2)}, u32[]{:S(2)}) collective-permute-start(bf16[320,128]{1,0:T(8,128)(2,1)S(1)} %add_convert_fusion.own_ref), channel_id=1, source_target_pairs={{0,12},{4,8},{8,4},{12,0},{1,13},{5,9},{9,5},{13,1},{2,14},{6,10},... | collective-permute-start | bytes 245768 | tf_op jit(solution)/shard_map/ppermute | solution.py:440
  33.7 6.3 %collective-permute-start.9 = (bf16[320,128]{1,0:T(8,128)(2,1)S(1)}, bf16[320,128]{1,0:T(8,128)(2,1)S(1)}, u32[]{:S(2)}, u32[]{:S(2)}) collective-permute-start(bf16[320,128]{1,0:T(8,128)(2,1)S(1)} %add_convert_fusion.own_ref), channel_id=1, source_target_pairs={{0,4},{4,0},{8,12},{12,8},{1,5},{5,1},{9,13},{13,9},{2,6},{6,2},{1... | collective-permute-start | bytes 245768 | tf_op jit(solution)/shard_map/ppermute | solution.py:440
  40.0 1.4 %collective-permute-start.11 = (bf16[512,128]{1,0:T(8,128)(2,1)S(1)}, bf16[512,128]{1,0:T(8,128)(2,1)S(1)}, u32[]{:S(2)}, u32[]{:S(2)}) collective-permute-start(bf16[512,128]{1,0:T(8,128)(2,1)S(1)} %shard_map.100.refs_0_), channel_id=1, source_target_pairs={{0,1},{1,0},{2,3},{3,2},{4,5},{5,4},{6,7},{7,6},{8,9},{9,8},{10,11... | collective-permute-start | bytes 393224 | tf_op jit(solution)/shard_map/ppermute | solution.py:451

commit v5 on v4

--- a/solution.py
+++ b/solution.py
@@ -177,24 +177,21 @@
     (
         message_ref,
         query_ref,
-        plain_ref,
         lines_ref,
         table_ref,
         before_ref,
         totals_ref,
-        positives_ref,
-        own_weights_ref,
         pos_ref,
         unit_ref,
         turned_ref,
-    ) = refs[:12]
-    weights_refs = refs[12 : 11 + others]
-    piece_refs = refs[11 + others : 11 + 2 * others]
-    own_ref, own_grad_ref, losses_ref, last_ref, grad_ref = refs[11 + 2 * others :]
-    rows, count = own_weights_ref.shape
+    ) = refs[:9]
+    weights_refs = refs[9 : 8 + others]
+    piece_refs = refs[8 + others : 8 + 2 * others]
+    own_grad_ref, sums_ref, last_ref, grad_ref = refs[8 + 2 * others :]
+    rows, count = last_ref.shape
     totals, weighted = add_block(message_ref, query_ref, lines_ref, table_ref, before_ref, totals_ref[0:1, :], last_ref)
-    losses_ref[...] = jnp.log(totals) - lines_ref[1:2, :]
     share = 1.0 / totals
+    sums_ref[...] = jnp.concatenate([totals, share, jnp.zeros((6, count), f32)], axis=0)
     cot = weighted * share - pos_ref[...]
     unit = unit_ref[...]
     along = jnp.sum(unit * cot, axis=0, keepdims=True)
@@ -202,9 +199,6 @@
     shared = (query_ref[...].astype(f32) * share).astype(bf16)
     for step, weights_ref in zip(chain, list(weights_refs) + [last_ref]):
         piece_refs[step - 1][0:rows, :] = contract(weights_ref[...], shared, (1, 1)).astype(bf16)
-    own = lax.broadcasted_iota(jnp.int32, (rows, count), 0) == positives_ref[...]
-    grads = (own_weights_ref[...] * share - own.astype(f32)).astype(bf16)
-    own_ref[...] = jnp.dot(grads, plain_ref[...], preferred_element_type=f32)
     grad_ref[...] = contract(turned_ref[...], dz, (1, 1))
     me = lax.axis_index("neg")
     part = grad_ref.shape[0] // ring
@@ -212,6 +206,13 @@
     for step, piece_ref in enumerate(piece_refs):
         target = source_of(me, step + 1, ring)
         piece_ref[rows : rows + part, :] = grad_ref[pl.ds(pl.multiple_of(target * part, part), part), :].astype(bf16)
+
+
+def own_block(sums_ref, lines_ref, positives_ref, weights_ref, plain_ref, own_ref, losses_ref):
+    losses_ref[...] = jnp.log(sums_ref[0:1, :]) - lines_ref[1:2, :]
+    own = lax.broadcasted_iota(jnp.int32, weights_ref.shape, 0) == positives_ref[...]
+    grads = (weights_ref[...] * sums_ref[1:2, :] - own.astype(f32)).astype(bf16)
+    own_ref[...] = jnp.dot(grads, plain_ref[...], preferred_element_type=f32)
 
 
 def item_gradient(scale, others, own_ref, own_grad_ref, unit_ref, inverse_ref, turned_ref, *refs):
@@ -418,13 +419,19 @@
         weights.append(block_weights)
     results = call(
         functools.partial(last_block, scale, others, ring, chain),
-        [out((rows + part, width), bf16)] * others + [out((rows, width)), out((part, width)), out((1, count))],
-        [received[chain[-1] - 1], queries, plain, lines, table, weighted, totals, spots, own_weights, pos_items, query_unit, turned] + weights,
+        [out((rows + part, width), bf16)] * others + [out((part, width)), out((8, count))],
+        [received[chain[-1] - 1], queries, lines, table, weighted, totals, pos_items, query_unit, turned] + weights,
         scratch=[pltpu.VMEM((rows, count), bf16), pltpu.VMEM((hidden, width), f32)],
         flops=6 * count * width * rows * (others + 1),
     )
-    own_piece, own_grad, losses = results[others:]
+    own_grad, sums = results[others:]
     back = [lax.ppermute(piece, "neg", sent_back(pairs)) for piece, pairs in zip(results, exchange)]
+    own_piece, losses = call(
+        own_block,
+        [out((rows, width)), out((1, count))],
+        [sums, lines, spots, own_weights, plain],
+        flops=2 * rows * width * count,
+    )
     kept = (hidden + part) // 2
     keep, send = call(
         functools.partial(item_gradient, scale, others),

time: 42.3 us -> 42.3 us (level)
  waiting for transfers between devices: 19.7 us -> 19 us
  Pallas kernels: 6.34 us -> 6.96 us
    ppermute x3, waiting for transfers between devices: 5.42 us -> 4.71 us  [on_device(): lax.ppermute(piece, 'neg', sent_back(pairs))]
    pallas_call x7 -> x8, Pallas kernels: 4.84 us -> 5.45 us  [call(): pl.pallas_call(kernel, out_shape=tuple((jax.ShapeDtypeStruct(s.shape, s.d...]
  transfers between devices with their start and end apart: 12 -> 12, of which waited for: 9 -> 9; matrix products, arithmetic and copies ran while one was open for 0% -> 0% of each run, Pallas kernels for 7% -> 8%
where the time goes in v5:
time: 42.3 us; the launch traced here: 42.1 us
  waiting for transfers between devices  19 us (45%)
  starting transfers between devices  15.4 us (36%)
  Pallas kernels  6.96 us (16%)
  between operations  0.73 us (2%)
    ppermute x3, starting transfers between devices, on_device(): received = [lax.ppermute(message, 'neg', pairs) for pairs in exchange]  5.67 us
    pallas_call x8, Pallas kernels, call(): pl.pallas_call(kernel, out_shape=tuple((jax.ShapeDtypeStruct(s.shape, s.d...  5.45 us
    ppermute x3, waiting for transfers between devices, on_device(): got = [lax.ppermute(half, 'neg', pairs) for pairs in exchange]  5.16 us
    ppermute x3, waiting for transfers between devices, on_device(): lax.ppermute(piece, 'neg', sent_back(pairs))  4.71 us
    ppermute x3, starting transfers between devices, on_device(): lax.ppermute(piece, 'neg', sent_back(pairs))  4.45 us
    ppermute x3, waiting for transfers between devices, on_device(): received = [lax.ppermute(message, 'neg', pairs) for pairs in exchange]  4.18 us
    ppermute x3, starting transfers between devices, on_device(): got = [lax.ppermute(half, 'neg', pairs) for pairs in exchange]  3.55 us
    ppermute x1, waiting for transfers between devices, sum_over(): lax.ppermute(values, axis, pairs).astype(f32)  3 us
  transfers between devices with their start and end apart: 12, of which 9 were waited for; matrix products, arithmetic and copies ran while one was open for 0% of the time, Pallas kernels for 8%

profile of v5, /device:TPU:0, one launch (start us, length us, event | category | flops | bytes accessed | tf_op | source)
XLA Modules:
  0.0 42.1 jit_solution(8726465715308627911)
XLA Ops:
  0.6 1.4 %shard_map.94 = (bf16[272,128]{1,0:T(8,128)(2,1)S(1)}, f32[256,128]{1,0:T(8,128)S(1)}, f32[256,128]{1,0:T(8,128)S(1)}, bf16[512,512]{1,0:T(8,128)(2,1)S(1)}, bf1...) custom-call(bf16[512,512]{1,0:T(8,128)(2,1)} %refs_0_.1, bf16[512,128]{1,0:T(8,128)(2,1)} %refs_1_.1, ...), custom_call_target="tpu_custom_call" | custom-call | flops 33554432 | bytes 2304000 | tf_op jit(solution)/shard_map/pallas_call | solution.py:297
  2.0 3.1 %collective-permute-start.2 = (bf16[272,128]{1,0:T(8,128)(2,1)S(1)}, bf16[272,128]{1,0:T(8,128)(2,1)S(1)}, u32[]{:S(2)}, u32[]{:S(2)}) collective-permute-start(bf16[272,128]{1,0:T(8,128)(2,1)S(1)} %get-tuple-element.39.message_ref), channel_id=1, source_target_pairs={{0,4},{4,0},{8,12},{12,8},{1,5},{5,1},{9,13},{13,9},{2,6},{6,2},{1... | collective-permute-start | bytes 208904 | tf_op jit(solution)/shard_map/ppermute | solution.py:390
  5.1 2.6 %collective-permute-start.1 = (bf16[272,128]{1,0:T(8,128)(2,1)S(1)}, bf16[272,128]{1,0:T(8,128)(2,1)S(1)}, u32[]{:S(2)}, u32[]{:S(2)}) collective-permute-start(bf16[272,128]{1,0:T(8,128)(2,1)S(1)} %get-tuple-element.39.message_ref), channel_id=1, source_target_pairs={{0,8},{4,12},{8,0},{12,4},{1,9},{5,13},{9,1},{13,5},{2,10},{6,14},... | collective-permute-start | bytes 208904 | tf_op jit(solution)/shard_map/ppermute | solution.py:390
  7.7 0.0 collective-permute-start
  7.7 0.9 %shard_map.95 = (f32[128,512]{1,0:T(8,128)S(1)}, bf16[128,512]{1,0:T(8,128)(2,1)S(1)}, bf16[512,128]{1,0:T(8,128)(2,1)S(1)}, f32[256,512]{1,0:T(8,128)S(1)}, f32...) custom-call(bf16[512,512]{1,0:T(8,128)(2,1)S(1)} %get-tuple-element., ...), custom_call_target="tpu_custom_call" | custom-call | flops 167772160 | bytes 3381248 | tf_op jit(solution)/shard_map/pallas_call | solution.py:297
  8.6 0.0 collective-permute-done.2.message_ref
  8.6 0.5 %shard_map.96 = (bf16[256,512]{1,0:T(8,128)(2,1)S(1)}, f32[128,512]{1,0:T(8,128)S(1)}, f32[8,512]{1,0:T(8,128)S(1)}) custom-call(bf16[272,128]{1,0:T(8,128)(2,1)S(1)} %collective-permute-done.2.message_ref, bf16[128,512]{1,0:T(8,128)(2,1)S(1)} %get-tuple-element.44.query_ref.refs_1_, f32[8,512]{1,0:T(8,128)S(1)} %get-tuple-element.45.lines_ref.totals_ref.refs_2_, ...), custom_call_target="tpu_custom_call" | custom-call | flops 67108864 | bytes 1052672 | tf_op jit(solution)/shard_map/pallas_call | solution.py:297
  9.2 3.4 %collective-permute-done.1.message_ref = bf16[272,128]{1,0:T(8,128)(2,1)S(1)} collective-permute-done((bf16[272,128]{1,0:T(8,128)(2,1)S(1)}, bf16[272,128]{1,0:T(8,128)(2,1)S(1)}, u32[]{:S(2)}, u32[]{:S(2)}) %collective-permute-start.1) | collective-permute-done | bytes 69664 | tf_op jit(solution)/shard_map/ppermute | solution.py:390
  12.6 0.5 %shard_map.97 = (bf16[256,512]{1,0:T(8,128)(2,1)S(1)}, f32[128,512]{1,0:T(8,128)S(1)}, f32[8,512]{1,0:T(8,128)S(1)}) custom-call(bf16[272,128]{1,0:T(8,128)(2,1)S(1)} %collective-permute-done.1.message_ref, bf16[128,512]{1,0:T(8,128)(2,1)S(1)} %get-tuple-element.44.query_ref.refs_1_, f32[8,512]{1,0:T(8,128)S(1)} %get-tuple-element.45.lines_ref.totals_ref.refs_2_, ...), custom_call_target="tpu_custom_call" | custom-call | flops 67108864 | bytes 1052672 | tf_op jit(solution)/shard_map/pallas_call | solution.py:297
  13.2 0.7 %collective-permute-done.refs_0_ = bf16[272,128]{1,0:T(8,128)(2,1)S(1)} collective-permute-done((bf16[272,128]{1,0:T(8,128)(2,1)S(1)}, bf16[272,128]{1,0:T(8,128)(2,1)S(1)}, u32[]{:S(2)}, u32[]{:S(2)}) %collective-permute-start) | collective-permute-done | bytes 69664 | tf_op jit(solution)/shard_map/ppermute | solution.py:390
  13.9 1.0 %shard_map.98 = (bf16[384,128]{1,0:T(8,128)(2,1)S(1)}, bf16[384,128]{1,0:T(8,128)(2,1)S(1)}, bf16[384,128]{1,0:T(8,128)(2,1)S(1)}, f32[128,128]{1,0:T(8,128)S(1)}, f32[8,512]{1,0:T(8,128)S(1)}) custom-call(bf16[272,128]{1,0:T(8,128)(2,1)S(1)} %collective-permute-done.refs_0_, bf16[128,512]{1,0:T(8,128)(2,1)S(1)} %get-tuple-element.44.query_ref.refs_1_, ...), custom_call_target="tpu_custom_call" | custom-call | flops 402653184 | bytes 2461696 | tf_op jit(solution)/shard_map/pallas_call | solution.py:297
  14.9 2.6 %collective-permute-start.3 = (bf16[384,128]{1,0:T(8,128)(2,1)S(1)}, bf16[384,128]{1,0:T(8,128)(2,1)S(1)}, u32[]{:S(2)}, u32[]{:S(2)}) collective-permute-start(bf16[384,128]{1,0:T(8,128)(2,1)S(1)} %get-tuple-element.65), channel_id=1, source_target_pairs={{12,0},{8,4},{4,8},{0,12},{13,1},{9,5},{5,9},{1,13},{14,2},{10,6},... | collective-permute-start | bytes 294920 | tf_op jit(solution)/shard_map/ppermute | solution.py:428
  17.5 0.0 collective-permute-start.4
  17.5 1.9 %collective-permute-start.5 = (bf16[384,128]{1,0:T(8,128)(2,1)S(1)}, bf16[384,128]{1,0:T(8,128)(2,1)S(1)}, u32[]{:S(2)}, u32[]{:S(2)}) collective-permute-start(bf16[384,128]{1,0:T(8,128)(2,1)S(1)} %get-tuple-element.67), channel_id=1, source_target_pairs={{4,0},{0,4},{12,8},{8,12},{5,1},{1,5},{13,9},{9,13},{6,2},{2,6},{1... | collective-permute-start | bytes 294920 | tf_op jit(solution)/shard_map/ppermute | solution.py:428
  19.4 0.7 %shard_map.99 = (f32[256,128]{1,0:T(8,128)S(1)}, f32[1,512]{1,0:T(1,128)}) custom-call(f32[8,512]{1,0:T(8,128)S(1)} %get-tuple-element.57.sums_ref, f32[8,512]{1,0:T(8,128)S(1)} %get-tuple-element.45.lines_ref.totals_ref.refs_2_, s32[1,512]{1,0:T(1,128)S(1)} %get-tuple-element.42.positives_ref, f32[256,512]{1,0:T(8,128)S(1)} %get-tuple-element.58.weights_ref, ...), custom_call_target="tpu_custom_call" | custom-call | flops 33554432 | bytes 823296 | tf_op jit(solution)/shard_map/pallas_call | solution.py:297
  20.1 1.9 %collective-permute-done.3.refs_0_ = bf16[384,128]{1,0:T(8,128)(2,1)S(1)} collective-permute-done((bf16[384,128]{1,0:T(8,128)(2,1)S(1)}, bf16[384,128]{1,0:T(8,128)(2,1)S(1)}, u32[]{:S(2)}, u32[]{:S(2)}) %collective-permute-start.3) | collective-permute-done | bytes 98336 | tf_op jit(solution)/shard_map/ppermute | solution.py:428
  22.0 2.8 %collective-permute-done.4.refs_1_ = bf16[384,128]{1,0:T(8,128)(2,1)S(1)} collective-permute-done((bf16[384,128]{1,0:T(8,128)(2,1)S(1)}, bf16[384,128]{1,0:T(8,128)(2,1)S(1)}, u32[]{:S(2)}, u32[]{:S(2)}) %collective-permute-start.4) | collective-permute-done | bytes 98336 | tf_op jit(solution)/shard_map/ppermute | solution.py:428
  24.8 0.0 collective-permute-done.5.refs_2_
  24.8 0.3 shard_map.100
  25.1 0.1 collective-permute-start.6
  25.2 1.4 %collective-permute-done.6 = f32[320,128]{1,0:T(8,128)S(1)} collective-permute-done((f32[320,128]{1,0:T(8,128)S(1)}, f32[320,128]{1,0:T(8,128)S(1)}, u32[]{:S(2)}, u32[]{:S(2)}) %collective-permute-start.6) | collective-permute-done | bytes 163872 | tf_op jit(solution)/shard_map/ppermute | solution.py:443
  26.6 1.6 %collective-permute-start.7 = (bf16[320,128]{1,0:T(8,128)(2,1)S(1)}, bf16[320,128]{1,0:T(8,128)(2,1)S(1)}, u32[]{:S(2)}, u32[]{:S(2)}) collective-permute-start(bf16[320,128]{1,0:T(8,128)(2,1)S(1)} %add_convert_fusion.1), channel_id=1, source_target_pairs={{0,2},{2,0},{1,3},{3,1},{4,6},{6,4},{5,7},{7,5},{8,10},{10,8},{9,1... | collective-permute-start | bytes 245768 | tf_op jit(solution)/shard_map/ppermute | solution.py:345
  28.2 3.0 %collective-permute-done.7 = bf16[320,128]{1,0:T(8,128)(2,1)S(1)} collective-permute-done((bf16[320,128]{1,0:T(8,128)(2,1)S(1)}, bf16[320,128]{1,0:T(8,128)(2,1)S(1)}, u32[]{:S(2)}, u32[]{:S(2)}) %collective-permute-start.7) | collective-permute-done | bytes 81952 | tf_op jit(solution)/shard_map/ppermute | solution.py:345
  31.2 0.3 collective-permute-start.10
  31.5 2.1 %collective-permute-start.8 = (bf16[320,128]{1,0:T(8,128)(2,1)S(1)}, bf16[320,128]{1,0:T(8,128)(2,1)S(1)}, u32[]{:S(2)}, u32[]{:S(2)}) collective-permute-start(bf16[320,128]{1,0:T(8,128)(2,1)S(1)} %add_convert_fusion.own_ref), channel_id=1, source_target_pairs={{0,12},{4,8},{8,4},{12,0},{1,13},{5,9},{9,5},{13,1},{2,14},{6,10},... | collective-permute-start | bytes 245768 | tf_op jit(solution)/shard_map/ppermute | solution.py:447
  33.6 1.2 %collective-permute-start.9 = (bf16[320,128]{1,0:T(8,128)(2,1)S(1)}, bf16[320,128]{1,0:T(8,128)(2,1)S(1)}, u32[]{:S(2)}, u32[]{:S(2)}) collective-permute-start(bf16[320,128]{1,0:T(8,128)(2,1)S(1)} %add_convert_fusion.own_ref), channel_id=1, source_target_pairs={{0,4},{4,0},{8,12},{12,8},{1,5},{5,1},{9,13},{13,9},{2,6},{6,2},{1... | collective-permute-start | bytes 245768 | tf_op jit(solution)/shard_map/ppermute | solution.py:447
  34.8 4.8 %collective-permute-done.10.refs_2_ = bf16[320,128]{1,0:T(8,128)(2,1)S(1)} collective-permute-done((bf16[320,128]{1,0:T(8,128)(2,1)S(1)}, bf16[320,128]{1,0:T(8,128)(2,1)S(1)}, u32[]{:S(2)}, u32[]{:S(2)}) %collective-permute-start.10) | collective-permute-done | bytes 81952 | tf_op jit(solution)/shard_map/ppermute | solution.py:447
  39.5 0.0 collective-permute-done.8.refs_0_
  39.5 0.4 collective-permute-done.9.refs_1_
  40.0 0.1 collective-permute-start.11
  40.0 0.8 %shard_map.102 = (f32[512,128]{1,0:T(8,128)}, f32[512,128]{1,0:T(8,128)}) custom-call(bf16[512,128]{1,0:T(8,128)(2,1)S(1)} %shard_map.101.refs_0_), custom_call_target="tpu_custom_call" | custom-call | bytes 393216 | tf_op jit(solution)/shard_map/pallas_call | solution.py:282
  40.8 0.6 %collective-permute-done.11.refs_0_ = bf16[512,128]{1,0:T(8,128)(2,1)S(1)} collective-permute-done((bf16[512,128]{1,0:T(8,128)(2,1)S(1)}, bf16[512,128]{1,0:T(8,128)(2,1)S(1)}, u32[]{:S(2)}, u32[]{:S(2)}) %collective-permute-start.11) | collective-permute-done | bytes 131104 | tf_op jit(solution)/shard_map/ppermute | solution.py:458
  41.4 0.8 %shard_map.103 = (f32[512,128]{1,0:T(8,128)}, f32[512,128]{1,0:T(8,128)}) custom-call(bf16[512,128]{1,0:T(8,128)(2,1)S(1)} %collective-permute-done.11.refs_0_, f32[512,128]{1,0:T(8,128)} %get-tuple-element.70.refs_1_, f32[512,128]{1,0:T(8,128)} %get-tuple-element.71.refs_2_), custom_call_target="tpu_custom_call", output_to_operand_aliasing={{0}: (1, {}), {1}: (2, {})} | custom-call | bytes 393216 | tf_op jit(solution)/shard_map/pallas_call | solution.py:282
  (3 shorter events, 0.1 us)
Async XLA Ops:
  2.0 6.6 %collective-permute-start.2 = (bf16[272,128]{1,0:T(8,128)(2,1)S(1)}, bf16[272,128]{1,0:T(8,128)(2,1)S(1)}, u32[]{:S(2)}, u32[]{:S(2)}) collective-permute-start(bf16[272,128]{1,0:T(8,128)(2,1)S(1)} %get-tuple-element.39.message_ref), channel_id=1, source_target_pairs={{0,4},{4,0},{8,12},{12,8},{1,5},{5,1},{9,13},{13,9},{2,6},{6,2},{1... | collective-permute-start | bytes 208904 | tf_op jit(solution)/shard_map/ppermute | solution.py:390
  5.1 7.5 %collective-permute-start.1 = (bf16[272,128]{1,0:T(8,128)(2,1)S(1)}, bf16[272,128]{1,0:T(8,128)(2,1)S(1)}, u32[]{:S(2)}, u32[]{:S(2)}) collective-permute-start(bf16[272,128]{1,0:T(8,128)(2,1)S(1)} %get-tuple-element.39.message_ref), channel_id=1, source_target_pairs={{0,8},{4,12},{8,0},{12,4},{1,9},{5,13},{9,1},{13,5},{2,10},{6,14},... | collective-permute-start | bytes 208904 | tf_op jit(solution)/shard_map/ppermute | solution.py:390
  7.7 6.2 %collective-permute-start = (bf16[272,128]{1,0:T(8,128)(2,1)S(1)}, bf16[272,128]{1,0:T(8,128)(2,1)S(1)}, u32[]{:S(2)}, u32[]{:S(2)}) collective-permute-start(bf16[272,128]{1,0:T(8,128)(2,1)S(1)} %get-tuple-element.39.message_ref), channel_id=1, source_target_pairs={{0,12},{4,8},{8,4},{12,0},{1,13},{5,9},{9,5},{13,1},{2,14},{6,10},... | collective-permute-start | bytes 208904 | tf_op jit(solution)/shard_map/ppermute | solution.py:390
  14.9 7.0 %collective-permute-start.3 = (bf16[384,128]{1,0:T(8,128)(2,1)S(1)}, bf16[384,128]{1,0:T(8,128)(2,1)S(1)}, u32[]{:S(2)}, u32[]{:S(2)}) collective-permute-start(bf16[384,128]{1,0:T(8,128)(2,1)S(1)} %get-tuple-element.65), channel_id=1, source_target_pairs={{12,0},{8,4},{4,8},{0,12},{13,1},{9,5},{5,9},{1,13},{14,2},{10,6},... | collective-permute-start | bytes 294920 | tf_op jit(solution)/shard_map/ppermute | solution.py:428
  17.5 7.3 %collective-permute-start.4 = (bf16[384,128]{1,0:T(8,128)(2,1)S(1)}, bf16[384,128]{1,0:T(8,128)(2,1)S(1)}, u32[]{:S(2)}, u32[]{:S(2)}) collective-permute-start(bf16[384,128]{1,0:T(8,128)(2,1)S(1)} %get-tuple-element.66), channel_id=1, source_target_pairs={{8,0},{12,4},{0,8},{4,12},{9,1},{13,5},{1,9},{5,13},{10,2},{14,6},... | collective-permute-start | bytes 294920 | tf_op jit(solution)/shard_map/ppermute | solution.py:428
  17.5 7.3 %collective-permute-start.5 = (bf16[384,128]{1,0:T(8,128)(2,1)S(1)}, bf16[384,128]{1,0:T(8,128)(2,1)S(1)}, u32[]{:S(2)}, u32[]{:S(2)}) collective-permute-start(bf16[384,128]{1,0:T(8,128)(2,1)S(1)} %get-tuple-element.67), channel_id=1, source_target_pairs={{4,0},{0,4},{12,8},{8,12},{5,1},{1,5},{13,9},{9,13},{6,2},{2,6},{1... | collective-permute-start | bytes 294920 | tf_op jit(solution)/shard_map/ppermute | solution.py:428
  25.1 1.5 %collective-permute-start.6 = (f32[320,128]{1,0:T(8,128)S(1)}, f32[320,128]{1,0:T(8,128)S(1)}, u32[]{:S(2)}, u32[]{:S(2)}) collective-permute-start(f32[320,128]{1,0:T(8,128)S(1)} %get-tuple-element.69), channel_id=1, source_target_pairs={{0,1},{1,0},{2,3},{3,2},{4,5},{5,4},{6,7},{7,6},{8,9},{9,8},{10,11... | collective-permute-start | bytes 491528 | tf_op jit(solution)/shard_map/ppermute | solution.py:443
  26.6 4.6 %collective-permute-start.7 = (bf16[320,128]{1,0:T(8,128)(2,1)S(1)}, bf16[320,128]{1,0:T(8,128)(2,1)S(1)}, u32[]{:S(2)}, u32[]{:S(2)}) collective-permute-start(bf16[320,128]{1,0:T(8,128)(2,1)S(1)} %add_convert_fusion.1), channel_id=1, source_target_pairs={{0,2},{2,0},{1,3},{3,1},{4,6},{6,4},{5,7},{7,5},{8,10},{10,8},{9,1... | collective-permute-start | bytes 245768 | tf_op jit(solution)/shard_map/ppermute | solution.py:345
  31.2 8.3 %collective-permute-start.10 = (bf16[320,128]{1,0:T(8,128)(2,1)S(1)}, bf16[320,128]{1,0:T(8,128)(2,1)S(1)}, u32[]{:S(2)}, u32[]{:S(2)}) collective-permute-start(bf16[320,128]{1,0:T(8,128)(2,1)S(1)} %add_convert_fusion.own_ref), channel_id=1, source_target_pairs={{0,8},{4,12},{8,0},{12,4},{1,9},{5,13},{9,1},{13,5},{2,10},{6,14},... | collective-permute-start | bytes 245768 | tf_op jit(solution)/shard_map/ppermute | solution.py:447
  31.5 8.0 %collective-permute-start.8 = (bf16[320,128]{1,0:T(8,128)(2,1)S(1)}, bf16[320,128]{1,0:T(8,128)(2,1)S(1)}, u32[]{:S(2)}, u32[]{:S(2)}) collective-permute-start(bf16[320,128]{1,0:T(8,128)(2,1)S(1)} %add_convert_fusion.own_ref), channel_id=1, source_target_pairs={{0,12},{4,8},{8,4},{12,0},{1,13},{5,9},{9,5},{13,1},{2,14},{6,10},... | collective-permute-start | bytes 245768 | tf_op jit(solution)/shard_map/ppermute | solution.py:447
  33.6 6.3 %collective-permute-start.9 = (bf16[320,128]{1,0:T(8,128)(2,1)S(1)}, bf16[320,128]{1,0:T(8,128)(2,1)S(1)}, u32[]{:S(2)}, u32[]{:S(2)}) collective-permute-start(bf16[320,128]{1,0:T(8,128)(2,1)S(1)} %add_convert_fusion.own_ref), channel_id=1, source_target_pairs={{0,4},{4,0},{8,12},{12,8},{1,5},{5,1},{9,13},{13,9},{2,6},{6,2},{1... | collective-permute-start | bytes 245768 | tf_op jit(solution)/shard_map/ppermute | solution.py:447
  40.0 1.4 %collective-permute-start.11 = (bf16[512,128]{1,0:T(8,128)(2,1)S(1)}, bf16[512,128]{1,0:T(8,128)(2,1)S(1)}, u32[]{:S(2)}, u32[]{:S(2)}) collective-permute-start(bf16[512,128]{1,0:T(8,128)(2,1)S(1)} %shard_map.101.refs_0_), channel_id=1, source_target_pairs={{0,1},{1,0},{2,3},{3,2},{4,5},{5,4},{6,7},{7,6},{8,9},{9,8},{10,11... | collective-permute-start | bytes 393224 | tf_op jit(solution)/shard_map/ppermute | solution.py:458

commit v6 on v5

--- a/solution.py
+++ b/solution.py
@@ -173,7 +173,7 @@
     sums_ref[...] = jnp.broadcast_to(totals, sums_ref.shape)
 
 
-def last_block(scale, others, ring, chain, *refs):
+def last_block(scale, others, chain, *refs):
     (
         message_ref,
         query_ref,
@@ -200,12 +200,11 @@
     for step, weights_ref in zip(chain, list(weights_refs) + [last_ref]):
         piece_refs[step - 1][0:rows, :] = contract(weights_ref[...], shared, (1, 1)).astype(bf16)
     grad_ref[...] = contract(turned_ref[...], dz, (1, 1))
-    me = lax.axis_index("neg")
-    part = grad_ref.shape[0] // ring
-    own_grad_ref[...] = grad_ref[pl.ds(pl.multiple_of(me * part, part), part), :]
-    for step, piece_ref in enumerate(piece_refs):
-        target = source_of(me, step + 1, ring)
-        piece_ref[rows : rows + part, :] = grad_ref[pl.ds(pl.multiple_of(target * part, part), part), :].astype(bf16)
+    part = grad_ref.shape[0] // 2
+    side = lax.rem(lax.axis_index("neg"), 2)
+    own_grad_ref[...] = grad_ref[pl.ds(pl.multiple_of(side * part, part), part), :]
+    sent = grad_ref[pl.ds(pl.multiple_of((1 - side) * part, part), part), :]
+    piece_refs[0][rows : rows + part, :] = sent.astype(bf16)
 
 
 def own_block(sums_ref, lines_ref, positives_ref, weights_ref, plain_ref, own_ref, losses_ref):
@@ -222,7 +221,8 @@
     query_grad = own_grad_ref[...]
     for ref in refs[:others]:
         cot = cot + ref[0:rows, :].astype(f32)
-        query_grad = query_grad + ref[rows:, :].astype(f32)
+        if ref.shape[0] > rows:
+            query_grad = query_grad + ref[rows:, :].astype(f32)
     unit = unit_ref[...]
     along = jnp.sum(unit * cot, axis=1, keepdims=True)
     dz = ((cot - unit * along) * (inverse_ref[...] * scale)).astype(bf16)
@@ -231,7 +231,7 @@
     for start, whole in ((0, grad), (grad.shape[0] // 2, query_grad)):
         half = whole.shape[0] // 2
         keep_ref[start : start + half, :] = jnp.where(first, whole[:half], whole[half:])
-        send_ref[start : start + half, :] = jnp.where(first, whole[half:], whole[:half])
+        send_ref[start : start + half, :] = jnp.where(first, whole[half:], whole[:half]).astype(bf16)
 
 
 def add_pieces(turns, item_rows, own_ref, *refs):
@@ -239,32 +239,32 @@
     values = [own_ref[...].astype(f32)]
     for step in range(1, len(turns) + 1):
         values.append(refs[turns.index(step)][...].astype(f32))
-    total = values[0] + values[1]
+    sums = [values[0], values[1]]
     if len(values) == 4:
-        total = total + (values[2] + values[3])
+        sums = [values[0] + values[2], values[1] + values[3]]
+    out_ref[0:item_rows, :] = (sums[0] + sums[1])[:item_rows].astype(bf16)
     query_rows = own_ref.shape[0] - item_rows
-    out_ref[0:item_rows, :] = total[:item_rows].astype(bf16)
-    for step, value in enumerate(values):
+    for step, value in enumerate(sums):
         start = item_rows + step * query_rows
         out_ref[start : start + query_rows, :] = value[item_rows:].astype(bf16)
 
 
-def place_kernel(ring, direct, other, *refs):
+def place_kernel(direct, other, *refs):
     values_ref = refs[0]
     query_hbm, item_hbm, wide_ref, sems = refs[-4:]
     sub = lax.axis_index("sub")
     side = 1 - sub if other else sub
-    base = lax.axis_index("neg") if direct else 0
+    base = lax.rem(lax.axis_index("neg"), 2) if direct else 0
     half = item_hbm.shape[0] // 2
-    part = half // ring
+    part = half // 2
     wide_ref[...] = values_ref[...].astype(f32)
     copies = [
         pltpu.make_async_copy(
-            wide_ref.at[pl.ds(0, half)], item_hbm.at[pl.ds(pl.multiple_of(side * half, half), half)], sems.at[ring]
+            wide_ref.at[pl.ds(0, half)], item_hbm.at[pl.ds(pl.multiple_of(side * half, half), half)], sems.at[2]
         )
     ]
-    for step in range(ring):
-        start = pl.multiple_of(partner_of(base, step, ring) * (2 * part) + side * part, part)
+    for step in range(2):
+        start = pl.multiple_of((base ^ step) * half + side * part, part)
         copies.append(
             pltpu.make_async_copy(
                 wide_ref.at[pl.ds(half + step * part, part)], query_hbm.at[pl.ds(start, part)], sems.at[step]
@@ -276,16 +276,16 @@
         copy.wait()
 
 
-def place(ring, direct, other, values, outs):
+def place(direct, other, values, outs):
     hbm = pl.BlockSpec(memory_space=pltpu.HBM)
     shape = jax.ShapeDtypeStruct(values.shape, f32)
     return pl.pallas_call(
-        functools.partial(place_kernel, ring, direct, other),
+        functools.partial(place_kernel, direct, other),
         out_shape=(shape, shape),
         in_specs=[pl.BlockSpec(memory_space=pltpu.VMEM)] + [hbm] * len(outs),
         out_specs=(hbm, hbm),
         input_output_aliases={1: 0, 2: 1} if outs else {},
-        scratch_shapes=[pltpu.VMEM(values.shape, f32), pltpu.SemaphoreType.DMA((ring + 1,))],
+        scratch_shapes=[pltpu.VMEM(values.shape, f32), pltpu.SemaphoreType.DMA((3,))],
         compiler_params=pltpu.CompilerParams(vmem_limit_bytes=32 * 1024 * 1024),
         cost_estimate=pl.CostEstimate(flops=0, bytes_accessed=6 * values.size, transcendentals=0),
     )(values, *outs)
@@ -356,7 +356,7 @@
     ring = lax.axis_size("neg")
     exchange = partners(ring)
     others = len(exchange)
-    part = hidden // ring
+    part = hidden // 2
     message, item_unit, item_inverse, query_feats, query_proj, spots, item_feats = call(
         item_tower,
         [
@@ -407,7 +407,7 @@
     )
     totals = lines
     weights = []
-    chain = ordered(others, (1, 2, 3))
+    chain = ordered(others, (3, 1, 2))
     for step in chain[:-1]:
         block = received[step - 1]
         block_weights, weighted, totals = call(
@@ -418,8 +418,8 @@
         )
         weights.append(block_weights)
     results = call(
-        functools.partial(last_block, scale, others, ring, chain),
-        [out((rows + part, width), bf16)] * others + [out((part, width)), out((8, count))],
+        functools.partial(last_block, scale, others, chain),
+        [out((rows + part, width), bf16)] + [out((rows, width), bf16)] * (others - 1) + [out((part, width)), out((8, count))],
         [received[chain[-1] - 1], queries, lines, table, weighted, totals, pos_items, query_unit, turned] + weights,
         scratch=[pltpu.VMEM((rows, count), bf16), pltpu.VMEM((hidden, width), f32)],
         flops=6 * count * width * rows * (others + 1),
@@ -435,29 +435,31 @@
     kept = (hidden + part) // 2
     keep, send = call(
         functools.partial(item_gradient, scale, others),
-        [out((kept, width)), out((kept, width))],
-        [own_piece, own_grad, item_unit, item_inverse, item_turned] + [back[step - 1] for step in ordered(others, (3, 2, 1))],
+        [out((kept, width)), out((kept, width), bf16)],
+        [own_piece, own_grad, item_unit, item_inverse, item_turned] + [back[step - 1] for step in ordered(others, (1, 3, 2))],
         flops=2 * rows * width * hidden,
     )
     swap = [(0, 1), (1, 0)]
-    half = sum_over(keep + lax.ppermute(send, "sub", swap), "rep")
+    half = sum_over(keep + lax.ppermute(send, "sub", swap).astype(f32), "rep")
     direct = ring in (2, 4)
     if direct:
         half = half.astype(bf16)
         got = [lax.ppermute(half, "neg", pairs) for pairs in exchange]
-        turns = ordered(others, (3, 1, 2))
+        turns = ordered(others, (1, 3, 2))
         mine = call(
             functools.partial(add_pieces, turns, hidden // 2),
             [out((hidden, width), bf16)],
             [half] + [got[step - 1] for step in turns],
         )[0]
     else:
-        item_half = lax.psum(half[: hidden // 2], "neg").astype(bf16)
-        query_half = lax.all_gather(half[hidden // 2 :].astype(bf16), "neg", axis=0, tiled=True)
-        mine = jnp.concatenate([item_half, query_half], axis=0)
+        item_half, query_half = half[: hidden // 2], half[hidden // 2 :]
+        first = lax.rem(lax.axis_index("neg"), 2) == 0
+        none = jnp.zeros_like(query_half)
+        both = [item_half, jnp.where(first, query_half, none), jnp.where(first, none, query_half)]
+        mine = lax.psum(jnp.concatenate(both, axis=0), "neg").astype(bf16)
     other = lax.ppermute(mine, "sub", swap)
-    outs = place(ring, direct, False, mine, ())
-    grad_query, grad_item = place(ring, direct, True, other, outs)
+    outs = place(direct, False, mine, ())
+    grad_query, grad_item = place(direct, True, other, outs)
     return (grad_query, grad_item, losses.reshape(count))
 
 

time: 42.3 us -> 41.9 us (level)
  waiting for transfers between devices: 19 us -> 18.4 us
    ppermute x3, waiting for transfers between devices: 4.18 us -> 3.05 us  [on_device(): received = [lax.ppermute(message, 'neg', pairs) for pairs in exchange]]
    ppermute x3, starting transfers between devices: 3.55 us -> 4.45 us  [on_device(): got = [lax.ppermute(half, 'neg', pairs) for pairs in exchange]]
    ppermute x3, starting transfers between devices: 4.45 us -> 3.66 us  [on_device(): lax.ppermute(piece, 'neg', sent_back(pairs))]
where the time goes in v6:
time: 41.9 us; the launch traced here: 41.7 us
  waiting for transfers between devices  18.4 us (44%)
  starting transfers between devices  15.6 us (37%)
  Pallas kernels  6.95 us (17%)
  between operations  0.72 us (2%)
    ppermute x3, starting transfers between devices, on_device(): received = [lax.ppermute(message, 'neg', pairs) for pairs in exchange]  5.75 us
    pallas_call x8, Pallas kernels, call(): pl.pallas_call(kernel, out_shape=tuple((jax.ShapeDtypeStruct(s.shape, s.d...  5.48 us
    ppermute x3, waiting for transfers between devices, on_device(): lax.ppermute(piece, 'neg', sent_back(pairs))  5.12 us
    ppermute x3, waiting for transfers between devices, on_device(): got = [lax.ppermute(half, 'neg', pairs) for pairs in exchange]  5.01 us
    ppermute x3, starting transfers between devices, on_device(): got = [lax.ppermute(half, 'neg', pairs) for pairs in exchange]  4.45 us
    ppermute x3, starting transfers between devices, on_device(): lax.ppermute(piece, 'neg', sent_back(pairs))  3.66 us
    ppermute x1, waiting for transfers between devices, sum_over(): lax.ppermute(values, axis, pairs).astype(f32)  3.35 us
    ppermute x3, waiting for transfers between devices, on_device(): received = [lax.ppermute(message, 'neg', pairs) for pairs in exchange]  3.05 us
  transfers between devices with their start and end apart: 12, of which 9 were waited for; matrix products, arithmetic and copies ran while one was open for 0% of the time, Pallas kernels for 8%

profile of v6, /device:TPU:0, one launch (start us, length us, event | category | flops | bytes accessed | tf_op | source)
XLA Modules:
  0.0 41.7 jit_solution(8913843564234137404)
XLA Ops:
  0.6 1.4 %shard_map.94 = (bf16[272,128]{1,0:T(8,128)(2,1)S(1)}, f32[256,128]{1,0:T(8,128)S(1)}, f32[256,128]{1,0:T(8,128)S(1)}, bf16[512,512]{1,0:T(8,128)(2,1)S(1)}, bf1...) custom-call(bf16[512,512]{1,0:T(8,128)(2,1)} %refs_0_.1, bf16[512,128]{1,0:T(8,128)(2,1)} %refs_1_.1, ...), custom_call_target="tpu_custom_call" | custom-call | flops 33554432 | bytes 2304000 | tf_op jit(solution)/shard_map/pallas_call | solution.py:297
  2.0 5.1 %collective-permute-start.2 = (bf16[272,128]{1,0:T(8,128)(2,1)S(1)}, bf16[272,128]{1,0:T(8,128)(2,1)S(1)}, u32[]{:S(2)}, u32[]{:S(2)}) collective-permute-start(bf16[272,128]{1,0:T(8,128)(2,1)S(1)} %get-tuple-element.39.message_ref), channel_id=1, source_target_pairs={{0,12},{4,8},{8,4},{12,0},{1,13},{5,9},{9,5},{13,1},{2,14},{6,10},... | collective-permute-start | bytes 208904 | tf_op jit(solution)/shard_map/ppermute | solution.py:390
  7.1 0.0 collective-permute-start.1
  7.1 0.6 %collective-permute-start = (bf16[272,128]{1,0:T(8,128)(2,1)S(1)}, bf16[272,128]{1,0:T(8,128)(2,1)S(1)}, u32[]{:S(2)}, u32[]{:S(2)}) collective-permute-start(bf16[272,128]{1,0:T(8,128)(2,1)S(1)} %get-tuple-element.39.message_ref), channel_id=1, source_target_pairs={{0,8},{4,12},{8,0},{12,4},{1,9},{5,13},{9,1},{13,5},{2,10},{6,14},... | collective-permute-start | bytes 208904 | tf_op jit(solution)/shard_map/ppermute | solution.py:390
  7.8 0.9 %shard_map.95 = (f32[128,512]{1,0:T(8,128)S(1)}, bf16[128,512]{1,0:T(8,128)(2,1)S(1)}, bf16[512,128]{1,0:T(8,128)(2,1)S(1)}, f32[256,512]{1,0:T(8,128)S(1)}, f32...) custom-call(bf16[512,512]{1,0:T(8,128)(2,1)S(1)} %get-tuple-element., ...), custom_call_target="tpu_custom_call" | custom-call | flops 167772160 | bytes 3381248 | tf_op jit(solution)/shard_map/pallas_call | solution.py:297
  8.7 1.5 %collective-permute-done.2.message_ref = bf16[272,128]{1,0:T(8,128)(2,1)S(1)} collective-permute-done((bf16[272,128]{1,0:T(8,128)(2,1)S(1)}, bf16[272,128]{1,0:T(8,128)(2,1)S(1)}, u32[]{:S(2)}, u32[]{:S(2)}) %collective-permute-start.2) | collective-permute-done | bytes 69664 | tf_op jit(solution)/shard_map/ppermute | solution.py:390
  10.1 0.5 %shard_map.96 = (bf16[256,512]{1,0:T(8,128)(2,1)S(1)}, f32[128,512]{1,0:T(8,128)S(1)}, f32[8,512]{1,0:T(8,128)S(1)}) custom-call(bf16[272,128]{1,0:T(8,128)(2,1)S(1)} %collective-permute-done.2.message_ref, bf16[128,512]{1,0:T(8,128)(2,1)S(1)} %get-tuple-element.44.query_ref.refs_1_, f32[8,512]{1,0:T(8,128)S(1)} %get-tuple-element.45.lines_ref.totals_ref.refs_2_, ...), custom_call_target="tpu_custom_call" | custom-call | flops 67108864 | bytes 1052672 | tf_op jit(solution)/shard_map/pallas_call | solution.py:297
  10.7 1.3 %collective-permute-done.1.message_ref = bf16[272,128]{1,0:T(8,128)(2,1)S(1)} collective-permute-done((bf16[272,128]{1,0:T(8,128)(2,1)S(1)}, bf16[272,128]{1,0:T(8,128)(2,1)S(1)}, u32[]{:S(2)}, u32[]{:S(2)}) %collective-permute-start.1) | collective-permute-done | bytes 69664 | tf_op jit(solution)/shard_map/ppermute | solution.py:390
  12.0 0.5 %shard_map.97 = (bf16[256,512]{1,0:T(8,128)(2,1)S(1)}, f32[128,512]{1,0:T(8,128)S(1)}, f32[8,512]{1,0:T(8,128)S(1)}) custom-call(bf16[272,128]{1,0:T(8,128)(2,1)S(1)} %collective-permute-done.1.message_ref, bf16[128,512]{1,0:T(8,128)(2,1)S(1)} %get-tuple-element.44.query_ref.refs_1_, f32[8,512]{1,0:T(8,128)S(1)} %get-tuple-element.45.lines_ref.totals_ref.refs_2_, ...), custom_call_target="tpu_custom_call" | custom-call | flops 67108864 | bytes 1052672 | tf_op jit(solution)/shard_map/pallas_call | solution.py:297
  12.5 0.3 collective-permute-done.refs_0_
  12.8 1.1 %shard_map.98 = (bf16[512,128]{1,0:T(8,128)(2,1)S(1)}, bf16[256,128]{1,0:T(8,128)(2,1)S(1)}, bf16[256,128]{1,0:T(8,128)(2,1)S(1)}, f32[256,128]{1,0:T(8,128)S(1)}, f32[8,512]{1,0:T(8,128)S(1)}) custom-call(bf16[272,128]{1,0:T(8,128)(2,1)S(1)} %collective-permute-done.refs_0_, bf16[128,512]{1,0:T(8,128)(2,1)S(1)} %get-tuple-element.44.query_ref.refs_1_, ...), custom_call_target="tpu_custom_call" | custom-call | flops 402653184 | bytes 2494464 | tf_op jit(solution)/shard_map/pallas_call | solution.py:297
  13.9 1.6 %collective-permute-start.3 = (bf16[512,128]{1,0:T(8,128)(2,1)S(1)}, bf16[512,128]{1,0:T(8,128)(2,1)S(1)}, u32[]{:S(2)}, u32[]{:S(2)}) collective-permute-start(bf16[512,128]{1,0:T(8,128)(2,1)S(1)} %get-tuple-element.65), channel_id=1, source_target_pairs={{4,0},{0,4},{12,8},{8,12},{5,1},{1,5},{13,9},{9,13},{6,2},{2,6},{1... | collective-permute-start | bytes 393224 | tf_op jit(solution)/shard_map/ppermute | solution.py:428
  15.5 2.0 %collective-permute-start.4 = (bf16[256,128]{1,0:T(8,128)(2,1)S(1)}, bf16[256,128]{1,0:T(8,128)(2,1)S(1)}, u32[]{:S(2)}, u32[]{:S(2)}) collective-permute-start(bf16[256,128]{1,0:T(8,128)(2,1)S(1)} %get-tuple-element.66), channel_id=1, source_target_pairs={{12,0},{8,4},{4,8},{0,12},{13,1},{9,5},{5,9},{1,13},{14,2},{10,6},... | collective-permute-start | bytes 196616 | tf_op jit(solution)/shard_map/ppermute | solution.py:428
  17.5 0.1 collective-permute-start.5
  17.6 0.7 %shard_map.99 = (f32[256,128]{1,0:T(8,128)S(1)}, f32[1,512]{1,0:T(1,128)}) custom-call(f32[8,512]{1,0:T(8,128)S(1)} %get-tuple-element.57.sums_ref, f32[8,512]{1,0:T(8,128)S(1)} %get-tuple-element.45.lines_ref.totals_ref.refs_2_, s32[1,512]{1,0:T(1,128)S(1)} %get-tuple-element.42.positives_ref, f32[256,512]{1,0:T(8,128)S(1)} %get-tuple-element.58.weights_ref, ...), custom_call_target="tpu_custom_call" | custom-call | flops 33554432 | bytes 823296 | tf_op jit(solution)/shard_map/pallas_call | solution.py:297
  18.3 3.5 %collective-permute-done.4.refs_1_ = bf16[256,128]{1,0:T(8,128)(2,1)S(1)} collective-permute-done((bf16[256,128]{1,0:T(8,128)(2,1)S(1)}, bf16[256,128]{1,0:T(8,128)(2,1)S(1)}, u32[]{:S(2)}, u32[]{:S(2)}) %collective-permute-start.4) | collective-permute-done | bytes 65568 | tf_op jit(solution)/shard_map/ppermute | solution.py:428
  21.8 1.6 %collective-permute-done.5.refs_2_ = bf16[256,128]{1,0:T(8,128)(2,1)S(1)} collective-permute-done((bf16[256,128]{1,0:T(8,128)(2,1)S(1)}, bf16[256,128]{1,0:T(8,128)(2,1)S(1)}, u32[]{:S(2)}, u32[]{:S(2)}) %collective-permute-start.5) | collective-permute-done | bytes 65568 | tf_op jit(solution)/shard_map/ppermute | solution.py:428
  23.4 0.0 collective-permute-done.3.refs_0_
  23.4 0.3 shard_map.100
  23.7 0.1 collective-permute-start.6
  23.8 1.3 %collective-permute-done.6 = bf16[384,128]{1,0:T(8,128)(2,1)S(1)} collective-permute-done((bf16[384,128]{1,0:T(8,128)(2,1)S(1)}, bf16[384,128]{1,0:T(8,128)(2,1)S(1)}, u32[]{:S(2)}, u32[]{:S(2)}) %collective-permute-start.6) | collective-permute-done | bytes 98336 | tf_op jit(solution)/shard_map/ppermute | solution.py:443
  25.1 1.6 %collective-permute-start.7 = (bf16[384,128]{1,0:T(8,128)(2,1)S(1)}, bf16[384,128]{1,0:T(8,128)(2,1)S(1)}, u32[]{:S(2)}, u32[]{:S(2)}) collective-permute-start(bf16[384,128]{1,0:T(8,128)(2,1)S(1)} %add_convert_fusion.1), channel_id=1, source_target_pairs={{0,2},{2,0},{1,3},{3,1},{4,6},{6,4},{5,7},{7,5},{8,10},{10,8},{9,1... | collective-permute-start | bytes 294920 | tf_op jit(solution)/shard_map/ppermute | solution.py:345
  26.7 3.3 %collective-permute-done.7 = bf16[384,128]{1,0:T(8,128)(2,1)S(1)} collective-permute-done((bf16[384,128]{1,0:T(8,128)(2,1)S(1)}, bf16[384,128]{1,0:T(8,128)(2,1)S(1)}, u32[]{:S(2)}, u32[]{:S(2)}) %collective-permute-start.7) | collective-permute-done | bytes 98336 | tf_op jit(solution)/shard_map/ppermute | solution.py:345
  30.0 0.4 collective-permute-start.10
  30.4 2.1 %collective-permute-start.8 = (bf16[384,128]{1,0:T(8,128)(2,1)S(1)}, bf16[384,128]{1,0:T(8,128)(2,1)S(1)}, u32[]{:S(2)}, u32[]{:S(2)}) collective-permute-start(bf16[384,128]{1,0:T(8,128)(2,1)S(1)} %add_convert_fusion.own_ref), channel_id=1, source_target_pairs={{0,4},{4,0},{8,12},{12,8},{1,5},{5,1},{9,13},{13,9},{2,6},{6,2},{1... | collective-permute-start | bytes 294920 | tf_op jit(solution)/shard_map/ppermute | solution.py:447
  32.5 2.0 %collective-permute-start.9 = (bf16[384,128]{1,0:T(8,128)(2,1)S(1)}, bf16[384,128]{1,0:T(8,128)(2,1)S(1)}, u32[]{:S(2)}, u32[]{:S(2)}) collective-permute-start(bf16[384,128]{1,0:T(8,128)(2,1)S(1)} %add_convert_fusion.own_ref), channel_id=1, source_target_pairs={{0,12},{4,8},{8,4},{12,0},{1,13},{5,9},{9,5},{13,1},{2,14},{6,10},... | collective-permute-start | bytes 294920 | tf_op jit(solution)/shard_map/ppermute | solution.py:447
  34.5 5.0 %collective-permute-done.10.refs_2_ = bf16[384,128]{1,0:T(8,128)(2,1)S(1)} collective-permute-done((bf16[384,128]{1,0:T(8,128)(2,1)S(1)}, bf16[384,128]{1,0:T(8,128)(2,1)S(1)}, u32[]{:S(2)}, u32[]{:S(2)}) %collective-permute-start.10) | collective-permute-done | bytes 98336 | tf_op jit(solution)/shard_map/ppermute | solution.py:447
  39.5 0.0 collective-permute-done.8.refs_0_
  39.5 0.0 collective-permute-done.9.refs_1_
  39.5 0.1 shard_map.101.refs_0_
  39.6 0.1 collective-permute-start.11
  39.6 0.7 %shard_map.102 = (f32[512,128]{1,0:T(8,128)}, f32[512,128]{1,0:T(8,128)}) custom-call(bf16[512,128]{1,0:T(8,128)(2,1)S(1)} %shard_map.101.refs_0_), custom_call_target="tpu_custom_call" | custom-call | bytes 393216 | tf_op jit(solution)/shard_map/pallas_call | solution.py:282
  40.4 0.6 %collective-permute-done.11.refs_0_ = bf16[512,128]{1,0:T(8,128)(2,1)S(1)} collective-permute-done((bf16[512,128]{1,0:T(8,128)(2,1)S(1)}, bf16[512,128]{1,0:T(8,128)(2,1)S(1)}, u32[]{:S(2)}, u32[]{:S(2)}) %collective-permute-start.11) | collective-permute-done | bytes 131104 | tf_op jit(solution)/shard_map/ppermute | solution.py:460
  41.0 0.7 %shard_map.103 = (f32[512,128]{1,0:T(8,128)}, f32[512,128]{1,0:T(8,128)}) custom-call(bf16[512,128]{1,0:T(8,128)(2,1)S(1)} %collective-permute-done.11.refs_0_, f32[512,128]{1,0:T(8,128)} %get-tuple-element.70.refs_1_, f32[512,128]{1,0:T(8,128)} %get-tuple-element.71.refs_2_), custom_call_target="tpu_custom_call", output_to_operand_aliasing={{0}: (1, {}), {1}: (2, {})} | custom-call | bytes 393216 | tf_op jit(solution)/shard_map/pallas_call | solution.py:282
  (2 shorter events, 0.1 us)
Async XLA Ops:
  2.0 8.1 %collective-permute-start.2 = (bf16[272,128]{1,0:T(8,128)(2,1)S(1)}, bf16[272,128]{1,0:T(8,128)(2,1)S(1)}, u32[]{:S(2)}, u32[]{:S(2)}) collective-permute-start(bf16[272,128]{1,0:T(8,128)(2,1)S(1)} %get-tuple-element.39.message_ref), channel_id=1, source_target_pairs={{0,12},{4,8},{8,4},{12,0},{1,13},{5,9},{9,5},{13,1},{2,14},{6,10},... | collective-permute-start | bytes 208904 | tf_op jit(solution)/shard_map/ppermute | solution.py:390
  7.1 4.9 %collective-permute-start.1 = (bf16[272,128]{1,0:T(8,128)(2,1)S(1)}, bf16[272,128]{1,0:T(8,128)(2,1)S(1)}, u32[]{:S(2)}, u32[]{:S(2)}) collective-permute-start(bf16[272,128]{1,0:T(8,128)(2,1)S(1)} %get-tuple-element.39.message_ref), channel_id=1, source_target_pairs={{0,4},{4,0},{8,12},{12,8},{1,5},{5,1},{9,13},{13,9},{2,6},{6,2},{1... | collective-permute-start | bytes 208904 | tf_op jit(solution)/shard_map/ppermute | solution.py:390
  7.1 5.7 %collective-permute-start = (bf16[272,128]{1,0:T(8,128)(2,1)S(1)}, bf16[272,128]{1,0:T(8,128)(2,1)S(1)}, u32[]{:S(2)}, u32[]{:S(2)}) collective-permute-start(bf16[272,128]{1,0:T(8,128)(2,1)S(1)} %get-tuple-element.39.message_ref), channel_id=1, source_target_pairs={{0,8},{4,12},{8,0},{12,4},{1,9},{5,13},{9,1},{13,5},{2,10},{6,14},... | collective-permute-start | bytes 208904 | tf_op jit(solution)/shard_map/ppermute | solution.py:390
  13.9 9.5 %collective-permute-start.3 = (bf16[512,128]{1,0:T(8,128)(2,1)S(1)}, bf16[512,128]{1,0:T(8,128)(2,1)S(1)}, u32[]{:S(2)}, u32[]{:S(2)}) collective-permute-start(bf16[512,128]{1,0:T(8,128)(2,1)S(1)} %get-tuple-element.65), channel_id=1, source_target_pairs={{4,0},{0,4},{12,8},{8,12},{5,1},{1,5},{13,9},{9,13},{6,2},{2,6},{1... | collective-permute-start | bytes 393224 | tf_op jit(solution)/shard_map/ppermute | solution.py:428
  15.5 6.3 %collective-permute-start.4 = (bf16[256,128]{1,0:T(8,128)(2,1)S(1)}, bf16[256,128]{1,0:T(8,128)(2,1)S(1)}, u32[]{:S(2)}, u32[]{:S(2)}) collective-permute-start(bf16[256,128]{1,0:T(8,128)(2,1)S(1)} %get-tuple-element.66), channel_id=1, source_target_pairs={{12,0},{8,4},{4,8},{0,12},{13,1},{9,5},{5,9},{1,13},{14,2},{10,6},... | collective-permute-start | bytes 196616 | tf_op jit(solution)/shard_map/ppermute | solution.py:428
  17.5 5.9 %collective-permute-start.5 = (bf16[256,128]{1,0:T(8,128)(2,1)S(1)}, bf16[256,128]{1,0:T(8,128)(2,1)S(1)}, u32[]{:S(2)}, u32[]{:S(2)}) collective-permute-start(bf16[256,128]{1,0:T(8,128)(2,1)S(1)} %get-tuple-element.67), channel_id=1, source_target_pairs={{8,0},{12,4},{0,8},{4,12},{9,1},{13,5},{1,9},{5,13},{10,2},{14,6},... | collective-permute-start | bytes 196616 | tf_op jit(solution)/shard_map/ppermute | solution.py:428
  23.7 1.4 %collective-permute-start.6 = (bf16[384,128]{1,0:T(8,128)(2,1)S(1)}, bf16[384,128]{1,0:T(8,128)(2,1)S(1)}, u32[]{:S(2)}, u32[]{:S(2)}) collective-permute-start(bf16[384,128]{1,0:T(8,128)(2,1)S(1)} %get-tuple-element.69), channel_id=1, source_target_pairs={{0,1},{1,0},{2,3},{3,2},{4,5},{5,4},{6,7},{7,6},{8,9},{9,8},{10,11... | collective-permute-start | bytes 294920 | tf_op jit(solution)/shard_map/ppermute | solution.py:443
  25.1 4.9 %collective-permute-start.7 = (bf16[384,128]{1,0:T(8,128)(2,1)S(1)}, bf16[384,128]{1,0:T(8,128)(2,1)S(1)}, u32[]{:S(2)}, u32[]{:S(2)}) collective-permute-start(bf16[384,128]{1,0:T(8,128)(2,1)S(1)} %add_convert_fusion.1), channel_id=1, source_target_pairs={{0,2},{2,0},{1,3},{3,1},{4,6},{6,4},{5,7},{7,5},{8,10},{10,8},{9,1... | collective-permute-start | bytes 294920 | tf_op jit(solution)/shard_map/ppermute | solution.py:345
  30.0 9.5 %collective-permute-start.10 = (bf16[384,128]{1,0:T(8,128)(2,1)S(1)}, bf16[384,128]{1,0:T(8,128)(2,1)S(1)}, u32[]{:S(2)}, u32[]{:S(2)}) collective-permute-start(bf16[384,128]{1,0:T(8,128)(2,1)S(1)} %add_convert_fusion.own_ref), channel_id=1, source_target_pairs={{0,8},{4,12},{8,0},{12,4},{1,9},{5,13},{9,1},{13,5},{2,10},{6,14},... | collective-permute-start | bytes 294920 | tf_op jit(solution)/shard_map/ppermute | solution.py:447
  30.4 9.1 %collective-permute-start.8 = (bf16[384,128]{1,0:T(8,128)(2,1)S(1)}, bf16[384,128]{1,0:T(8,128)(2,1)S(1)}, u32[]{:S(2)}, u32[]{:S(2)}) collective-permute-start(bf16[384,128]{1,0:T(8,128)(2,1)S(1)} %add_convert_fusion.own_ref), channel_id=1, source_target_pairs={{0,4},{4,0},{8,12},{12,8},{1,5},{5,1},{9,13},{13,9},{2,6},{6,2},{1... | collective-permute-start | bytes 294920 | tf_op jit(solution)/shard_map/ppermute | solution.py:447
  32.5 7.0 %collective-permute-start.9 = (bf16[384,128]{1,0:T(8,128)(2,1)S(1)}, bf16[384,128]{1,0:T(8,128)(2,1)S(1)}, u32[]{:S(2)}, u32[]{:S(2)}) collective-permute-start(bf16[384,128]{1,0:T(8,128)(2,1)S(1)} %add_convert_fusion.own_ref), channel_id=1, source_target_pairs={{0,12},{4,8},{8,4},{12,0},{1,13},{5,9},{9,5},{13,1},{2,14},{6,10},... | collective-permute-start | bytes 294920 | tf_op jit(solution)/shard_map/ppermute | solution.py:447
  39.6 1.4 %collective-permute-start.11 = (bf16[512,128]{1,0:T(8,128)(2,1)S(1)}, bf16[512,128]{1,0:T(8,128)(2,1)S(1)}, u32[]{:S(2)}, u32[]{:S(2)}) collective-permute-start(bf16[512,128]{1,0:T(8,128)(2,1)S(1)} %shard_map.101.refs_0_), channel_id=1, source_target_pairs={{0,1},{1,0},{2,3},{3,2},{4,5},{5,4},{6,7},{7,6},{8,9},{9,8},{10,11... | collective-permute-start | bytes 393224 | tf_op jit(solution)/shard_map/ppermute | solution.py:460

commit v7 on v6

--- a/solution.py
+++ b/solution.py
@@ -187,7 +187,7 @@
     ) = refs[:9]
     weights_refs = refs[9 : 8 + others]
     piece_refs = refs[8 + others : 8 + 2 * others]
-    own_grad_ref, sums_ref, last_ref, grad_ref = refs[8 + 2 * others :]
+    dz_ref, sums_ref, last_ref = refs[8 + 2 * others :]
     rows, count = last_ref.shape
     totals, weighted = add_block(message_ref, query_ref, lines_ref, table_ref, before_ref, totals_ref[0:1, :], last_ref)
     share = 1.0 / totals
@@ -199,15 +199,20 @@
     shared = (query_ref[...].astype(f32) * share).astype(bf16)
     for step, weights_ref in zip(chain, list(weights_refs) + [last_ref]):
         piece_refs[step - 1][0:rows, :] = contract(weights_ref[...], shared, (1, 1)).astype(bf16)
-    grad_ref[...] = contract(turned_ref[...], dz, (1, 1))
-    part = grad_ref.shape[0] // 2
+    part = turned_ref.shape[0] // 2
     side = lax.rem(lax.axis_index("neg"), 2)
-    own_grad_ref[...] = grad_ref[pl.ds(pl.multiple_of(side * part, part), part), :]
-    sent = grad_ref[pl.ds(pl.multiple_of((1 - side) * part, part), part), :]
-    piece_refs[0][rows : rows + part, :] = sent.astype(bf16)
-
-
-def own_block(sums_ref, lines_ref, positives_ref, weights_ref, plain_ref, own_ref, losses_ref):
+    dz_ref[...] = dz
+    other = turned_ref[pl.ds(pl.multiple_of((1 - side) * part, part), part), :]
+    piece_refs[0][rows : rows + part, :] = contract(other, dz, (1, 1)).astype(bf16)
+
+
+def own_block(
+    sums_ref, lines_ref, positives_ref, weights_ref, plain_ref, turned_ref, dz_ref, own_ref, losses_ref, own_grad_ref
+):
+    part = own_grad_ref.shape[0]
+    side = lax.rem(lax.axis_index("neg"), 2)
+    mine = turned_ref[pl.ds(pl.multiple_of(side * part, part), part), :]
+    own_grad_ref[...] = contract(mine, dz_ref[...], (1, 1))
     losses_ref[...] = jnp.log(sums_ref[0:1, :]) - lines_ref[1:2, :]
     own = lax.broadcasted_iota(jnp.int32, weights_ref.shape, 0) == positives_ref[...]
     grads = (weights_ref[...] * sums_ref[1:2, :] - own.astype(f32)).astype(bf16)
@@ -419,18 +424,18 @@
         weights.append(block_weights)
     results = call(
         functools.partial(last_block, scale, others, chain),
-        [out((rows + part, width), bf16)] + [out((rows, width), bf16)] * (others - 1) + [out((part, width)), out((8, count))],
+        [out((rows + part, width), bf16)] + [out((rows, width), bf16)] * (others - 1) + [out((width, count), bf16), out((8, count))],
         [received[chain[-1] - 1], queries, lines, table, weighted, totals, pos_items, query_unit, turned] + weights,
-        scratch=[pltpu.VMEM((rows, count), bf16), pltpu.VMEM((hidden, width), f32)],
+        scratch=[pltpu.VMEM((rows, count), bf16)],
         flops=6 * count * width * rows * (others + 1),
     )
-    own_grad, sums = results[others:]
+    query_dz, sums = results[others:]
     back = [lax.ppermute(piece, "neg", sent_back(pairs)) for piece, pairs in zip(results, exchange)]
-    own_piece, losses = call(
+    own_piece, losses, own_grad = call(
         own_block,
-        [out((rows, width)), out((1, count))],
-        [sums, lines, spots, own_weights, plain],
-        flops=2 * rows * width * count,
+        [out((rows, width)), out((1, count)), out((part, width))],
+        [sums, lines, spots, own_weights, plain, turned, query_dz],
+        flops=2 * (rows + part) * width * count,
     )
     kept = (hidden + part) // 2
     keep, send = call(

time: 41.9 us -> 41.7 us (level)
  transfers between devices with their start and end apart: 12 -> 12, of which waited for: 9 -> 9; matrix products, arithmetic and copies ran while one was open for 0% -> 0% of each run, Pallas kernels for 8% -> 9%
where the time goes in v7:
time: 41.7 us; the launch traced here: 41.6 us
  waiting for transfers between devices  18.3 us (44%)
  starting transfers between devices  15.6 us (37%)
  Pallas kernels  6.9 us (17%)
  between operations  0.72 us (2%)
    ppermute x3, starting transfers between devices, on_device(): received = [lax.ppermute(message, 'neg', pairs) for pairs in exchange]  5.75 us
    pallas_call x8, Pallas kernels, call(): pl.pallas_call(kernel, out_shape=tuple((jax.ShapeDtypeStruct(s.shape, s.d...  5.42 us
    ppermute x3, waiting for transfers between devices, on_device(): lax.ppermute(piece, 'neg', sent_back(pairs))  5.02 us
    ppermute x3, waiting for transfers between devices, on_device(): got = [lax.ppermute(half, 'neg', pairs) for pairs in exchange]  5.01 us
    ppermute x3, starting transfers between devices, on_device(): got = [lax.ppermute(half, 'neg', pairs) for pairs in exchange]  4.45 us
    ppermute x3, starting transfers between devices, on_device(): lax.ppermute(piece, 'neg', sent_back(pairs))  3.67 us
    ppermute x1, waiting for transfers between devices, sum_over(): lax.ppermute(values, axis, pairs).astype(f32)  3.35 us
    ppermute x3, waiting for transfers between devices, on_device(): received = [lax.ppermute(message, 'neg', pairs) for pairs in exchange]  3.05 us
  transfers between devices with their start and end apart: 12, of which 9 were waited for; matrix products, arithmetic and copies ran while one was open for 0% of the time, Pallas kernels for 9%

profile of v7, /device:TPU:0, one launch (start us, length us, event | category | flops | bytes accessed | tf_op | source)
XLA Modules:
  0.0 41.6 jit_solution(15257052017477670530)
XLA Ops:
  0.6 1.4 %shard_map.94 = (bf16[272,128]{1,0:T(8,128)(2,1)S(1)}, f32[256,128]{1,0:T(8,128)S(1)}, f32[256,128]{1,0:T(8,128)S(1)}, bf16[512,512]{1,0:T(8,128)(2,1)S(1)}, bf1...) custom-call(bf16[512,512]{1,0:T(8,128)(2,1)} %refs_0_.1, bf16[512,128]{1,0:T(8,128)(2,1)} %refs_1_.1, ...), custom_call_target="tpu_custom_call" | custom-call | flops 33554432 | bytes 2304000 | tf_op jit(solution)/shard_map/pallas_call | solution.py:302
  2.0 5.1 %collective-permute-start.2 = (bf16[272,128]{1,0:T(8,128)(2,1)S(1)}, bf16[272,128]{1,0:T(8,128)(2,1)S(1)}, u32[]{:S(2)}, u32[]{:S(2)}) collective-permute-start(bf16[272,128]{1,0:T(8,128)(2,1)S(1)} %get-tuple-element.40.message_ref), channel_id=1, source_target_pairs={{0,12},{4,8},{8,4},{12,0},{1,13},{5,9},{9,5},{13,1},{2,14},{6,10},... | collective-permute-start | bytes 208904 | tf_op jit(solution)/shard_map/ppermute | solution.py:395
  7.1 0.0 collective-permute-start.1
  7.1 0.6 %collective-permute-start = (bf16[272,128]{1,0:T(8,128)(2,1)S(1)}, bf16[272,128]{1,0:T(8,128)(2,1)S(1)}, u32[]{:S(2)}, u32[]{:S(2)}) collective-permute-start(bf16[272,128]{1,0:T(8,128)(2,1)S(1)} %get-tuple-element.40.message_ref), channel_id=1, source_target_pairs={{0,8},{4,12},{8,0},{12,4},{1,9},{5,13},{9,1},{13,5},{2,10},{6,14},... | collective-permute-start | bytes 208904 | tf_op jit(solution)/shard_map/ppermute | solution.py:395
  7.8 0.9 %shard_map.95 = (f32[128,512]{1,0:T(8,128)S(1)}, bf16[128,512]{1,0:T(8,128)(2,1)S(1)}, bf16[512,128]{1,0:T(8,128)(2,1)S(1)}, f32[256,512]{1,0:T(8,128)S(1)}, f32...) custom-call(bf16[512,512]{1,0:T(8,128)(2,1)S(1)} %get-tuple-element., ...), custom_call_target="tpu_custom_call" | custom-call | flops 167772160 | bytes 3381248 | tf_op jit(solution)/shard_map/pallas_call | solution.py:302
  8.7 1.5 %collective-permute-done.2.message_ref = bf16[272,128]{1,0:T(8,128)(2,1)S(1)} collective-permute-done((bf16[272,128]{1,0:T(8,128)(2,1)S(1)}, bf16[272,128]{1,0:T(8,128)(2,1)S(1)}, u32[]{:S(2)}, u32[]{:S(2)}) %collective-permute-start.2) | collective-permute-done | bytes 69664 | tf_op jit(solution)/shard_map/ppermute | solution.py:395
  10.1 0.5 %shard_map.96 = (bf16[256,512]{1,0:T(8,128)(2,1)S(1)}, f32[128,512]{1,0:T(8,128)S(1)}, f32[8,512]{1,0:T(8,128)S(1)}) custom-call(bf16[272,128]{1,0:T(8,128)(2,1)S(1)} %collective-permute-done.2.message_ref, bf16[128,512]{1,0:T(8,128)(2,1)S(1)} %get-tuple-element.45.query_ref.refs_1_, f32[8,512]{1,0:T(8,128)S(1)} %get-tuple-element.46.lines_ref.totals_ref.refs_2_, ...), custom_call_target="tpu_custom_call" | custom-call | flops 67108864 | bytes 1052672 | tf_op jit(solution)/shard_map/pallas_call | solution.py:302
  10.7 1.3 %collective-permute-done.1.message_ref = bf16[272,128]{1,0:T(8,128)(2,1)S(1)} collective-permute-done((bf16[272,128]{1,0:T(8,128)(2,1)S(1)}, bf16[272,128]{1,0:T(8,128)(2,1)S(1)}, u32[]{:S(2)}, u32[]{:S(2)}) %collective-permute-start.1) | collective-permute-done | bytes 69664 | tf_op jit(solution)/shard_map/ppermute | solution.py:395
  12.0 0.5 %shard_map.97 = (bf16[256,512]{1,0:T(8,128)(2,1)S(1)}, f32[128,512]{1,0:T(8,128)S(1)}, f32[8,512]{1,0:T(8,128)S(1)}) custom-call(bf16[272,128]{1,0:T(8,128)(2,1)S(1)} %collective-permute-done.1.message_ref, bf16[128,512]{1,0:T(8,128)(2,1)S(1)} %get-tuple-element.45.query_ref.refs_1_, f32[8,512]{1,0:T(8,128)S(1)} %get-tuple-element.46.lines_ref.totals_ref.refs_2_, ...), custom_call_target="tpu_custom_call" | custom-call | flops 67108864 | bytes 1052672 | tf_op jit(solution)/shard_map/pallas_call | solution.py:302
  12.5 0.3 collective-permute-done.refs_0_
  12.8 0.9 %shard_map.98 = (bf16[512,128]{1,0:T(8,128)(2,1)S(1)}, bf16[256,128]{1,0:T(8,128)(2,1)S(1)}, bf16[256,128]{1,0:T(8,128)(2,1)S(1)}, bf16[128,512]{1,0:T(8,128)(2,1)S(1)}, f32[8,512]{1,0:T(8,128)S(1)}) custom-call(bf16[272,128]{1,0:T(8,128)(2,1)S(1)} %collective-permute-done.refs_0_, bf16[128,512]{1,0:T(8,128)(2,1)S(1)} %get-tuple-element.45.query_ref.refs_1_, ...), custom_call_target="tpu_custom_call" | custom-call | flops 402653184 | bytes 2494464 | tf_op jit(solution)/shard_map/pallas_call | solution.py:302
  13.7 1.6 %collective-permute-start.3 = (bf16[512,128]{1,0:T(8,128)(2,1)S(1)}, bf16[512,128]{1,0:T(8,128)(2,1)S(1)}, u32[]{:S(2)}, u32[]{:S(2)}) collective-permute-start(bf16[512,128]{1,0:T(8,128)(2,1)S(1)} %get-tuple-element.67), channel_id=1, source_target_pairs={{4,0},{0,4},{12,8},{8,12},{5,1},{1,5},{13,9},{9,13},{6,2},{2,6},{1... | collective-permute-start | bytes 393224 | tf_op jit(solution)/shard_map/ppermute | solution.py:433
  15.3 2.0 %collective-permute-start.4 = (bf16[256,128]{1,0:T(8,128)(2,1)S(1)}, bf16[256,128]{1,0:T(8,128)(2,1)S(1)}, u32[]{:S(2)}, u32[]{:S(2)}) collective-permute-start(bf16[256,128]{1,0:T(8,128)(2,1)S(1)} %get-tuple-element.68), channel_id=1, source_target_pairs={{12,0},{8,4},{4,8},{0,12},{13,1},{9,5},{5,9},{1,13},{14,2},{10,6},... | collective-permute-start | bytes 196616 | tf_op jit(solution)/shard_map/ppermute | solution.py:433
  17.4 0.1 collective-permute-start.5
  17.4 0.8 %shard_map.99 = (f32[256,128]{1,0:T(8,128)S(1)}, f32[1,512]{1,0:T(1,128)}, f32[256,128]{1,0:T(8,128)S(1)}) custom-call(f32[8,512]{1,0:T(8,128)S(1)} %get-tuple-element.58.sums_ref, f32[8,512]{1,0:T(8,128)S(1)} %get-tuple-element.46.lines_ref.totals_ref.refs_2_, s32[1,512]{1,0:T(1,128)S(1)} %get-tuple-element.43.positives_ref, ...), custom_call_target="tpu_custom_call" | custom-call | flops 67108864 | bytes 1609728 | tf_op jit(solution)/shard_map/pallas_call | solution.py:302
  18.2 3.4 %collective-permute-done.4.refs_1_ = bf16[256,128]{1,0:T(8,128)(2,1)S(1)} collective-permute-done((bf16[256,128]{1,0:T(8,128)(2,1)S(1)}, bf16[256,128]{1,0:T(8,128)(2,1)S(1)}, u32[]{:S(2)}, u32[]{:S(2)}) %collective-permute-start.4) | collective-permute-done | bytes 65568 | tf_op jit(solution)/shard_map/ppermute | solution.py:433
  21.6 1.6 %collective-permute-done.5.refs_2_ = bf16[256,128]{1,0:T(8,128)(2,1)S(1)} collective-permute-done((bf16[256,128]{1,0:T(8,128)(2,1)S(1)}, bf16[256,128]{1,0:T(8,128)(2,1)S(1)}, u32[]{:S(2)}, u32[]{:S(2)}) %collective-permute-start.5) | collective-permute-done | bytes 65568 | tf_op jit(solution)/shard_map/ppermute | solution.py:433
  23.2 0.0 collective-permute-done.3.refs_0_
  23.2 0.3 shard_map.100
  23.5 0.1 collective-permute-start.6
  23.6 1.3 %collective-permute-done.6 = bf16[384,128]{1,0:T(8,128)(2,1)S(1)} collective-permute-done((bf16[384,128]{1,0:T(8,128)(2,1)S(1)}, bf16[384,128]{1,0:T(8,128)(2,1)S(1)}, u32[]{:S(2)}, u32[]{:S(2)}) %collective-permute-start.6) | collective-permute-done | bytes 98336 | tf_op jit(solution)/shard_map/ppermute | solution.py:448
  24.9 1.6 %collective-permute-start.7 = (bf16[384,128]{1,0:T(8,128)(2,1)S(1)}, bf16[384,128]{1,0:T(8,128)(2,1)S(1)}, u32[]{:S(2)}, u32[]{:S(2)}) collective-permute-start(bf16[384,128]{1,0:T(8,128)(2,1)S(1)} %add_convert_fusion.1), channel_id=1, source_target_pairs={{0,2},{2,0},{1,3},{3,1},{4,6},{6,4},{5,7},{7,5},{8,10},{10,8},{9,1... | collective-permute-start | bytes 294920 | tf_op jit(solution)/shard_map/ppermute | solution.py:350
  26.5 3.4 %collective-permute-done.7 = bf16[384,128]{1,0:T(8,128)(2,1)S(1)} collective-permute-done((bf16[384,128]{1,0:T(8,128)(2,1)S(1)}, bf16[384,128]{1,0:T(8,128)(2,1)S(1)}, u32[]{:S(2)}, u32[]{:S(2)}) %collective-permute-start.7) | collective-permute-done | bytes 98336 | tf_op jit(solution)/shard_map/ppermute | solution.py:350
  29.9 0.4 collective-permute-start.10
  30.3 2.1 %collective-permute-start.8 = (bf16[384,128]{1,0:T(8,128)(2,1)S(1)}, bf16[384,128]{1,0:T(8,128)(2,1)S(1)}, u32[]{:S(2)}, u32[]{:S(2)}) collective-permute-start(bf16[384,128]{1,0:T(8,128)(2,1)S(1)} %add_convert_fusion.own_ref), channel_id=1, source_target_pairs={{0,4},{4,0},{8,12},{12,8},{1,5},{5,1},{9,13},{13,9},{2,6},{6,2},{1... | collective-permute-start | bytes 294920 | tf_op jit(solution)/shard_map/ppermute | solution.py:452
  32.3 2.0 %collective-permute-start.9 = (bf16[384,128]{1,0:T(8,128)(2,1)S(1)}, bf16[384,128]{1,0:T(8,128)(2,1)S(1)}, u32[]{:S(2)}, u32[]{:S(2)}) collective-permute-start(bf16[384,128]{1,0:T(8,128)(2,1)S(1)} %add_convert_fusion.own_ref), channel_id=1, source_target_pairs={{0,12},{4,8},{8,4},{12,0},{1,13},{5,9},{9,5},{13,1},{2,14},{6,10},... | collective-permute-start | bytes 294920 | tf_op jit(solution)/shard_map/ppermute | solution.py:452
  34.3 5.0 %collective-permute-done.10.refs_2_ = bf16[384,128]{1,0:T(8,128)(2,1)S(1)} collective-permute-done((bf16[384,128]{1,0:T(8,128)(2,1)S(1)}, bf16[384,128]{1,0:T(8,128)(2,1)S(1)}, u32[]{:S(2)}, u32[]{:S(2)}) %collective-permute-start.10) | collective-permute-done | bytes 98336 | tf_op jit(solution)/shard_map/ppermute | solution.py:452
  39.3 0.0 collective-permute-done.8.refs_0_
  39.4 0.0 collective-permute-done.9.refs_1_
  39.4 0.1 shard_map.101.refs_0_
  39.4 0.1 collective-permute-start.11
  39.5 0.7 %shard_map.102 = (f32[512,128]{1,0:T(8,128)}, f32[512,128]{1,0:T(8,128)}) custom-call(bf16[512,128]{1,0:T(8,128)(2,1)S(1)} %shard_map.101.refs_0_), custom_call_target="tpu_custom_call" | custom-call | bytes 393216 | tf_op jit(solution)/shard_map/pallas_call | solution.py:287
  40.2 0.6 %collective-permute-done.11.refs_0_ = bf16[512,128]{1,0:T(8,128)(2,1)S(1)} collective-permute-done((bf16[512,128]{1,0:T(8,128)(2,1)S(1)}, bf16[512,128]{1,0:T(8,128)(2,1)S(1)}, u32[]{:S(2)}, u32[]{:S(2)}) %collective-permute-start.11) | collective-permute-done | bytes 131104 | tf_op jit(solution)/shard_map/ppermute | solution.py:465
  40.8 0.7 %shard_map.103 = (f32[512,128]{1,0:T(8,128)}, f32[512,128]{1,0:T(8,128)}) custom-call(bf16[512,128]{1,0:T(8,128)(2,1)S(1)} %collective-permute-done.11.refs_0_, f32[512,128]{1,0:T(8,128)} %get-tuple-element.72.refs_1_, f32[512,128]{1,0:T(8,128)} %get-tuple-element.73.refs_2_), custom_call_target="tpu_custom_call", output_to_operand_aliasing={{0}: (1, {}), {1}: (2, {})} | custom-call | bytes 393216 | tf_op jit(solution)/shard_map/pallas_call | solution.py:287
  (2 shorter events, 0.1 us)
Async XLA Ops:
  2.0 8.1 %collective-permute-start.2 = (bf16[272,128]{1,0:T(8,128)(2,1)S(1)}, bf16[272,128]{1,0:T(8,128)(2,1)S(1)}, u32[]{:S(2)}, u32[]{:S(2)}) collective-permute-start(bf16[272,128]{1,0:T(8,128)(2,1)S(1)} %get-tuple-element.40.message_ref), channel_id=1, source_target_pairs={{0,12},{4,8},{8,4},{12,0},{1,13},{5,9},{9,5},{13,1},{2,14},{6,10},... | collective-permute-start | bytes 208904 | tf_op jit(solution)/shard_map/ppermute | solution.py:395
  7.1 4.9 %collective-permute-start.1 = (bf16[272,128]{1,0:T(8,128)(2,1)S(1)}, bf16[272,128]{1,0:T(8,128)(2,1)S(1)}, u32[]{:S(2)}, u32[]{:S(2)}) collective-permute-start(bf16[272,128]{1,0:T(8,128)(2,1)S(1)} %get-tuple-element.40.message_ref), channel_id=1, source_target_pairs={{0,4},{4,0},{8,12},{12,8},{1,5},{5,1},{9,13},{13,9},{2,6},{6,2},{1... | collective-permute-start | bytes 208904 | tf_op jit(solution)/shard_map/ppermute | solution.py:395
  7.1 5.7 %collective-permute-start = (bf16[272,128]{1,0:T(8,128)(2,1)S(1)}, bf16[272,128]{1,0:T(8,128)(2,1)S(1)}, u32[]{:S(2)}, u32[]{:S(2)}) collective-permute-start(bf16[272,128]{1,0:T(8,128)(2,1)S(1)} %get-tuple-element.40.message_ref), channel_id=1, source_target_pairs={{0,8},{4,12},{8,0},{12,4},{1,9},{5,13},{9,1},{13,5},{2,10},{6,14},... | collective-permute-start | bytes 208904 | tf_op jit(solution)/shard_map/ppermute | solution.py:395
  13.7 9.5 %collective-permute-start.3 = (bf16[512,128]{1,0:T(8,128)(2,1)S(1)}, bf16[512,128]{1,0:T(8,128)(2,1)S(1)}, u32[]{:S(2)}, u32[]{:S(2)}) collective-permute-start(bf16[512,128]{1,0:T(8,128)(2,1)S(1)} %get-tuple-element.67), channel_id=1, source_target_pairs={{4,0},{0,4},{12,8},{8,12},{5,1},{1,5},{13,9},{9,13},{6,2},{2,6},{1... | collective-permute-start | bytes 393224 | tf_op jit(solution)/shard_map/ppermute | solution.py:433
  15.3 6.3 %collective-permute-start.4 = (bf16[256,128]{1,0:T(8,128)(2,1)S(1)}, bf16[256,128]{1,0:T(8,128)(2,1)S(1)}, u32[]{:S(2)}, u32[]{:S(2)}) collective-permute-start(bf16[256,128]{1,0:T(8,128)(2,1)S(1)} %get-tuple-element.68), channel_id=1, source_target_pairs={{12,0},{8,4},{4,8},{0,12},{13,1},{9,5},{5,9},{1,13},{14,2},{10,6},... | collective-permute-start | bytes 196616 | tf_op jit(solution)/shard_map/ppermute | solution.py:433
  17.4 5.9 %collective-permute-start.5 = (bf16[256,128]{1,0:T(8,128)(2,1)S(1)}, bf16[256,128]{1,0:T(8,128)(2,1)S(1)}, u32[]{:S(2)}, u32[]{:S(2)}) collective-permute-start(bf16[256,128]{1,0:T(8,128)(2,1)S(1)} %get-tuple-element.69), channel_id=1, source_target_pairs={{8,0},{12,4},{0,8},{4,12},{9,1},{13,5},{1,9},{5,13},{10,2},{14,6},... | collective-permute-start | bytes 196616 | tf_op jit(solution)/shard_map/ppermute | solution.py:433
  23.5 1.4 %collective-permute-start.6 = (bf16[384,128]{1,0:T(8,128)(2,1)S(1)}, bf16[384,128]{1,0:T(8,128)(2,1)S(1)}, u32[]{:S(2)}, u32[]{:S(2)}) collective-permute-start(bf16[384,128]{1,0:T(8,128)(2,1)S(1)} %get-tuple-element.71), channel_id=1, source_target_pairs={{0,1},{1,0},{2,3},{3,2},{4,5},{5,4},{6,7},{7,6},{8,9},{9,8},{10,11... | collective-permute-start | bytes 294920 | tf_op jit(solution)/shard_map/ppermute | solution.py:448
  24.9 4.9 %collective-permute-start.7 = (bf16[384,128]{1,0:T(8,128)(2,1)S(1)}, bf16[384,128]{1,0:T(8,128)(2,1)S(1)}, u32[]{:S(2)}, u32[]{:S(2)}) collective-permute-start(bf16[384,128]{1,0:T(8,128)(2,1)S(1)} %add_convert_fusion.1), channel_id=1, source_target_pairs={{0,2},{2,0},{1,3},{3,1},{4,6},{6,4},{5,7},{7,5},{8,10},{10,8},{9,1... | collective-permute-start | bytes 294920 | tf_op jit(solution)/shard_map/ppermute | solution.py:350
  29.9 9.5 %collective-permute-start.10 = (bf16[384,128]{1,0:T(8,128)(2,1)S(1)}, bf16[384,128]{1,0:T(8,128)(2,1)S(1)}, u32[]{:S(2)}, u32[]{:S(2)}) collective-permute-start(bf16[384,128]{1,0:T(8,128)(2,1)S(1)} %add_convert_fusion.own_ref), channel_id=1, source_target_pairs={{0,8},{4,12},{8,0},{12,4},{1,9},{5,13},{9,1},{13,5},{2,10},{6,14},... | collective-permute-start | bytes 294920 | tf_op jit(solution)/shard_map/ppermute | solution.py:452
  30.3 9.1 %collective-permute-start.8 = (bf16[384,128]{1,0:T(8,128)(2,1)S(1)}, bf16[384,128]{1,0:T(8,128)(2,1)S(1)}, u32[]{:S(2)}, u32[]{:S(2)}) collective-permute-start(bf16[384,128]{1,0:T(8,128)(2,1)S(1)} %add_convert_fusion.own_ref), channel_id=1, source_target_pairs={{0,4},{4,0},{8,12},{12,8},{1,5},{5,1},{9,13},{13,9},{2,6},{6,2},{1... | collective-permute-start | bytes 294920 | tf_op jit(solution)/shard_map/ppermute | solution.py:452
  32.3 7.0 %collective-permute-start.9 = (bf16[384,128]{1,0:T(8,128)(2,1)S(1)}, bf16[384,128]{1,0:T(8,128)(2,1)S(1)}, u32[]{:S(2)}, u32[]{:S(2)}) collective-permute-start(bf16[384,128]{1,0:T(8,128)(2,1)S(1)} %add_convert_fusion.own_ref), channel_id=1, source_target_pairs={{0,12},{4,8},{8,4},{12,0},{1,13},{5,9},{9,5},{13,1},{2,14},{6,10},... | collective-permute-start | bytes 294920 | tf_op jit(solution)/shard_map/ppermute | solution.py:452
  39.4 1.4 %collective-permute-start.11 = (bf16[512,128]{1,0:T(8,128)(2,1)S(1)}, bf16[512,128]{1,0:T(8,128)(2,1)S(1)}, u32[]{:S(2)}, u32[]{:S(2)}) collective-permute-start(bf16[512,128]{1,0:T(8,128)(2,1)S(1)} %shard_map.101.refs_0_), channel_id=1, source_target_pairs={{0,1},{1,0},{2,3},{3,2},{4,5},{5,4},{6,7},{7,6},{8,9},{9,8},{10,11... | collective-permute-start | bytes 393224 | tf_op jit(solution)/shard_map/ppermute | solution.py:465

commit v8 on v7

--- a/solution.py
+++ b/solution.py
@@ -441,7 +441,7 @@
     keep, send = call(
         functools.partial(item_gradient, scale, others),
         [out((kept, width)), out((kept, width), bf16)],
-        [own_piece, own_grad, item_unit, item_inverse, item_turned] + [back[step - 1] for step in ordered(others, (1, 3, 2))],
+        [own_piece, own_grad, item_unit, item_inverse, item_turned] + [back[step - 1] for step in ordered(others, (1, 2, 3))],
         flops=2 * rows * width * hidden,
     )
     swap = [(0, 1), (1, 0)]
@@ -450,7 +450,7 @@
     if direct:
         half = half.astype(bf16)
         got = [lax.ppermute(half, "neg", pairs) for pairs in exchange]
-        turns = ordered(others, (1, 3, 2))
+        turns = ordered(others, (1, 2, 3))
         mine = call(
             functools.partial(add_pieces, turns, hidden // 2),
             [out((hidden, width), bf16)],

time: 41.7 us -> 41.6 us (level)
  waiting for transfers between devices: 18.3 us -> 17.4 us
  starting transfers between devices: 15.6 us -> 16.4 us
    ppermute x3, starting transfers between devices: 3.67 us -> 4.45 us  [on_device(): lax.ppermute(piece, 'neg', sent_back(pairs))]
    ppermute x3, waiting for transfers between devices: 5.02 us -> 4.48 us  [on_device(): lax.ppermute(piece, 'neg', sent_back(pairs))]
  transfers between devices with their start and end apart: 12 -> 12, of which waited for: 9 -> 11; matrix products, arithmetic and copies ran while one was open for 0% -> 0% of each run, Pallas kernels for 9% -> 9%
where the time goes in v8:
time: 41.6 us; the launch traced here: 41.4 us
  waiting for transfers between devices  17.4 us (42%)
  starting transfers between devices  16.4 us (39%)
  Pallas kernels  6.91 us (17%)
  between operations  0.72 us (2%)
    ppermute x3, starting transfers between devices, on_device(): received = [lax.ppermute(message, 'neg', pairs) for pairs in exchange]  5.75 us
    pallas_call x8, Pallas kernels, call(): pl.pallas_call(kernel, out_shape=tuple((jax.ShapeDtypeStruct(s.shape, s.d...  5.44 us
    ppermute x3, waiting for transfers between devices, on_device(): got = [lax.ppermute(half, 'neg', pairs) for pairs in exchange]  4.64 us
    ppermute x3, waiting for transfers between devices, on_device(): lax.ppermute(piece, 'neg', sent_back(pairs))  4.48 us
    ppermute x3, starting transfers between devices, on_device(): got = [lax.ppermute(half, 'neg', pairs) for pairs in exchange]  4.45 us
    ppermute x3, starting transfers between devices, on_device(): lax.ppermute(piece, 'neg', sent_back(pairs))  4.45 us
    ppermute x1, waiting for transfers between devices, sum_over(): lax.ppermute(values, axis, pairs).astype(f32)  3.36 us
    ppermute x3, waiting for transfers between devices, on_device(): received = [lax.ppermute(message, 'neg', pairs) for pairs in exchange]  3.05 us
  transfers between devices with their start and end apart: 12, of which 11 were waited for; matrix products, arithmetic and copies ran while one was open for 0% of the time, Pallas kernels for 9%

profile of v8, /device:TPU:0, one launch (start us, length us, event | category | flops | bytes accessed | tf_op | source)
XLA Modules:
  0.0 41.4 jit_solution(7286021714429202631)
XLA Ops:
  0.6 1.4 %shard_map.94 = (bf16[272,128]{1,0:T(8,128)(2,1)S(1)}, f32[256,128]{1,0:T(8,128)S(1)}, f32[256,128]{1,0:T(8,128)S(1)}, bf16[512,512]{1,0:T(8,128)(2,1)S(1)}, bf1...) custom-call(bf16[512,512]{1,0:T(8,128)(2,1)} %refs_0_.1, bf16[512,128]{1,0:T(8,128)(2,1)} %refs_1_.1, ...), custom_call_target="tpu_custom_call" | custom-call | flops 33554432 | bytes 2304000 | tf_op jit(solution)/shard_map/pallas_call | solution.py:302
  2.0 5.1 %collective-permute-start.2 = (bf16[272,128]{1,0:T(8,128)(2,1)S(1)}, bf16[272,128]{1,0:T(8,128)(2,1)S(1)}, u32[]{:S(2)}, u32[]{:S(2)}) collective-permute-start(bf16[272,128]{1,0:T(8,128)(2,1)S(1)} %get-tuple-element.40.message_ref), channel_id=1, source_target_pairs={{0,12},{4,8},{8,4},{12,0},{1,13},{5,9},{9,5},{13,1},{2,14},{6,10},... | collective-permute-start | bytes 208904 | tf_op jit(solution)/shard_map/ppermute | solution.py:395
  7.1 0.0 collective-permute-start.1
  7.1 0.6 %collective-permute-start = (bf16[272,128]{1,0:T(8,128)(2,1)S(1)}, bf16[272,128]{1,0:T(8,128)(2,1)S(1)}, u32[]{:S(2)}, u32[]{:S(2)}) collective-permute-start(bf16[272,128]{1,0:T(8,128)(2,1)S(1)} %get-tuple-element.40.message_ref), channel_id=1, source_target_pairs={{0,8},{4,12},{8,0},{12,4},{1,9},{5,13},{9,1},{13,5},{2,10},{6,14},... | collective-permute-start | bytes 208904 | tf_op jit(solution)/shard_map/ppermute | solution.py:395
  7.8 0.9 %shard_map.95 = (f32[128,512]{1,0:T(8,128)S(1)}, bf16[128,512]{1,0:T(8,128)(2,1)S(1)}, bf16[512,128]{1,0:T(8,128)(2,1)S(1)}, f32[256,512]{1,0:T(8,128)S(1)}, f32...) custom-call(bf16[512,512]{1,0:T(8,128)(2,1)S(1)} %get-tuple-element., ...), custom_call_target="tpu_custom_call" | custom-call | flops 167772160 | bytes 3381248 | tf_op jit(solution)/shard_map/pallas_call | solution.py:302
  8.7 1.5 %collective-permute-done.2.message_ref = bf16[272,128]{1,0:T(8,128)(2,1)S(1)} collective-permute-done((bf16[272,128]{1,0:T(8,128)(2,1)S(1)}, bf16[272,128]{1,0:T(8,128)(2,1)S(1)}, u32[]{:S(2)}, u32[]{:S(2)}) %collective-permute-start.2) | collective-permute-done | bytes 69664 | tf_op jit(solution)/shard_map/ppermute | solution.py:395
  10.1 0.5 %shard_map.96 = (bf16[256,512]{1,0:T(8,128)(2,1)S(1)}, f32[128,512]{1,0:T(8,128)S(1)}, f32[8,512]{1,0:T(8,128)S(1)}) custom-call(bf16[272,128]{1,0:T(8,128)(2,1)S(1)} %collective-permute-done.2.message_ref, bf16[128,512]{1,0:T(8,128)(2,1)S(1)} %get-tuple-element.45.query_ref.refs_1_, f32[8,512]{1,0:T(8,128)S(1)} %get-tuple-element.46.lines_ref.totals_ref.refs_2_, ...), custom_call_target="tpu_custom_call" | custom-call | flops 67108864 | bytes 1052672 | tf_op jit(solution)/shard_map/pallas_call | solution.py:302
  10.7 1.3 %collective-permute-done.1.message_ref = bf16[272,128]{1,0:T(8,128)(2,1)S(1)} collective-permute-done((bf16[272,128]{1,0:T(8,128)(2,1)S(1)}, bf16[272,128]{1,0:T(8,128)(2,1)S(1)}, u32[]{:S(2)}, u32[]{:S(2)}) %collective-permute-start.1) | collective-permute-done | bytes 69664 | tf_op jit(solution)/shard_map/ppermute | solution.py:395
  12.0 0.5 %shard_map.97 = (bf16[256,512]{1,0:T(8,128)(2,1)S(1)}, f32[128,512]{1,0:T(8,128)S(1)}, f32[8,512]{1,0:T(8,128)S(1)}) custom-call(bf16[272,128]{1,0:T(8,128)(2,1)S(1)} %collective-permute-done.1.message_ref, bf16[128,512]{1,0:T(8,128)(2,1)S(1)} %get-tuple-element.45.query_ref.refs_1_, f32[8,512]{1,0:T(8,128)S(1)} %get-tuple-element.46.lines_ref.totals_ref.refs_2_, ...), custom_call_target="tpu_custom_call" | custom-call | flops 67108864 | bytes 1052672 | tf_op jit(solution)/shard_map/pallas_call | solution.py:302
  12.5 0.3 collective-permute-done.refs_0_
  12.8 0.9 %shard_map.98 = (bf16[512,128]{1,0:T(8,128)(2,1)S(1)}, bf16[256,128]{1,0:T(8,128)(2,1)S(1)}, bf16[256,128]{1,0:T(8,128)(2,1)S(1)}, bf16[128,512]{1,0:T(8,128)(2,1)S(1)}, f32[8,512]{1,0:T(8,128)S(1)}) custom-call(bf16[272,128]{1,0:T(8,128)(2,1)S(1)} %collective-permute-done.refs_0_, bf16[128,512]{1,0:T(8,128)(2,1)S(1)} %get-tuple-element.45.query_ref.refs_1_, ...), custom_call_target="tpu_custom_call" | custom-call | flops 402653184 | bytes 2494464 | tf_op jit(solution)/shard_map/pallas_call | solution.py:302
  13.7 1.6 %collective-permute-start.3 = (bf16[512,128]{1,0:T(8,128)(2,1)S(1)}, bf16[512,128]{1,0:T(8,128)(2,1)S(1)}, u32[]{:S(2)}, u32[]{:S(2)}) collective-permute-start(bf16[512,128]{1,0:T(8,128)(2,1)S(1)} %get-tuple-element.67), channel_id=1, source_target_pairs={{4,0},{0,4},{12,8},{8,12},{5,1},{1,5},{13,9},{9,13},{6,2},{2,6},{1... | collective-permute-start | bytes 393224 | tf_op jit(solution)/shard_map/ppermute | solution.py:433
  15.3 2.1 %collective-permute-start.4 = (bf16[256,128]{1,0:T(8,128)(2,1)S(1)}, bf16[256,128]{1,0:T(8,128)(2,1)S(1)}, u32[]{:S(2)}, u32[]{:S(2)}) collective-permute-start(bf16[256,128]{1,0:T(8,128)(2,1)S(1)} %get-tuple-element.68), channel_id=1, source_target_pairs={{8,0},{12,4},{0,8},{4,12},{9,1},{13,5},{1,9},{5,13},{10,2},{14,6},... | collective-permute-start | bytes 196616 | tf_op jit(solution)/shard_map/ppermute | solution.py:433
  17.4 0.8 %collective-permute-start.5 = (bf16[256,128]{1,0:T(8,128)(2,1)S(1)}, bf16[256,128]{1,0:T(8,128)(2,1)S(1)}, u32[]{:S(2)}, u32[]{:S(2)}) collective-permute-start(bf16[256,128]{1,0:T(8,128)(2,1)S(1)} %get-tuple-element.69), channel_id=1, source_target_pairs={{12,0},{8,4},{4,8},{0,12},{13,1},{9,5},{5,9},{1,13},{14,2},{10,6},... | collective-permute-start | bytes 196616 | tf_op jit(solution)/shard_map/ppermute | solution.py:433
  18.2 0.8 %shard_map.99 = (f32[256,128]{1,0:T(8,128)S(1)}, f32[1,512]{1,0:T(1,128)}, f32[256,128]{1,0:T(8,128)S(1)}) custom-call(f32[8,512]{1,0:T(8,128)S(1)} %get-tuple-element.58.sums_ref, f32[8,512]{1,0:T(8,128)S(1)} %get-tuple-element.46.lines_ref.totals_ref.refs_2_, s32[1,512]{1,0:T(1,128)S(1)} %get-tuple-element.43.positives_ref, ...), custom_call_target="tpu_custom_call" | custom-call | flops 67108864 | bytes 1609728 | tf_op jit(solution)/shard_map/pallas_call | solution.py:302
  19.0 2.8 %collective-permute-done.4.refs_1_ = bf16[256,128]{1,0:T(8,128)(2,1)S(1)} collective-permute-done((bf16[256,128]{1,0:T(8,128)(2,1)S(1)}, bf16[256,128]{1,0:T(8,128)(2,1)S(1)}, u32[]{:S(2)}, u32[]{:S(2)}) %collective-permute-start.4) | collective-permute-done | bytes 65568 | tf_op jit(solution)/shard_map/ppermute | solution.py:433
  21.8 1.7 %collective-permute-done.5.refs_2_ = bf16[256,128]{1,0:T(8,128)(2,1)S(1)} collective-permute-done((bf16[256,128]{1,0:T(8,128)(2,1)S(1)}, bf16[256,128]{1,0:T(8,128)(2,1)S(1)}, u32[]{:S(2)}, u32[]{:S(2)}) %collective-permute-start.5) | collective-permute-done | bytes 65568 | tf_op jit(solution)/shard_map/ppermute | solution.py:433
  23.5 0.0 collective-permute-done.3.refs_0_
  23.5 0.3 shard_map.100
  23.8 0.1 collective-permute-start.6
  23.9 1.3 %collective-permute-done.6 = bf16[384,128]{1,0:T(8,128)(2,1)S(1)} collective-permute-done((bf16[384,128]{1,0:T(8,128)(2,1)S(1)}, bf16[384,128]{1,0:T(8,128)(2,1)S(1)}, u32[]{:S(2)}, u32[]{:S(2)}) %collective-permute-start.6) | collective-permute-done | bytes 98336 | tf_op jit(solution)/shard_map/ppermute | solution.py:448
  25.2 1.6 %collective-permute-start.7 = (bf16[384,128]{1,0:T(8,128)(2,1)S(1)}, bf16[384,128]{1,0:T(8,128)(2,1)S(1)}, u32[]{:S(2)}, u32[]{:S(2)}) collective-permute-start(bf16[384,128]{1,0:T(8,128)(2,1)S(1)} %add_convert_fusion.1), channel_id=1, source_target_pairs={{0,2},{2,0},{1,3},{3,1},{4,6},{6,4},{5,7},{7,5},{8,10},{10,8},{9,1... | collective-permute-start | bytes 294920 | tf_op jit(solution)/shard_map/ppermute | solution.py:350
  26.7 3.4 %collective-permute-done.7 = bf16[384,128]{1,0:T(8,128)(2,1)S(1)} collective-permute-done((bf16[384,128]{1,0:T(8,128)(2,1)S(1)}, bf16[384,128]{1,0:T(8,128)(2,1)S(1)}, u32[]{:S(2)}, u32[]{:S(2)}) %collective-permute-start.7) | collective-permute-done | bytes 98336 | tf_op jit(solution)/shard_map/ppermute | solution.py:350
  30.1 0.9 %collective-permute-start.10 = (bf16[384,128]{1,0:T(8,128)(2,1)S(1)}, bf16[384,128]{1,0:T(8,128)(2,1)S(1)}, u32[]{:S(2)}, u32[]{:S(2)}) collective-permute-start(bf16[384,128]{1,0:T(8,128)(2,1)S(1)} %add_convert_fusion.own_ref), channel_id=1, source_target_pairs={{0,12},{4,8},{8,4},{12,0},{1,13},{5,9},{9,5},{13,1},{2,14},{6,10},... | collective-permute-start | bytes 294920 | tf_op jit(solution)/shard_map/ppermute | solution.py:452
  31.0 0.4 collective-permute-start.8
  31.4 3.2 %collective-permute-start.9 = (bf16[384,128]{1,0:T(8,128)(2,1)S(1)}, bf16[384,128]{1,0:T(8,128)(2,1)S(1)}, u32[]{:S(2)}, u32[]{:S(2)}) collective-permute-start(bf16[384,128]{1,0:T(8,128)(2,1)S(1)} %add_convert_fusion.own_ref), channel_id=1, source_target_pairs={{0,8},{4,12},{8,0},{12,4},{1,9},{5,13},{9,1},{13,5},{2,10},{6,14},... | collective-permute-start | bytes 294920 | tf_op jit(solution)/shard_map/ppermute | solution.py:452
  34.6 3.1 %collective-permute-done.10.refs_2_ = bf16[384,128]{1,0:T(8,128)(2,1)S(1)} collective-permute-done((bf16[384,128]{1,0:T(8,128)(2,1)S(1)}, bf16[384,128]{1,0:T(8,128)(2,1)S(1)}, u32[]{:S(2)}, u32[]{:S(2)}) %collective-permute-start.10) | collective-permute-done | bytes 98336 | tf_op jit(solution)/shard_map/ppermute | solution.py:452
  37.7 0.7 %collective-permute-done.8.refs_0_ = bf16[384,128]{1,0:T(8,128)(2,1)S(1)} collective-permute-done((bf16[384,128]{1,0:T(8,128)(2,1)S(1)}, bf16[384,128]{1,0:T(8,128)(2,1)S(1)}, u32[]{:S(2)}, u32[]{:S(2)}) %collective-permute-start.8) | collective-permute-done | bytes 98336 | tf_op jit(solution)/shard_map/ppermute | solution.py:452
  38.5 0.8 %collective-permute-done.9.refs_1_ = bf16[384,128]{1,0:T(8,128)(2,1)S(1)} collective-permute-done((bf16[384,128]{1,0:T(8,128)(2,1)S(1)}, bf16[384,128]{1,0:T(8,128)(2,1)S(1)}, u32[]{:S(2)}, u32[]{:S(2)}) %collective-permute-start.9) | collective-permute-done | bytes 98336 | tf_op jit(solution)/shard_map/ppermute | solution.py:452
  39.2 0.1 shard_map.101.refs_0_
  39.3 0.1 collective-permute-start.11
  39.4 0.7 %shard_map.102 = (f32[512,128]{1,0:T(8,128)}, f32[512,128]{1,0:T(8,128)}) custom-call(bf16[512,128]{1,0:T(8,128)(2,1)S(1)} %shard_map.101.refs_0_), custom_call_target="tpu_custom_call" | custom-call | bytes 393216 | tf_op jit(solution)/shard_map/pallas_call | solution.py:287
  40.1 0.6 %collective-permute-done.11.refs_0_ = bf16[512,128]{1,0:T(8,128)(2,1)S(1)} collective-permute-done((bf16[512,128]{1,0:T(8,128)(2,1)S(1)}, bf16[512,128]{1,0:T(8,128)(2,1)S(1)}, u32[]{:S(2)}, u32[]{:S(2)}) %collective-permute-start.11) | collective-permute-done | bytes 131104 | tf_op jit(solution)/shard_map/ppermute | solution.py:465
  40.7 0.7 %shard_map.103 = (f32[512,128]{1,0:T(8,128)}, f32[512,128]{1,0:T(8,128)}) custom-call(bf16[512,128]{1,0:T(8,128)(2,1)S(1)} %collective-permute-done.11.refs_0_, f32[512,128]{1,0:T(8,128)} %get-tuple-element.72.refs_1_, f32[512,128]{1,0:T(8,128)} %get-tuple-element.73.refs_2_), custom_call_target="tpu_custom_call", output_to_operand_aliasing={{0}: (1, {}), {1}: (2, {})} | custom-call | bytes 393216 | tf_op jit(solution)/shard_map/pallas_call | solution.py:287
  (2 shorter events, 0.1 us)
Async XLA Ops:
  2.0 8.1 %collective-permute-start.2 = (bf16[272,128]{1,0:T(8,128)(2,1)S(1)}, bf16[272,128]{1,0:T(8,128)(2,1)S(1)}, u32[]{:S(2)}, u32[]{:S(2)}) collective-permute-start(bf16[272,128]{1,0:T(8,128)(2,1)S(1)} %get-tuple-element.40.message_ref), channel_id=1, source_target_pairs={{0,12},{4,8},{8,4},{12,0},{1,13},{5,9},{9,5},{13,1},{2,14},{6,10},... | collective-permute-start | bytes 208904 | tf_op jit(solution)/shard_map/ppermute | solution.py:395
  7.1 4.9 %collective-permute-start.1 = (bf16[272,128]{1,0:T(8,128)(2,1)S(1)}, bf16[272,128]{1,0:T(8,128)(2,1)S(1)}, u32[]{:S(2)}, u32[]{:S(2)}) collective-permute-start(bf16[272,128]{1,0:T(8,128)(2,1)S(1)} %get-tuple-element.40.message_ref), channel_id=1, source_target_pairs={{0,4},{4,0},{8,12},{12,8},{1,5},{5,1},{9,13},{13,9},{2,6},{6,2},{1... | collective-permute-start | bytes 208904 | tf_op jit(solution)/shard_map/ppermute | solution.py:395
  7.1 5.7 %collective-permute-start = (bf16[272,128]{1,0:T(8,128)(2,1)S(1)}, bf16[272,128]{1,0:T(8,128)(2,1)S(1)}, u32[]{:S(2)}, u32[]{:S(2)}) collective-permute-start(bf16[272,128]{1,0:T(8,128)(2,1)S(1)} %get-tuple-element.40.message_ref), channel_id=1, source_target_pairs={{0,8},{4,12},{8,0},{12,4},{1,9},{5,13},{9,1},{13,5},{2,10},{6,14},... | collective-permute-start | bytes 208904 | tf_op jit(solution)/shard_map/ppermute | solution.py:395
  13.7 9.7 %collective-permute-start.3 = (bf16[512,128]{1,0:T(8,128)(2,1)S(1)}, bf16[512,128]{1,0:T(8,128)(2,1)S(1)}, u32[]{:S(2)}, u32[]{:S(2)}) collective-permute-start(bf16[512,128]{1,0:T(8,128)(2,1)S(1)} %get-tuple-element.67), channel_id=1, source_target_pairs={{4,0},{0,4},{12,8},{8,12},{5,1},{1,5},{13,9},{9,13},{6,2},{2,6},{1... | collective-permute-start | bytes 393224 | tf_op jit(solution)/shard_map/ppermute | solution.py:433
  15.3 6.5 %collective-permute-start.4 = (bf16[256,128]{1,0:T(8,128)(2,1)S(1)}, bf16[256,128]{1,0:T(8,128)(2,1)S(1)}, u32[]{:S(2)}, u32[]{:S(2)}) collective-permute-start(bf16[256,128]{1,0:T(8,128)(2,1)S(1)} %get-tuple-element.68), channel_id=1, source_target_pairs={{8,0},{12,4},{0,8},{4,12},{9,1},{13,5},{1,9},{5,13},{10,2},{14,6},... | collective-permute-start | bytes 196616 | tf_op jit(solution)/shard_map/ppermute | solution.py:433
  17.4 6.1 %collective-permute-start.5 = (bf16[256,128]{1,0:T(8,128)(2,1)S(1)}, bf16[256,128]{1,0:T(8,128)(2,1)S(1)}, u32[]{:S(2)}, u32[]{:S(2)}) collective-permute-start(bf16[256,128]{1,0:T(8,128)(2,1)S(1)} %get-tuple-element.69), channel_id=1, source_target_pairs={{12,0},{8,4},{4,8},{0,12},{13,1},{9,5},{5,9},{1,13},{14,2},{10,6},... | collective-permute-start | bytes 196616 | tf_op jit(solution)/shard_map/ppermute | solution.py:433
  23.8 1.4 %collective-permute-start.6 = (bf16[384,128]{1,0:T(8,128)(2,1)S(1)}, bf16[384,128]{1,0:T(8,128)(2,1)S(1)}, u32[]{:S(2)}, u32[]{:S(2)}) collective-permute-start(bf16[384,128]{1,0:T(8,128)(2,1)S(1)} %get-tuple-element.71), channel_id=1, source_target_pairs={{0,1},{1,0},{2,3},{3,2},{4,5},{5,4},{6,7},{7,6},{8,9},{9,8},{10,11... | collective-permute-start | bytes 294920 | tf_op jit(solution)/shard_map/ppermute | solution.py:448
  25.2 4.9 %collective-permute-start.7 = (bf16[384,128]{1,0:T(8,128)(2,1)S(1)}, bf16[384,128]{1,0:T(8,128)(2,1)S(1)}, u32[]{:S(2)}, u32[]{:S(2)}) collective-permute-start(bf16[384,128]{1,0:T(8,128)(2,1)S(1)} %add_convert_fusion.1), channel_id=1, source_target_pairs={{0,2},{2,0},{1,3},{3,1},{4,6},{6,4},{5,7},{7,5},{8,10},{10,8},{9,1... | collective-permute-start | bytes 294920 | tf_op jit(solution)/shard_map/ppermute | solution.py:350
  30.1 7.6 %collective-permute-start.10 = (bf16[384,128]{1,0:T(8,128)(2,1)S(1)}, bf16[384,128]{1,0:T(8,128)(2,1)S(1)}, u32[]{:S(2)}, u32[]{:S(2)}) collective-permute-start(bf16[384,128]{1,0:T(8,128)(2,1)S(1)} %add_convert_fusion.own_ref), channel_id=1, source_target_pairs={{0,12},{4,8},{8,4},{12,0},{1,13},{5,9},{9,5},{13,1},{2,14},{6,10},... | collective-permute-start | bytes 294920 | tf_op jit(solution)/shard_map/ppermute | solution.py:452
  31.0 7.4 %collective-permute-start.8 = (bf16[384,128]{1,0:T(8,128)(2,1)S(1)}, bf16[384,128]{1,0:T(8,128)(2,1)S(1)}, u32[]{:S(2)}, u32[]{:S(2)}) collective-permute-start(bf16[384,128]{1,0:T(8,128)(2,1)S(1)} %add_convert_fusion.own_ref), channel_id=1, source_target_pairs={{0,4},{4,0},{8,12},{12,8},{1,5},{5,1},{9,13},{13,9},{2,6},{6,2},{1... | collective-permute-start | bytes 294920 | tf_op jit(solution)/shard_map/ppermute | solution.py:452
  31.4 7.8 %collective-permute-start.9 = (bf16[384,128]{1,0:T(8,128)(2,1)S(1)}, bf16[384,128]{1,0:T(8,128)(2,1)S(1)}, u32[]{:S(2)}, u32[]{:S(2)}) collective-permute-start(bf16[384,128]{1,0:T(8,128)(2,1)S(1)} %add_convert_fusion.own_ref), channel_id=1, source_target_pairs={{0,8},{4,12},{8,0},{12,4},{1,9},{5,13},{9,1},{13,5},{2,10},{6,14},... | collective-permute-start | bytes 294920 | tf_op jit(solution)/shard_map/ppermute | solution.py:452
  39.3 1.4 %collective-permute-start.11 = (bf16[512,128]{1,0:T(8,128)(2,1)S(1)}, bf16[512,128]{1,0:T(8,128)(2,1)S(1)}, u32[]{:S(2)}, u32[]{:S(2)}) collective-permute-start(bf16[512,128]{1,0:T(8,128)(2,1)S(1)} %shard_map.101.refs_0_), channel_id=1, source_target_pairs={{0,1},{1,0},{2,3},{3,2},{4,5},{5,4},{6,7},{7,6},{8,9},{9,8},{10,11... | collective-permute-start | bytes 393224 | tf_op jit(solution)/shard_map/ppermute | solution.py:465

commit v9 on v8

--- a/solution.py
+++ b/solution.py
@@ -53,7 +53,7 @@
     copies[6].wait()
     copies[5].wait()
     z = jnp.dot(feats_ref[...], proj_ref[...], preferred_element_type=f32)
-    inverse = 1.0 / jnp.sqrt(jnp.sum(z * z, axis=1, keepdims=True) + epsilon)
+    inverse = lax.rsqrt(jnp.sum(z * z, axis=1, keepdims=True) + epsilon)
     unit = z * inverse
     message_ref[0:rows, :] = unit.astype(bf16)
     unit_ref[...] = unit

time: 41.6 us -> 41.6 us (level)
  no operation moved by 1% of the time
where the time goes in v9:
time: 41.6 us; the launch traced here: 41.4 us
  waiting for transfers between devices  17.4 us (42%)
  starting transfers between devices  16.4 us (39%)
  Pallas kernels  6.89 us (17%)
  between operations  0.72 us (2%)
    ppermute x3, starting transfers between devices, on_device(): received = [lax.ppermute(message, 'neg', pairs) for pairs in exchange]  5.75 us
    pallas_call x8, Pallas kernels, call(): pl.pallas_call(kernel, out_shape=tuple((jax.ShapeDtypeStruct(s.shape, s.d...  5.42 us
    ppermute x3, waiting for transfers between devices, on_device(): got = [lax.ppermute(half, 'neg', pairs) for pairs in exchange]  4.64 us
    ppermute x3, waiting for transfers between devices, on_device(): lax.ppermute(piece, 'neg', sent_back(pairs))  4.48 us
    ppermute x3, starting transfers between devices, on_device(): got = [lax.ppermute(half, 'neg', pairs) for pairs in exchange]  4.45 us
    ppermute x3, starting transfers between devices, on_device(): lax.ppermute(piece, 'neg', sent_back(pairs))  4.45 us
    ppermute x1, waiting for transfers between devices, sum_over(): lax.ppermute(values, axis, pairs).astype(f32)  3.35 us
    ppermute x3, waiting for transfers between devices, on_device(): received = [lax.ppermute(message, 'neg', pairs) for pairs in exchange]  3.05 us
  transfers between devices with their start and end apart: 12, of which 11 were waited for; matrix products, arithmetic and copies ran while one was open for 0% of the time, Pallas kernels for 9%

profile of v9, /device:TPU:0, one launch (start us, length us, event | category | flops | bytes accessed | tf_op | source)
XLA Modules:
  0.0 41.4 jit_solution(10836406541729456253)
XLA Ops:
  0.6 1.4 %shard_map.94 = (bf16[272,128]{1,0:T(8,128)(2,1)S(1)}, f32[256,128]{1,0:T(8,128)S(1)}, f32[256,128]{1,0:T(8,128)S(1)}, bf16[512,512]{1,0:T(8,128)(2,1)S(1)}, bf1...) custom-call(bf16[512,512]{1,0:T(8,128)(2,1)} %refs_0_.1, bf16[512,128]{1,0:T(8,128)(2,1)} %refs_1_.1, ...), custom_call_target="tpu_custom_call" | custom-call | flops 33554432 | bytes 2304000 | tf_op jit(solution)/shard_map/pallas_call | solution.py:302
  2.0 5.1 %collective-permute-start.2 = (bf16[272,128]{1,0:T(8,128)(2,1)S(1)}, bf16[272,128]{1,0:T(8,128)(2,1)S(1)}, u32[]{:S(2)}, u32[]{:S(2)}) collective-permute-start(bf16[272,128]{1,0:T(8,128)(2,1)S(1)} %get-tuple-element.40.message_ref), channel_id=1, source_target_pairs={{0,12},{4,8},{8,4},{12,0},{1,13},{5,9},{9,5},{13,1},{2,14},{6,10},... | collective-permute-start | bytes 208904 | tf_op jit(solution)/shard_map/ppermute | solution.py:395
  7.1 0.0 collective-permute-start.1
  7.1 0.6 %collective-permute-start = (bf16[272,128]{1,0:T(8,128)(2,1)S(1)}, bf16[272,128]{1,0:T(8,128)(2,1)S(1)}, u32[]{:S(2)}, u32[]{:S(2)}) collective-permute-start(bf16[272,128]{1,0:T(8,128)(2,1)S(1)} %get-tuple-element.40.message_ref), channel_id=1, source_target_pairs={{0,8},{4,12},{8,0},{12,4},{1,9},{5,13},{9,1},{13,5},{2,10},{6,14},... | collective-permute-start | bytes 208904 | tf_op jit(solution)/shard_map/ppermute | solution.py:395
  7.7 0.9 %shard_map.95 = (f32[128,512]{1,0:T(8,128)S(1)}, bf16[128,512]{1,0:T(8,128)(2,1)S(1)}, bf16[512,128]{1,0:T(8,128)(2,1)S(1)}, f32[256,512]{1,0:T(8,128)S(1)}, f32...) custom-call(bf16[512,512]{1,0:T(8,128)(2,1)S(1)} %get-tuple-element., ...), custom_call_target="tpu_custom_call" | custom-call | flops 167772160 | bytes 3381248 | tf_op jit(solution)/shard_map/pallas_call | solution.py:302
  8.7 1.5 %collective-permute-done.2.message_ref = bf16[272,128]{1,0:T(8,128)(2,1)S(1)} collective-permute-done((bf16[272,128]{1,0:T(8,128)(2,1)S(1)}, bf16[272,128]{1,0:T(8,128)(2,1)S(1)}, u32[]{:S(2)}, u32[]{:S(2)}) %collective-permute-start.2) | collective-permute-done | bytes 69664 | tf_op jit(solution)/shard_map/ppermute | solution.py:395
  10.1 0.5 %shard_map.96 = (bf16[256,512]{1,0:T(8,128)(2,1)S(1)}, f32[128,512]{1,0:T(8,128)S(1)}, f32[8,512]{1,0:T(8,128)S(1)}) custom-call(bf16[272,128]{1,0:T(8,128)(2,1)S(1)} %collective-permute-done.2.message_ref, bf16[128,512]{1,0:T(8,128)(2,1)S(1)} %get-tuple-element.45.query_ref.refs_1_, f32[8,512]{1,0:T(8,128)S(1)} %get-tuple-element.46.lines_ref.totals_ref.refs_2_, ...), custom_call_target="tpu_custom_call" | custom-call | flops 67108864 | bytes 1052672 | tf_op jit(solution)/shard_map/pallas_call | solution.py:302
  10.7 1.3 %collective-permute-done.1.message_ref = bf16[272,128]{1,0:T(8,128)(2,1)S(1)} collective-permute-done((bf16[272,128]{1,0:T(8,128)(2,1)S(1)}, bf16[272,128]{1,0:T(8,128)(2,1)S(1)}, u32[]{:S(2)}, u32[]{:S(2)}) %collective-permute-start.1) | collective-permute-done | bytes 69664 | tf_op jit(solution)/shard_map/ppermute | solution.py:395
  12.0 0.5 %shard_map.97 = (bf16[256,512]{1,0:T(8,128)(2,1)S(1)}, f32[128,512]{1,0:T(8,128)S(1)}, f32[8,512]{1,0:T(8,128)S(1)}) custom-call(bf16[272,128]{1,0:T(8,128)(2,1)S(1)} %collective-permute-done.1.message_ref, bf16[128,512]{1,0:T(8,128)(2,1)S(1)} %get-tuple-element.45.query_ref.refs_1_, f32[8,512]{1,0:T(8,128)S(1)} %get-tuple-element.46.lines_ref.totals_ref.refs_2_, ...), custom_call_target="tpu_custom_call" | custom-call | flops 67108864 | bytes 1052672 | tf_op jit(solution)/shard_map/pallas_call | solution.py:302
  12.5 0.3 collective-permute-done.refs_0_
  12.8 0.9 %shard_map.98 = (bf16[512,128]{1,0:T(8,128)(2,1)S(1)}, bf16[256,128]{1,0:T(8,128)(2,1)S(1)}, bf16[256,128]{1,0:T(8,128)(2,1)S(1)}, bf16[128,512]{1,0:T(8,128)(2,1)S(1)}, f32[8,512]{1,0:T(8,128)S(1)}) custom-call(bf16[272,128]{1,0:T(8,128)(2,1)S(1)} %collective-permute-done.refs_0_, bf16[128,512]{1,0:T(8,128)(2,1)S(1)} %get-tuple-element.45.query_ref.refs_1_, ...), custom_call_target="tpu_custom_call" | custom-call | flops 402653184 | bytes 2494464 | tf_op jit(solution)/shard_map/pallas_call | solution.py:302
  13.7 1.6 %collective-permute-start.3 = (bf16[512,128]{1,0:T(8,128)(2,1)S(1)}, bf16[512,128]{1,0:T(8,128)(2,1)S(1)}, u32[]{:S(2)}, u32[]{:S(2)}) collective-permute-start(bf16[512,128]{1,0:T(8,128)(2,1)S(1)} %get-tuple-element.67), channel_id=1, source_target_pairs={{4,0},{0,4},{12,8},{8,12},{5,1},{1,5},{13,9},{9,13},{6,2},{2,6},{1... | collective-permute-start | bytes 393224 | tf_op jit(solution)/shard_map/ppermute | solution.py:433
  15.3 2.1 %collective-permute-start.4 = (bf16[256,128]{1,0:T(8,128)(2,1)S(1)}, bf16[256,128]{1,0:T(8,128)(2,1)S(1)}, u32[]{:S(2)}, u32[]{:S(2)}) collective-permute-start(bf16[256,128]{1,0:T(8,128)(2,1)S(1)} %get-tuple-element.68), channel_id=1, source_target_pairs={{8,0},{12,4},{0,8},{4,12},{9,1},{13,5},{1,9},{5,13},{10,2},{14,6},... | collective-permute-start | bytes 196616 | tf_op jit(solution)/shard_map/ppermute | solution.py:433
  17.4 0.8 %collective-permute-start.5 = (bf16[256,128]{1,0:T(8,128)(2,1)S(1)}, bf16[256,128]{1,0:T(8,128)(2,1)S(1)}, u32[]{:S(2)}, u32[]{:S(2)}) collective-permute-start(bf16[256,128]{1,0:T(8,128)(2,1)S(1)} %get-tuple-element.69), channel_id=1, source_target_pairs={{12,0},{8,4},{4,8},{0,12},{13,1},{9,5},{5,9},{1,13},{14,2},{10,6},... | collective-permute-start | bytes 196616 | tf_op jit(solution)/shard_map/ppermute | solution.py:433
  18.2 0.8 %shard_map.99 = (f32[256,128]{1,0:T(8,128)S(1)}, f32[1,512]{1,0:T(1,128)}, f32[256,128]{1,0:T(8,128)S(1)}) custom-call(f32[8,512]{1,0:T(8,128)S(1)} %get-tuple-element.58.sums_ref, f32[8,512]{1,0:T(8,128)S(1)} %get-tuple-element.46.lines_ref.totals_ref.refs_2_, s32[1,512]{1,0:T(1,128)S(1)} %get-tuple-element.43.positives_ref, ...), custom_call_target="tpu_custom_call" | custom-call | flops 67108864 | bytes 1609728 | tf_op jit(solution)/shard_map/pallas_call | solution.py:302
  19.0 2.8 %collective-permute-done.4.refs_1_ = bf16[256,128]{1,0:T(8,128)(2,1)S(1)} collective-permute-done((bf16[256,128]{1,0:T(8,128)(2,1)S(1)}, bf16[256,128]{1,0:T(8,128)(2,1)S(1)}, u32[]{:S(2)}, u32[]{:S(2)}) %collective-permute-start.4) | collective-permute-done | bytes 65568 | tf_op jit(solution)/shard_map/ppermute | solution.py:433
  21.8 1.6 %collective-permute-done.5.refs_2_ = bf16[256,128]{1,0:T(8,128)(2,1)S(1)} collective-permute-done((bf16[256,128]{1,0:T(8,128)(2,1)S(1)}, bf16[256,128]{1,0:T(8,128)(2,1)S(1)}, u32[]{:S(2)}, u32[]{:S(2)}) %collective-permute-start.5) | collective-permute-done | bytes 65568 | tf_op jit(solution)/shard_map/ppermute | solution.py:433
  23.5 0.0 collective-permute-done.3.refs_0_
  23.5 0.3 shard_map.100
  23.8 0.1 collective-permute-start.6
  23.9 1.3 %collective-permute-done.6 = bf16[384,128]{1,0:T(8,128)(2,1)S(1)} collective-permute-done((bf16[384,128]{1,0:T(8,128)(2,1)S(1)}, bf16[384,128]{1,0:T(8,128)(2,1)S(1)}, u32[]{:S(2)}, u32[]{:S(2)}) %collective-permute-start.6) | collective-permute-done | bytes 98336 | tf_op jit(solution)/shard_map/ppermute | solution.py:448
  25.2 1.6 %collective-permute-start.7 = (bf16[384,128]{1,0:T(8,128)(2,1)S(1)}, bf16[384,128]{1,0:T(8,128)(2,1)S(1)}, u32[]{:S(2)}, u32[]{:S(2)}) collective-permute-start(bf16[384,128]{1,0:T(8,128)(2,1)S(1)} %add_convert_fusion.1), channel_id=1, source_target_pairs={{0,2},{2,0},{1,3},{3,1},{4,6},{6,4},{5,7},{7,5},{8,10},{10,8},{9,1... | collective-permute-start | bytes 294920 | tf_op jit(solution)/shard_map/ppermute | solution.py:350
  26.7 3.4 %collective-permute-done.7 = bf16[384,128]{1,0:T(8,128)(2,1)S(1)} collective-permute-done((bf16[384,128]{1,0:T(8,128)(2,1)S(1)}, bf16[384,128]{1,0:T(8,128)(2,1)S(1)}, u32[]{:S(2)}, u32[]{:S(2)}) %collective-permute-start.7) | collective-permute-done | bytes 98336 | tf_op jit(solution)/shard_map/ppermute | solution.py:350
  30.1 0.9 %collective-permute-start.10 = (bf16[384,128]{1,0:T(8,128)(2,1)S(1)}, bf16[384,128]{1,0:T(8,128)(2,1)S(1)}, u32[]{:S(2)}, u32[]{:S(2)}) collective-permute-start(bf16[384,128]{1,0:T(8,128)(2,1)S(1)} %add_convert_fusion.own_ref), channel_id=1, source_target_pairs={{0,12},{4,8},{8,4},{12,0},{1,13},{5,9},{9,5},{13,1},{2,14},{6,10},... | collective-permute-start | bytes 294920 | tf_op jit(solution)/shard_map/ppermute | solution.py:452
  31.0 0.4 collective-permute-start.8
  31.4 3.2 %collective-permute-start.9 = (bf16[384,128]{1,0:T(8,128)(2,1)S(1)}, bf16[384,128]{1,0:T(8,128)(2,1)S(1)}, u32[]{:S(2)}, u32[]{:S(2)}) collective-permute-start(bf16[384,128]{1,0:T(8,128)(2,1)S(1)} %add_convert_fusion.own_ref), channel_id=1, source_target_pairs={{0,8},{4,12},{8,0},{12,4},{1,9},{5,13},{9,1},{13,5},{2,10},{6,14},... | collective-permute-start | bytes 294920 | tf_op jit(solution)/shard_map/ppermute | solution.py:452
  34.6 3.1 %collective-permute-done.10.refs_2_ = bf16[384,128]{1,0:T(8,128)(2,1)S(1)} collective-permute-done((bf16[384,128]{1,0:T(8,128)(2,1)S(1)}, bf16[384,128]{1,0:T(8,128)(2,1)S(1)}, u32[]{:S(2)}, u32[]{:S(2)}) %collective-permute-start.10) | collective-permute-done | bytes 98336 | tf_op jit(solution)/shard_map/ppermute | solution.py:452
  37.7 0.7 %collective-permute-done.8.refs_0_ = bf16[384,128]{1,0:T(8,128)(2,1)S(1)} collective-permute-done((bf16[384,128]{1,0:T(8,128)(2,1)S(1)}, bf16[384,128]{1,0:T(8,128)(2,1)S(1)}, u32[]{:S(2)}, u32[]{:S(2)}) %collective-permute-start.8) | collective-permute-done | bytes 98336 | tf_op jit(solution)/shard_map/ppermute | solution.py:452
  38.5 0.8 %collective-permute-done.9.refs_1_ = bf16[384,128]{1,0:T(8,128)(2,1)S(1)} collective-permute-done((bf16[384,128]{1,0:T(8,128)(2,1)S(1)}, bf16[384,128]{1,0:T(8,128)(2,1)S(1)}, u32[]{:S(2)}, u32[]{:S(2)}) %collective-permute-start.9) | collective-permute-done | bytes 98336 | tf_op jit(solution)/shard_map/ppermute | solution.py:452
  39.2 0.1 shard_map.101.refs_0_
  39.3 0.1 collective-permute-start.11
  39.4 0.7 %shard_map.102 = (f32[512,128]{1,0:T(8,128)}, f32[512,128]{1,0:T(8,128)}) custom-call(bf16[512,128]{1,0:T(8,128)(2,1)S(1)} %shard_map.101.refs_0_), custom_call_target="tpu_custom_call" | custom-call | bytes 393216 | tf_op jit(solution)/shard_map/pallas_call | solution.py:287
  40.1 0.6 %collective-permute-done.11.refs_0_ = bf16[512,128]{1,0:T(8,128)(2,1)S(1)} collective-permute-done((bf16[512,128]{1,0:T(8,128)(2,1)S(1)}, bf16[512,128]{1,0:T(8,128)(2,1)S(1)}, u32[]{:S(2)}, u32[]{:S(2)}) %collective-permute-start.11) | collective-permute-done | bytes 131104 | tf_op jit(solution)/shard_map/ppermute | solution.py:465
  40.7 0.7 %shard_map.103 = (f32[512,128]{1,0:T(8,128)}, f32[512,128]{1,0:T(8,128)}) custom-call(bf16[512,128]{1,0:T(8,128)(2,1)S(1)} %collective-permute-done.11.refs_0_, f32[512,128]{1,0:T(8,128)} %get-tuple-element.72.refs_1_, f32[512,128]{1,0:T(8,128)} %get-tuple-element.73.refs_2_), custom_call_target="tpu_custom_call", output_to_operand_aliasing={{0}: (1, {}), {1}: (2, {})} | custom-call | bytes 393216 | tf_op jit(solution)/shard_map/pallas_call | solution.py:287
  (2 shorter events, 0.1 us)
Async XLA Ops:
  2.0 8.1 %collective-permute-start.2 = (bf16[272,128]{1,0:T(8,128)(2,1)S(1)}, bf16[272,128]{1,0:T(8,128)(2,1)S(1)}, u32[]{:S(2)}, u32[]{:S(2)}) collective-permute-start(bf16[272,128]{1,0:T(8,128)(2,1)S(1)} %get-tuple-element.40.message_ref), channel_id=1, source_target_pairs={{0,12},{4,8},{8,4},{12,0},{1,13},{5,9},{9,5},{13,1},{2,14},{6,10},... | collective-permute-start | bytes 208904 | tf_op jit(solution)/shard_map/ppermute | solution.py:395
  7.1 4.9 %collective-permute-start.1 = (bf16[272,128]{1,0:T(8,128)(2,1)S(1)}, bf16[272,128]{1,0:T(8,128)(2,1)S(1)}, u32[]{:S(2)}, u32[]{:S(2)}) collective-permute-start(bf16[272,128]{1,0:T(8,128)(2,1)S(1)} %get-tuple-element.40.message_ref), channel_id=1, source_target_pairs={{0,4},{4,0},{8,12},{12,8},{1,5},{5,1},{9,13},{13,9},{2,6},{6,2},{1... | collective-permute-start | bytes 208904 | tf_op jit(solution)/shard_map/ppermute | solution.py:395
  7.1 5.7 %collective-permute-start = (bf16[272,128]{1,0:T(8,128)(2,1)S(1)}, bf16[272,128]{1,0:T(8,128)(2,1)S(1)}, u32[]{:S(2)}, u32[]{:S(2)}) collective-permute-start(bf16[272,128]{1,0:T(8,128)(2,1)S(1)} %get-tuple-element.40.message_ref), channel_id=1, source_target_pairs={{0,8},{4,12},{8,0},{12,4},{1,9},{5,13},{9,1},{13,5},{2,10},{6,14},... | collective-permute-start | bytes 208904 | tf_op jit(solution)/shard_map/ppermute | solution.py:395
  13.7 9.7 %collective-permute-start.3 = (bf16[512,128]{1,0:T(8,128)(2,1)S(1)}, bf16[512,128]{1,0:T(8,128)(2,1)S(1)}, u32[]{:S(2)}, u32[]{:S(2)}) collective-permute-start(bf16[512,128]{1,0:T(8,128)(2,1)S(1)} %get-tuple-element.67), channel_id=1, source_target_pairs={{4,0},{0,4},{12,8},{8,12},{5,1},{1,5},{13,9},{9,13},{6,2},{2,6},{1... | collective-permute-start | bytes 393224 | tf_op jit(solution)/shard_map/ppermute | solution.py:433
  15.3 6.5 %collective-permute-start.4 = (bf16[256,128]{1,0:T(8,128)(2,1)S(1)}, bf16[256,128]{1,0:T(8,128)(2,1)S(1)}, u32[]{:S(2)}, u32[]{:S(2)}) collective-permute-start(bf16[256,128]{1,0:T(8,128)(2,1)S(1)} %get-tuple-element.68), channel_id=1, source_target_pairs={{8,0},{12,4},{0,8},{4,12},{9,1},{13,5},{1,9},{5,13},{10,2},{14,6},... | collective-permute-start | bytes 196616 | tf_op jit(solution)/shard_map/ppermute | solution.py:433
  17.4 6.1 %collective-permute-start.5 = (bf16[256,128]{1,0:T(8,128)(2,1)S(1)}, bf16[256,128]{1,0:T(8,128)(2,1)S(1)}, u32[]{:S(2)}, u32[]{:S(2)}) collective-permute-start(bf16[256,128]{1,0:T(8,128)(2,1)S(1)} %get-tuple-element.69), channel_id=1, source_target_pairs={{12,0},{8,4},{4,8},{0,12},{13,1},{9,5},{5,9},{1,13},{14,2},{10,6},... | collective-permute-start | bytes 196616 | tf_op jit(solution)/shard_map/ppermute | solution.py:433
  23.8 1.4 %collective-permute-start.6 = (bf16[384,128]{1,0:T(8,128)(2,1)S(1)}, bf16[384,128]{1,0:T(8,128)(2,1)S(1)}, u32[]{:S(2)}, u32[]{:S(2)}) collective-permute-start(bf16[384,128]{1,0:T(8,128)(2,1)S(1)} %get-tuple-element.71), channel_id=1, source_target_pairs={{0,1},{1,0},{2,3},{3,2},{4,5},{5,4},{6,7},{7,6},{8,9},{9,8},{10,11... | collective-permute-start | bytes 294920 | tf_op jit(solution)/shard_map/ppermute | solution.py:448
  25.2 4.9 %collective-permute-start.7 = (bf16[384,128]{1,0:T(8,128)(2,1)S(1)}, bf16[384,128]{1,0:T(8,128)(2,1)S(1)}, u32[]{:S(2)}, u32[]{:S(2)}) collective-permute-start(bf16[384,128]{1,0:T(8,128)(2,1)S(1)} %add_convert_fusion.1), channel_id=1, source_target_pairs={{0,2},{2,0},{1,3},{3,1},{4,6},{6,4},{5,7},{7,5},{8,10},{10,8},{9,1... | collective-permute-start | bytes 294920 | tf_op jit(solution)/shard_map/ppermute | solution.py:350
  30.1 7.6 %collective-permute-start.10 = (bf16[384,128]{1,0:T(8,128)(2,1)S(1)}, bf16[384,128]{1,0:T(8,128)(2,1)S(1)}, u32[]{:S(2)}, u32[]{:S(2)}) collective-permute-start(bf16[384,128]{1,0:T(8,128)(2,1)S(1)} %add_convert_fusion.own_ref), channel_id=1, source_target_pairs={{0,12},{4,8},{8,4},{12,0},{1,13},{5,9},{9,5},{13,1},{2,14},{6,10},... | collective-permute-start | bytes 294920 | tf_op jit(solution)/shard_map/ppermute | solution.py:452
  31.0 7.4 %collective-permute-start.8 = (bf16[384,128]{1,0:T(8,128)(2,1)S(1)}, bf16[384,128]{1,0:T(8,128)(2,1)S(1)}, u32[]{:S(2)}, u32[]{:S(2)}) collective-permute-start(bf16[384,128]{1,0:T(8,128)(2,1)S(1)} %add_convert_fusion.own_ref), channel_id=1, source_target_pairs={{0,4},{4,0},{8,12},{12,8},{1,5},{5,1},{9,13},{13,9},{2,6},{6,2},{1... | collective-permute-start | bytes 294920 | tf_op jit(solution)/shard_map/ppermute | solution.py:452
  31.4 7.8 %collective-permute-start.9 = (bf16[384,128]{1,0:T(8,128)(2,1)S(1)}, bf16[384,128]{1,0:T(8,128)(2,1)S(1)}, u32[]{:S(2)}, u32[]{:S(2)}) collective-permute-start(bf16[384,128]{1,0:T(8,128)(2,1)S(1)} %add_convert_fusion.own_ref), channel_id=1, source_target_pairs={{0,8},{4,12},{8,0},{12,4},{1,9},{5,13},{9,1},{13,5},{2,10},{6,14},... | collective-permute-start | bytes 294920 | tf_op jit(solution)/shard_map/ppermute | solution.py:452
  39.3 1.4 %collective-permute-start.11 = (bf16[512,128]{1,0:T(8,128)(2,1)S(1)}, bf16[512,128]{1,0:T(8,128)(2,1)S(1)}, u32[]{:S(2)}, u32[]{:S(2)}) collective-permute-start(bf16[512,128]{1,0:T(8,128)(2,1)S(1)} %shard_map.101.refs_0_), channel_id=1, source_target_pairs={{0,1},{1,0},{2,3},{3,2},{4,5},{5,4},{6,7},{7,6},{8,9},{9,8},{10,11... | collective-permute-start | bytes 393224 | tf_op jit(solution)/shard_map/ppermute | solution.py:465
